TPU v7x, 32 devices: a whole 2x2x4 slice. The times are simulated.
32 devices in a mesh: member: 2 (over y), dom: 8 (over z, x), feat: 2 (over core).
Axes of the slice: x: 2, y: 2, z: 4, core: 2. Of those that a mesh axis runs over, the one named last changes fastest.
Arguments:
- grid_lat: bfloat16 [16384, 512], P(('member', 'dom'), 'feat'), parts along dimension 0, may hold values from -6 to 6
- mesh_lat: bfloat16 [8192, 512], P(('member', 'dom'), 'feat'), parts along dimension 0, may hold values from -6 to 6
- w_grid_send: bfloat16 [512, 512], P(None, 'feat'), may hold values from -0.25 to 0.25
- w_grid_recv: bfloat16 [512, 512], P(None, 'feat'), may hold values from -0.25 to 0.25
- g2m_bias: float32 [512], P('feat'), may hold values from -4 to 4
- w_grid_out: bfloat16 [512, 512], P('feat'), may hold values from -0.125 to 0.125
- w_edge_send: bfloat16 [512, 512], P(None, 'feat'), may hold values from -0.25 to 0.25
- w_edge_recv: bfloat16 [512, 512], P(None, 'feat'), may hold values from -0.25 to 0.25
- edge_bias: float32 [512], P('feat'), may hold values from -4 to 4
- w_edge_out: bfloat16 [512, 512], P('feat'), may hold values from -0.125 to 0.125
- send_grid: int32 [8, 4096], P('dom'), may hold values from 0 to 1023, as said below
- recv_row: int32 [8, 4096], P('dom'), may hold values from 0 to 512, as said below
- halo_rows: int32 [8, 1024], P('dom'), may hold values from 0 to 511, as said below
- edge_src: int32 [128, 128], P('dom'), may hold values from 0 to 1535, as said below
- edge_dst: int32 [128, 128], P('dom'), may hold values from 0 to 511
Outputs:
- mesh_encoded: bfloat16 [8192, 512], P(('member', 'dom'), 'feat'), parts along dimension 0
- mesh_out: bfloat16 [8192, 512], P(('member', 'dom'), 'feat'), parts along dimension 0
There are 2 independent parts, one for each index of `member`. A program takes and returns all parts, laid end to end along the dimension named above; an argument that names none is the same for every part. Nothing has to cross between parts.
Inputs may be any that keep to these rules, and one draw needn't show every extreme that they name: `send_grid`: entry p, j * 512 + k names a grid row (within partition p) for slot k from p to j. Every grid row of p is named by exactly one slot whose recv_row entry is below 512. `recv_row`: entry j, p * 512 + k is the mesh row of partition j that slot k from p feeds, or 512 for an empty slot. In every draw some partition gets 512 filled slots from every partition. `halo_rows`: entry p, j * 128 + k is the k-th of 128 different mesh rows of partition p that partition j reads. `edge_src`: each value 512 to 1535 appears in every partition's tiles.
All inputs are finite; a program needn't handle non-finite values.
Results may differ from a plain program's by a relative error of at most 0.013.
Values may be sent and summed in bfloat16 or wider, within the bound.
No kernel may reach another device: no remote copies, remote signals or barrier semaphores. Data moves between devices by JAX's collectives and lax.ppermute only.
A program may use at most 64 MiB of HBM per device.

v0:
```python
import jax
import jax.numpy as jnp
from jax import lax
from jax.sharding import PartitionSpec as P


def aggregate(targets, hidden, mesh_rows):
    onehot = (
        lax.broadcasted_iota(jnp.int32, (mesh_rows, targets.shape[0]), 0) == targets[None, :]
    ).astype(jnp.bfloat16)
    return jnp.dot(onehot, hidden, preferred_element_type=jnp.float32).astype(jnp.bfloat16)


def pick_rows(table, index):
    selector = (
        index[:, None] == lax.broadcasted_iota(jnp.int32, (index.shape[0], table.shape[0]), 1)
    ).astype(jnp.bfloat16)
    return jnp.dot(selector, table, preferred_element_type=jnp.float32).astype(jnp.bfloat16)


def shards(
    grid_lat,
    mesh_lat,
    w_grid_send,
    w_grid_recv,
    g2m_bias,
    w_grid_out,
    w_edge_send,
    w_edge_recv,
    edge_bias,
    w_edge_out,
    send_grid,
    recv_row,
    halo_rows,
    edge_src,
    edge_dst,
):
    mesh_rows = mesh_lat.shape[0]
    mesh_full = lax.all_gather(mesh_lat, "feat", axis=1, tiled=True)
    mesh_rproj = jnp.dot(mesh_full, w_grid_recv, preferred_element_type=jnp.float32).astype(
        jnp.bfloat16
    )
    slot_ids = send_grid.reshape(-1)
    packed = pick_rows(grid_lat, slot_ids)
    arrived = lax.all_to_all(packed, "dom", split_axis=0, concat_axis=0, tiled=True)
    slot_full = lax.all_gather(arrived, "feat", axis=1, tiled=True)
    slot_proj = jnp.dot(slot_full, w_grid_send, preferred_element_type=jnp.float32).astype(
        jnp.bfloat16
    )
    targets = recv_row.reshape(-1)
    mesh_term = pick_rows(mesh_rproj, targets)
    preact = slot_proj.astype(jnp.float32) + mesh_term.astype(jnp.float32) + g2m_bias[None, :]
    hidden = jax.nn.silu(preact).astype(jnp.bfloat16)
    g2m_sum = aggregate(targets, hidden, mesh_rows)
    partial_value = jnp.dot(g2m_sum, w_grid_out, preferred_element_type=jnp.float32)
    encoder_update = lax.psum_scatter(partial_value, "feat", scatter_dimension=1, tiled=True)
    mesh_encoded = (mesh_lat.astype(jnp.float32) + encoder_update).astype(jnp.bfloat16)
    halo_index = halo_rows.reshape(-1)
    halo_latent = lax.all_to_all(
        pick_rows(mesh_encoded, halo_index), "dom", split_axis=0, concat_axis=0, tiled=True
    )
    joined = lax.all_gather(
        jnp.concatenate([mesh_encoded, halo_latent], axis=0), "feat", axis=1, tiled=True
    )
    encoded_full = joined[:mesh_rows]
    lookup_table = jnp.dot(joined, w_edge_send, preferred_element_type=jnp.float32).astype(
        jnp.bfloat16
    )
    recv_proj = jnp.dot(encoded_full, w_edge_recv, preferred_element_type=jnp.float32).astype(
        jnp.bfloat16
    )
    senders = edge_src.reshape(-1)
    receivers = edge_dst.reshape(-1)
    edge_pre = (
        pick_rows(lookup_table, senders).astype(jnp.float32)
        + pick_rows(recv_proj, receivers).astype(jnp.float32)
        + edge_bias[None, :]
    )
    edge_hidden = jax.nn.silu(edge_pre).astype(jnp.bfloat16)
    proc_sum = aggregate(receivers, edge_hidden, mesh_rows)
    proc_partial = jnp.dot(proc_sum, w_edge_out, preferred_element_type=jnp.float32)
    proc_update = lax.psum_scatter(proc_partial, "feat", scatter_dimension=1, tiled=True)
    mesh_out = (mesh_encoded.astype(jnp.float32) + proc_update).astype(jnp.bfloat16)
    return (mesh_encoded, mesh_out)


def solution(mesh):
    placed = (
        P(("member", "dom"), "feat"),
        P(("member", "dom"), "feat"),
        P(None, "feat"),
        P(None, "feat"),
        P("feat"),
        P("feat", None),
        P(None, "feat"),
        P(None, "feat"),
        P("feat"),
        P("feat", None),
        P("dom", None),
        P("dom", None),
        P("dom", None),
        P("dom", None),
        P("dom", None),
    )
    return jax.shard_map(
        shards,
        mesh=mesh,
        in_specs=placed,
        out_specs=(P(("member", "dom"), "feat"), P(("member", "dom"), "feat")),
        check_vma=False,
    )
```

profile of v0, /device:TPU:0, one launch (start us, length us, event | category | flops | bytes accessed | tf_op | source)
XLA Modules:
  0.0 169.0 jit_solution(1296683829388273606)
XLA Ops:
  7.2 0.0 copy-start
  7.2 0.0 all-gather.3.cloned.1.call-start
  7.2 1.0 copy-done
  8.2 4.2 %fusion.10 = bf16[4096,256]{1,0:T(8,128)(2,1)S(1)} fusion(bf16[1024,256]{1,0:T(8,128)(2,1)S(1)} %copy-done, s32[4096]{0:T(1024)} %bitcast.26), kind=kOutput, calls=%fused_computation.14 | convolution fusion | flops 2152726528 | bytes 2637824 | tf_op jit(solution)/shard_map/dot_general | solution.py:18
  12.4 55.4 %all_to_all.24 = bf16[8,512,256]{2,1,0:T(8,128)(2,1)} all-to-all(bf16[8,512,256]{2,1,0:T(8,128)(2,1)S(1)} %bitcast.24), channel_id=1, replica_groups=mesh['member'=2,'dom'=8,'feat'=2] {'dom'}, dimensions={0} | all-to-all | bytes 4194304 | tf_op jit(solution)/shard_map/all_to_all | solution.py:45
  67.8 0.0 all-gather.3.cloned.1.call-update
  67.9 0.0 reduce-scatter.3.cloned.1.call-start
  67.9 0.9 copy-done.2
  68.8 2.2 %all_gather.10 = bf16[512,512]{1,0:T(8,128)(2,1)S(1)} all-gather(bf16[512,256]{1,0:T(8,128)(2,1)S(1)} %copy-done.2), channel_id=1, replica_groups=mesh['member'=2,'dom'=8,'feat'=2] {'feat'}, dimensions={1}, use_global_device_ids=true | all-gather | bytes 786432 | tf_op jit(solution)/shard_map/all_gather | solution.py:39
  71.0 9.1 %all-gather.3.cloned.1.call-done = bf16[4096,512]{1,0:T(8,128)(2,1)} async-done(((bf16[4096,256]{1,0:T(8,128)(2,1)}), bf16[4096,512]{1,0:T(8,128)(2,1)}) %all-gather.3.cloned.1.call-update) | async-done | bytes 4194320 | tf_op jit(solution)/shard_map/all_gather | solution.py:46
  80.0 0.0 copy-done.3
  80.0 5.4 %fusion.11 = f32[4096,256]{1,0:T(8,128)} fusion(bf16[4096,512]{1,0:T(8,128)(2,1)} %all-gather.3.cloned.1.call-done, bf16[512,256]{1,0:T(8,128)(2,1)S(1)} %copy-done.3), kind=kOutput, calls=%fused_computation.16 | convolution fusion | flops 1075838976 | bytes 8650752 | tf_op jit(solution)/shard_map/dot_general | solution.py:47
  85.5 0.0 copy-done.5
  85.5 0.0 copy-done.10
  85.5 0.0 copy-done.14
  85.5 0.0 copy-start.6
  85.5 5.8 %multiply_convert_fusion = bf16[4096,256]{1,0:T(8,128)(2,1)} fusion(f32[4096,256]{1,0:T(8,128)} %fusion.11, s32[4096]{0:T(1024)S(1)} %bitcast.27, f32[256]{0:T(256)S(1)} %copy-done.14, bf16[512,512]{1,0:T(8,128)(2,1)S(1)} %all_gather.10, bf16[512,256]{1,0:T(8,128)(2,1)S(1)} %copy-done.5), kind=kOutput, calls=%fused_computation.19 | convolution fusion | flops 1219624960 | bytes 7095296 | tf_op jit(solution)/shard_map/dot_general | solution.py:18
  91.3 0.0 copy-done.6
  91.3 4.3 %fusion.27 = f32[512,512]{1,0:T(8,128)} fusion(bf16[256,512]{1,0:T(8,128)(2,1)S(1)} %copy-done.6, bf16[4096,256]{1,0:T(8,128)(2,1)} %multiply_convert_fusion, s32[4096]{0:T(1024)S(1)} %bitcast.28), kind=kOutput, calls=%fused_computation.38 | convolution fusion | flops 1210187776 | bytes 3424256 | tf_op jit(solution)/shard_map/dot_general | solution.py:55
  95.6 0.0 reduce-scatter.3.cloned.1.call-update
  95.6 0.0 all-gather.5.cloned.1.call-start
  95.7 9.9 %reduce-scatter.3.cloned.1.call-done = f32[512,256]{1,0:T(8,128)} async-done(((f32[512,512]{1,0:T(8,128)}), f32[512,256]{1,0:T(8,128)}) %reduce-scatter.3.cloned.1.call-update) | async-done | bytes 524304 | tf_op jit(solution)/shard_map/reduce_scatter | solution.py:56
  105.5 1.1 add_convert_fusion.1
  106.6 0.0 copy-start.1
  106.6 0.0 copy-done.13
  106.6 0.0 copy-start.7
  106.7 0.0 copy-start.12
  106.7 0.5 fusion.25
  107.2 20.5 %all_to_all.25 = bf16[8,128,256]{2,1,0:T(8,128)(2,1)S(1)} all-to-all(bf16[8,128,256]{2,1,0:T(8,128)(2,1)S(1)} %bitcast.25), channel_id=1, replica_groups=mesh['member'=2,'dom'=8,'feat'=2] {'dom'}, dimensions={0} | all-to-all | bytes 1048576 | tf_op jit(solution)/shard_map/all_to_all | solution.py:59
  127.7 0.9 pad_maximum_fusion
  128.6 0.0 all-gather.5.cloned.1.call-update
  128.7 0.2 reduce-scatter.5.cloned.1.call-start
  128.9 8.6 %all-gather.5.cloned.1.call-done = bf16[1536,512]{1,0:T(8,128)(2,1)} async-done(((bf16[1536,256]{1,0:T(8,128)(2,1)}), bf16[1536,512]{1,0:T(8,128)(2,1)}) %all-gather.5.cloned.1.call-update) | async-done | bytes 1572880 | tf_op jit(solution)/shard_map/all_gather | solution.py:62
  137.5 0.0 copy-done.7
  137.5 0.0 copy-done.12
  137.5 3.7 %fusion.21 = f32[2048,256]{1,0:T(8,128)} fusion(s32[2048]{0:T(1024)S(1)} %bitcast.30, bf16[512,256]{1,0:T(8,128)(2,1)S(1)} %copy-done.7, bf16[1536,512]{1,0:T(8,128)(2,1)} %all-gather.5.cloned.1.call-done), kind=kOutput, calls=%fused_computation.30 | convolution fusion | flops 673316864 | bytes 2891776 | tf_op jit(solution)/shard_map/dot_general | solution.py:18
  141.2 0.0 copy-done.8
  141.2 0.0 copy-done.11
  141.2 0.0 copy-done.15
  141.2 0.0 copy-done.4
  141.2 0.0 copy-start.9
  141.3 6.1 %multiply_convert_fusion.1 = bf16[2048,256]{1,0:T(8,128)(2,1)} fusion(f32[2048,256]{1,0:T(8,128)} %fusion.21, s32[2048]{0:T(1024)S(1)} %bitcast.29, bf16[1536,512]{1,0:T(8,128)(2,1)S(1)} %copy-done.4, bf16[512,256]{1,0:T(8,128)(2,1)S(1)} %copy-done.8, f32[256]{0:T(256)S(1)} %copy-done.15), kind=kOutput, calls=%fused_computation.31 | convolution fusion | flops 2021523456 | bytes 4989952 | tf_op jit(solution)/shard_map/dot_general | solution.py:18
  147.3 0.0 copy-done.9
  147.3 3.4 %fusion.29 = f32[512,512]{1,0:T(8,128)} fusion(bf16[256,512]{1,0:T(8,128)(2,1)S(1)} %copy-done.9, bf16[2048,256]{1,0:T(8,128)(2,1)} %multiply_convert_fusion.1, s32[2048]{0:T(1024)S(1)} %bitcast.31), kind=kOutput, calls=%fused_computation.42 | convolution fusion | flops 672268288 | bytes 2367488 | tf_op jit(solution)/shard_map/dot_general | solution.py:81
  150.7 0.0 reduce-scatter.5.cloned.1.call-update
  150.7 9.9 %reduce-scatter.5.cloned.1.call-done = f32[512,256]{1,0:T(8,128)} async-done(((f32[512,512]{1,0:T(8,128)}), f32[512,256]{1,0:T(8,128)}) %reduce-scatter.5.cloned.1.call-update) | async-done | bytes 524304 | tf_op jit(solution)/shard_map/reduce_scatter | solution.py:82
  160.6 0.0 copy-done.1
  160.6 1.8 %add_convert_fusion = bf16[512,256]{1,0:T(8,128)(2,1)} fusion(f32[512,256]{1,0:T(8,128)} %reduce-scatter.5.cloned.1.call-done, bf16[512,256]{1,0:T(8,128)(2,1)S(1)} %add_convert_fusion.1), kind=kLoop, calls=%fused_computation.46 | loop fusion | flops 393216 | bytes 1048576 | tf_op jit(solution)/shard_map/convert_element_type | solution.py:83
  (10 shorter events, 0.0 us)
Async XLA Ops:
  7.2 1.0 copy-start
  7.2 72.9 %all-gather.3.cloned.1.call-start = ((), (), s32[]{:S(2)}) async-start(), calls=%async_computation.4 | async-start | bytes 6291456 | tf_op jit(solution)/shard_map/all_gather | solution.py:46
  67.8 1.0 copy-start.2
  67.8 12.2 %copy-start.3 = (bf16[512,256]{1,0:T(8,128)(2,1)S(1)}, bf16[512,256]{1,0:T(8,128)(2,1)}, u32[]{:S(2)}) copy-start(bf16[512,256]{1,0:T(8,128)(2,1)} %param.17) | copy-start | bytes 786436
  67.9 37.7 %reduce-scatter.3.cloned.1.call-start = ((), (), s32[]{:S(2)}) async-start(), calls=%async_computation.5 | async-start | bytes 1572864 | tf_op jit(solution)/shard_map/reduce_scatter | solution.py:56
  71.0 14.5 %copy-start.5 = (bf16[512,256]{1,0:T(8,128)(2,1)S(1)}, bf16[512,256]{1,0:T(8,128)(2,1)}, u32[]{:S(2)}) copy-start(bf16[512,256]{1,0:T(8,128)(2,1)} %param.18) | copy-start | bytes 786436
  71.0 14.5 %copy-start.10 = (s32[1,4096]{1,0:T(1,128)S(1)}, s32[1,4096]{1,0:T(1,128)}, u32[]{:S(2)}) copy-start(s32[1,4096]{1,0:T(1,128)} %param.26) | copy-start | bytes 49156
  71.0 14.5 %copy-start.14 = (f32[256]{0:T(256)S(1)}, f32[256]{0:T(256)}, u32[]{:S(2)}) copy-start(f32[256]{0:T(256)} %param.19) | copy-start | bytes 3076
  85.5 5.8 %copy-start.6 = (bf16[256,512]{1,0:T(8,128)(2,1)S(1)}, bf16[256,512]{1,0:T(8,128)(2,1)}, u32[]{:S(2)}) copy-start(bf16[256,512]{1,0:T(8,128)(2,1)} %param.20) | copy-start | bytes 786436
  95.6 11.1 %copy-start.13 = (s32[1,1024]{1,0:T(1,128)S(1)}, s32[1,1024]{1,0:T(1,128)}, u32[]{:S(2)}) copy-start(s32[1,1024]{1,0:T(1,128)} %param.27) | copy-start | bytes 12292
  95.6 41.9 %all-gather.5.cloned.1.call-start = ((), (), s32[]{:S(2)}) async-start(), calls=%async_computation.6 | async-start | bytes 2359296 | tf_op jit(solution)/shard_map/all_gather | solution.py:62
  106.6 54.0 %copy-start.1 = (bf16[512,256]{1,0:T(8,128)(2,1)}, bf16[512,256]{1,0:T(8,128)(2,1)S(1)}, u32[]{:S(2)}) copy-start(bf16[512,256]{1,0:T(8,128)(2,1)S(1)} %add_convert_fusion.1) | copy-start | bytes 786436
  106.6 30.9 %copy-start.7 = (bf16[512,256]{1,0:T(8,128)(2,1)S(1)}, bf16[512,256]{1,0:T(8,128)(2,1)}, u32[]{:S(2)}) copy-start(bf16[512,256]{1,0:T(8,128)(2,1)} %param.22) | copy-start | bytes 786436
  106.7 30.9 %copy-start.12 = (s32[16,128]{1,0:T(8,128)S(1)}, s32[16,128]{1,0:T(8,128)}, u32[]{:S(2)}) copy-start(s32[16,128]{1,0:T(8,128)} %param.29) | copy-start | bytes 24580
  128.6 12.6 %copy-start.8 = (bf16[512,256]{1,0:T(8,128)(2,1)S(1)}, bf16[512,256]{1,0:T(8,128)(2,1)}, u32[]{:S(2)}) copy-start(bf16[512,256]{1,0:T(8,128)(2,1)} %param.21) | copy-start | bytes 786436
  128.6 12.6 %copy-start.11 = (s32[16,128]{1,0:T(8,128)S(1)}, s32[16,128]{1,0:T(8,128)}, u32[]{:S(2)}) copy-start(s32[16,128]{1,0:T(8,128)} %param.28) | copy-start | bytes 24580
  128.6 12.6 %copy-start.15 = (f32[256]{0:T(256)S(1)}, f32[256]{0:T(256)}, u32[]{:S(2)}) copy-start(f32[256]{0:T(256)} %param.23) | copy-start | bytes 3076
  128.7 32.0 %reduce-scatter.5.cloned.1.call-start = ((), (), s32[]{:S(2)}) async-start(), calls=%async_computation.7 | async-start | bytes 1572864 | tf_op jit(solution)/shard_map/reduce_scatter | solution.py:82
  137.5 3.7 %copy-start.4 = (bf16[1536,512]{1,0:T(8,128)(2,1)S(1)}, bf16[1536,512]{1,0:T(8,128)(2,1)}, u32[]{:S(2)}) copy-start(bf16[1536,512]{1,0:T(8,128)(2,1)} %all-gather.5.cloned.1.call-done) | copy-start | bytes 4718596
  141.2 6.1 %copy-start.9 = (bf16[256,512]{1,0:T(8,128)(2,1)S(1)}, bf16[256,512]{1,0:T(8,128)(2,1)}, u32[]{:S(2)}) copy-start(bf16[256,512]{1,0:T(8,128)(2,1)} %param.24) | copy-start | bytes 786436
Sparse Core Ops, SparseCore 0:
  68.0 12.0 all-gather.2
  95.7 9.7 reduce-scatter.2
  128.8 8.6 all-gather.4
  150.8 9.7 reduce-scatter.4
where the time goes:
time: 170 us; the launch traced here: 169 us
  blocking collectives  78.1 us (46%)
  waiting for transfers between devices  37.5 us (22%)
  matrix products  33.4 us (20%)
  between operations  13.9 us (8%)
  other arithmetic  3.83 us (2%)
  local copies, waits for them, and re-layouts  1.93 us (1%)
    all_to_all x1, blocking collectives, shards(): lax.all_to_all(packed, 'dom', split_axis=0, concat_axis=0, tiled=True)  55.4 us
    all_to_all x1, blocking collectives, shards(): lax.all_to_all(pick_rows(mesh_encoded, halo_index), 'dom', split_axis=0,...  20.5 us
    dot_general x5, matrix products, pick_rows(): jnp.dot(selector, table, preferred_element_type=jnp.float32)  20.3 us
    reduce_scatter x1, waiting for transfers between devices, shards(): lax.psum_scatter(proc_partial, 'feat', scatter_dimension=1, tiled=True)  9.91 us
    reduce_scatter x1, waiting for transfers between devices, shards(): lax.psum_scatter(partial_value, 'feat', scatter_dimension=1, tiled=True)  9.87 us
    all_gather x1, waiting for transfers between devices, shards(): slot_full = lax.all_gather(arrived, 'feat', axis=1, tiled=True)  9.07 us
    all_gather x1, waiting for transfers between devices, shards(): lax.all_gather(jnp.concatenate([mesh_encoded, halo_latent], axis=0), 'fea...  8.61 us
    dot_general x1, matrix products, shards(): jnp.dot(slot_full, w_grid_send, preferred_element_type=jnp.float32)  5.44 us
  transfers between devices with their start and end apart: 4, of which 4 were waited for; matrix products, arithmetic and copies ran while one was open for 0% of the time, Pallas kernels for 0%

commit v1 on v0

v1 whole, which is shorter than its diff:
```python
import jax
import jax.numpy as jnp
from jax import lax
from jax.sharding import PartitionSpec as P

BF16, F32 = jnp.bfloat16, jnp.float32


def dot(a, b):
    return jnp.dot(a, b, preferred_element_type=F32)


def hot_rows(index, width):
    return (index[:, None] == lax.broadcasted_iota(jnp.int32, (index.shape[0], width), 1)).astype(BF16)


def hot_columns(index, height):
    return (lax.broadcasted_iota(jnp.int32, (height, index.shape[0]), 0) == index[None, :]).astype(BF16)


def swap(x):
    return lax.ppermute(x, "feat", [(0, 1), (1, 0)])


def from_xor(x, bits, n_dom):
    return lax.ppermute(x, "dom", [(i, i ^ bits) for i in range(n_dom)])


def own_first(w, axis):
    return jnp.where(lax.axis_index("feat") == 0, w, jnp.roll(w, w.shape[axis] // 2, axis))


def silu_bf16(v):
    return (v / (1.0 + jnp.exp(-v))).astype(BF16)


def block(row, at, size):
    return lax.dynamic_slice_in_dim(row, at * size, size, 0)


def sums_by_halves(grid_proj, mesh_rproj, bias, send_grid, recv_row, n_dom):
    me = lax.axis_index("dom")
    half = n_dom // 2
    mesh_rows = mesh_rproj.shape[0]
    grid_rows = grid_proj.shape[0]
    cap = send_grid.shape[0] // n_dom
    width = grid_proj.shape[1] // 2
    send_mirror = from_xor(send_grid, half, n_dom)
    recv_near = [recv_row] + [from_xor(recv_row, k, n_dom) for k in range(1, half)]
    mirrored = [from_xor(grid_proj[:, c * width : (c + 1) * width], half, n_dom) for c in range(2)]
    table = jnp.concatenate([mesh_rproj] + [from_xor(mesh_rproj, k, n_dom) for k in range(1, half)], axis=0)

    def targets_of(sender, send_list):
        ids = jnp.concatenate([block(send_list, me ^ k, cap) for k in range(half)])
        rows = [block(recv_near[k], sender, cap) for k in range(half)]
        goal = jnp.concatenate([jnp.where(r < mesh_rows, r + (k * mesh_rows + 1), 0) for k, r in enumerate(rows)])
        match = lax.broadcasted_iota(jnp.int32, (grid_rows, ids.shape[0]), 0) == ids[None, :]
        return jnp.sum(jnp.where(match, goal[None, :], 0), axis=1) - 1

    goal_own = targets_of(me, send_grid)
    goal_mirror = targets_of(me ^ half, send_mirror)
    term_own = dot(hot_rows(goal_own, half * mesh_rows), table) + bias[None, :]
    term_mirror = dot(hot_rows(goal_mirror, half * mesh_rows), table) + bias[None, :]
    hidden_own = silu_bf16(grid_proj.astype(F32) + term_own)
    sum_own = dot(hot_columns(goal_own, half * mesh_rows), hidden_own)
    chunks = []
    for c in range(2):
        part = slice(c * width, (c + 1) * width)
        hidden = silu_bf16(mirrored[c].astype(F32) + term_mirror[:, part])
        total = sum_own[:, part] + dot(hot_columns(goal_mirror, half * mesh_rows), hidden)
        result = total[:mesh_rows]
        for k in range(1, half):
            result += from_xor(total[k * mesh_rows : (k + 1) * mesh_rows].astype(BF16), k, n_dom).astype(F32)
        chunks.append(result.astype(BF16))
    return chunks


def sums_by_all_to_all(grid_proj, mesh_rproj, bias, send_grid, recv_row, n_dom):
    packed = dot(hot_rows(send_grid, grid_proj.shape[0]), grid_proj).astype(BF16)
    arrived = lax.all_to_all(packed, "dom", split_axis=0, concat_axis=0, tiled=True)
    term = dot(hot_rows(recv_row, mesh_rproj.shape[0]), mesh_rproj) + bias[None, :]
    hidden = silu_bf16(arrived.astype(F32) + term)
    return [dot(hot_columns(recv_row, mesh_rproj.shape[0]), hidden).astype(BF16)]


def shards(
    grid_lat,
    mesh_lat,
    w_grid_send,
    w_grid_recv,
    g2m_bias,
    w_grid_out,
    w_edge_send,
    w_edge_recv,
    edge_bias,
    w_edge_out,
    send_grid,
    recv_row,
    halo_rows,
    edge_src,
    edge_dst,
):
    n_dom = lax.axis_size("dom")
    mesh_rows, feats = mesh_lat.shape
    grid_other = swap(grid_lat)
    mesh_other = swap(mesh_lat)
    w_send = own_first(w_grid_send, 0)
    w_recv = own_first(w_grid_recv, 0)
    grid_proj = (dot(grid_lat, w_send[:feats]) + dot(grid_other, w_send[feats:])).astype(BF16)
    mesh_rproj = (dot(mesh_lat, w_recv[:feats]) + dot(mesh_other, w_recv[feats:])).astype(BF16)
    w_out = own_first(w_grid_out, 1)
    w_out_other = own_first(swap(w_grid_out), 1)
    w_out2 = w_edge_out[:, :]
    w_out2_other = swap(w_edge_out)
    own_at = lax.axis_index("feat") * feats
    w_out2 = lax.dynamic_slice_in_dim(w_out2, own_at, feats, 1)
    w_out2_other = lax.dynamic_slice_in_dim(w_out2_other, own_at, feats, 1)
    w_edge = jnp.concatenate([own_first(w_edge_send, 0), own_first(w_edge_recv, 0)], axis=1)

    sums = sums_by_halves if n_dom == 8 else sums_by_all_to_all
    chunks = sums(grid_proj, mesh_rproj, g2m_bias, send_grid.reshape(-1), recv_row.reshape(-1), n_dom)

    update = jnp.zeros((mesh_rows, 2 * feats), F32)
    at = 0
    for chunk in chunks:
        rows = slice(at, at + chunk.shape[1])
        update += dot(chunk, w_out[rows]) + dot(swap(chunk), w_out_other[rows])
        at += chunk.shape[1]
    encoded = (jnp.concatenate([mesh_lat, mesh_other], axis=1).astype(F32) + update).astype(BF16)
    mesh_encoded = encoded[:, :feats]

    proj = dot(encoded, w_edge).astype(BF16)
    send_proj, recv_proj = proj[:, :feats], proj[:, feats:]
    halo_out = dot(hot_rows(halo_rows.reshape(-1), mesh_rows), send_proj).astype(BF16)
    halo_in = lax.all_to_all(halo_out, "dom", split_axis=0, concat_axis=0, tiled=True)

    senders = edge_src.reshape(-1)
    receivers = edge_dst.reshape(-1)
    near = (
        dot(hot_rows(senders, mesh_rows), send_proj)
        + dot(hot_rows(receivers, mesh_rows), recv_proj)
        + edge_bias[None, :]
    )
    far = dot(hot_rows(senders - mesh_rows, halo_in.shape[0]), halo_in)
    hidden = silu_bf16(near + far)
    proc_sum = dot(hot_columns(receivers, mesh_rows), hidden).astype(BF16)
    update = dot(proc_sum, w_out2) + dot(swap(proc_sum), w_out2_other)
    mesh_out = (mesh_encoded.astype(F32) + update).astype(BF16)
    return (mesh_encoded, mesh_out)


def solution(mesh):
    placed = (
        P(("member", "dom"), "feat"),
        P(("member", "dom"), "feat"),
        P(None, "feat"),
        P(None, "feat"),
        P("feat"),
        P("feat", None),
        P(None, "feat"),
        P(None, "feat"),
        P("feat"),
        P("feat", None),
        P("dom", None),
        P("dom", None),
        P("dom", None),
        P("dom", None),
        P("dom", None),
    )
    return jax.shard_map(
        shards,
        mesh=mesh,
        in_specs=placed,
        out_specs=(P(("member", "dom"), "feat"), P(("member", "dom"), "feat")),
        check_vma=False,
    )
```

time: 170 us -> 105 us (0.62)
  blocking collectives: 78.1 us -> 0 us
  starting transfers between devices: 0.34 us -> 27 us
  between operations: 13.9 us -> 1.13 us
  other arithmetic: 3.83 us -> 9.14 us
  matrix products: 33.4 us -> 29.1 us
  waiting for transfers between devices: 37.5 us -> 33.6 us
  local copies, waits for them, and re-layouts: 1.93 us -> 4.22 us
    all_to_all x2 -> x0, blocking collectives: 75.9 us -> none  [the longest x1 55.4 us: shards(): lax.all_to_all(packed, 'dom', split_axis=0, concat_axis=0, tiled=True)]
    ppermute x0 -> x22, starting transfers between devices: none -> 22.6 us  [the longest x15 21.8 us: from_xor(): return lax.ppermute(x, 'dom', [(i, i ^ bits) for i in range(n_dom)])]
    ppermute x0 -> x22, waiting for transfers between devices: none -> 20.9 us  [the longest x15 18.9 us: from_xor(): return lax.ppermute(x, 'dom', [(i, i ^ bits) for i in range(n_dom)])]
    reduce_scatter x2 -> x0, waiting for transfers between devices: 19.8 us -> none  [the longest x1 9.91 us: shards(): lax.psum_scatter(proc_partial, 'feat', scatter_dimension=1, tiled=True)]
    all_gather x2 -> x0, waiting for transfers between devices: 17.7 us -> none  [the longest x1 9.07 us: shards(): slot_full = lax.all_gather(arrived, 'feat', axis=1, tiled=True)]
    all_to_all x0 -> x1, waiting for transfers between devices: none -> 12.7 us  [shards(): lax.all_to_all(halo_out, 'dom', split_axis=0, concat_axis=0, tiled=True)]
    select_n x0 -> x9, other arithmetic: none -> 7.13 us  [the longest x5 4.15 us: own_first(): jnp.where(lax.axis_index('feat') == 0, w, jnp.roll(w, w.shape[axis] // 2,...]
    all_to_all x0 -> x1, starting transfers between devices: none -> 4.4 us  [shards(): lax.all_to_all(halo_out, 'dom', split_axis=0, concat_axis=0, tiled=True)]
  transfers between devices with their start and end apart: 4 -> 23, of which waited for: 4 -> 10; matrix products, arithmetic and copies ran while one was open for 0% -> 37% of each run, Pallas kernels for 0% -> 0%
where the time goes in v1:
time: 105 us; the launch traced here: 104 us
  waiting for transfers between devices  33.6 us (32%)
  matrix products  29.1 us (28%)
  starting transfers between devices  27 us (26%)
  other arithmetic  9.14 us (9%)
  local copies, waits for them, and re-layouts  4.22 us (4%)
  between operations  1.13 us (1%)
    dot_general x19, matrix products, dot(): return jnp.dot(a, b, preferred_element_type=F32)  29.1 us
    ppermute x15, starting transfers between devices, from_xor(): return lax.ppermute(x, 'dom', [(i, i ^ bits) for i in range(n_dom)])  21.8 us
    ppermute x15, waiting for transfers between devices, from_xor(): return lax.ppermute(x, 'dom', [(i, i ^ bits) for i in range(n_dom)])  18.9 us
    all_to_all x1, waiting for transfers between devices, shards(): lax.all_to_all(halo_out, 'dom', split_axis=0, concat_axis=0, tiled=True)  12.7 us
    all_to_all x1, starting transfers between devices, shards(): lax.all_to_all(halo_out, 'dom', split_axis=0, concat_axis=0, tiled=True)  4.4 us
    select_n x5, other arithmetic, own_first(): jnp.where(lax.axis_index('feat') == 0, w, jnp.roll(w, w.shape[axis] // 2,...  4.15 us
    slice x6, local copies, waits for them, and re-layouts, own_first(): jnp.roll(w, w.shape[axis] // 2, axis)  3.2 us
    select_n x4, other arithmetic, targets_of(): jnp.where(r < mesh_rows, r + (k * mesh_rows + 1), 0)  2.98 us
  transfers between devices with their start and end apart: 23, of which 10 were waited for; matrix products, arithmetic and copies ran while one was open for 37% of the time, Pallas kernels for 0%

profile of v1, /device:TPU:0, one launch (start us, length us, event | category | flops | bytes accessed | tf_op | source)
XLA Modules:
  0.0 104.2 jit_solution(10834412183644161611)
XLA Ops:
  0.6 3.0 %collective-permute-start.1 = (s32[4096]{0:T(1024)}, s32[4096]{0:T(1024)}, u32[]{:S(2)}, u32[]{:S(2)}) collective-permute-start(s32[4096]{0:T(1024)} %bitcast.39), channel_id=1, source_target_pairs={{0,2},{2,0},{4,6},{6,4},{8,10},{10,8},{12,14},{14,12},{1,3},{3,1},... | collective-permute-start | bytes 49160 | tf_op jit(solution)/shard_map/ppermute | solution.py:26
  3.6 1.6 %collective-permute-start.2 = (s32[4096]{0:T(1024)}, s32[4096]{0:T(1024)}, u32[]{:S(2)}, u32[]{:S(2)}) collective-permute-start(s32[4096]{0:T(1024)} %bitcast.40), channel_id=1, source_target_pairs={{0,4},{2,6},{4,0},{6,2},{8,12},{10,14},{12,8},{14,10},{1,5},{3,7},... | collective-permute-start | bytes 49160 | tf_op jit(solution)/shard_map/ppermute | solution.py:26
  5.2 0.5 collective-permute-start.4
  5.7 1.0 %fusion.87 = (bf16[256,256]{1,0:T(8,128)(2,1)S(1)}, bf16[256,256]{1,0:T(8,128)(2,1)S(1)}) fusion(bf16[512,256]{1,0:T(8,128)(2,1)} %param.18), kind=kLoop, calls=%fused_computation.137 | loop fusion | bytes 524288 | tf_op jit(solution)/shard_map/jit(_roll_static)/slice | solution.py:30
  6.8 1.0 maximum_select_fusion.1
  7.8 1.3 %fusion.62 = f32[256,512]{1,0:T(8,128)S(1)} fusion(bf16[512,256]{1,0:T(8,128)(2,1)} %param.16, bf16[512,256]{1,0:T(8,128)(2,1)S(1)} %maximum_select_fusion.1), kind=kOutput, calls=%fused_computation.94 | convolution fusion | flops 67108864 | bytes 917504 | tf_op jit(solution)/shard_map/dot_general | solution.py:10
  9.6 0.7 fusion.85
  10.3 0.7 fusion.83
  11.0 0.7 fusion.84
  11.7 1.0 maximum_select_fusion.2
  12.8 2.0 %maximum_select_fusion.4 = (bf16[512,256]{1,0:T(8,128)(2,1)}, bf16[512,256]{1,0:T(8,128)(2,1)}) fusion(bf16[512,256]{1,0:T(8,128)(2,1)S(1)} %copy-done.1, bf16[256,256]{1,0:T(8,128)(2,1)} %get-tuple-element.11, bf16[256,256]{1,0:T(8,128)(2,1)S(1)} %get-tuple-element.10, pred[]{:T(512)S(6)} %eq.110, bf16[512,256]{1,0:T(8,128)(2,1)S(1)} %copy-done.2, ...), kind=kLoop, calls=%fused_computation.81 | loop fusion | flops 1310720 | bytes 1572865 | tf_op jit(solution)/shard_map/jit(_where)/select_n | solution.py:30
  14.8 0.7 compare_select_fusion.1
  15.6 0.8 add_select_fusion.5
  16.3 3.0 %collective-permute-start.8 = (s32[4096]{0:T(1024)S(1)}, s32[4096]{0:T(1024)S(1)}, u32[]{:S(2)}, u32[]{:S(2)}) collective-permute-start(s32[4096]{0:T(1024)S(1)} %bitcast.38), channel_id=1, source_target_pairs={{0,8},{2,10},{4,12},{6,14},{8,0},{10,2},{12,4},{14,6},{1,9},{3,11}... | collective-permute-start | bytes 49160 | tf_op jit(solution)/shard_map/ppermute | solution.py:26
  19.4 0.8 add_select_fusion.4
  20.1 0.8 add_select_fusion.3
  20.9 0.9 select_reduce_fusion.1
  21.9 0.9 select_reduce_fusion
  23.1 1.6 %collective-permute-start.5 = (bf16[512,256]{0,1:T(8,128)(2,1)S(1)}, bf16[512,256]{0,1:T(8,128)(2,1)S(1)}, u32[]{:S(2)}, u32[]{:S(2)}) collective-permute-start(bf16[512,256]{0,1:T(8,128)(2,1)S(1)} %fusion.34), channel_id=1, source_target_pairs={{0,2},{2,0},{4,6},{6,4},{8,10},{10,8},{12,14},{14,12},{1,3},{3,1},... | collective-permute-start | bytes 786440 | tf_op jit(solution)/shard_map/ppermute | solution.py:26
  24.7 1.6 %collective-permute-start.6 = (bf16[512,256]{0,1:T(8,128)(2,1)S(1)}, bf16[512,256]{0,1:T(8,128)(2,1)S(1)}, u32[]{:S(2)}, u32[]{:S(2)}) collective-permute-start(bf16[512,256]{0,1:T(8,128)(2,1)S(1)} %fusion.34), channel_id=1, source_target_pairs={{0,4},{2,6},{4,0},{6,2},{8,12},{10,14},{12,8},{14,10},{1,5},{3,7},... | collective-permute-start | bytes 786440 | tf_op jit(solution)/shard_map/ppermute | solution.py:26
  26.8 1.4 %fusion.29 = bf16[1024,256]{0,1:T(8,128)(2,1)S(1)} fusion(f32[256,1024]{1,0:T(8,128)S(1)} %fusion.65, bf16[1024,256]{1,0:T(8,128)(2,1)} %collective-permute-done.4, bf16[512,256]{1,0:T(8,128)(2,1)S(1)} %maximum_select_fusion), kind=kOutput, calls=%fused_computation.47 | convolution fusion | flops 134742016 | bytes 2228224 | tf_op jit(solution)/shard_map/dot_general | solution.py:10
  28.3 2.2 %collective-permute-start.9 = (bf16[1024,128]{0,1:T(8,128)(2,1)S(1)}, bf16[1024,128]{0,1:T(8,128)(2,1)S(1)}, u32[]{:S(2)}, u32[]{:S(2)}) collective-permute-start(bf16[1024,128]{0,1:T(8,128)(2,1)S(1)} %get-tuple-element.5), channel_id=1, source_target_pairs={{0,8},{2,10},{4,12},{6,14},{8,0},{10,2},{12,4},{14,6},{1,9},{3,11}... | collective-permute-start | bytes 786440 | tf_op jit(solution)/shard_map/ppermute | solution.py:26
  30.5 0.7 collective-permute-start.15
  31.6 10.3 %collective-permute-done.6 = bf16[512,256]{0,1:T(8,128)(2,1)S(1)} collective-permute-done((bf16[512,256]{0,1:T(8,128)(2,1)S(1)}, bf16[512,256]{0,1:T(8,128)(2,1)S(1)}, u32[]{:S(2)}, u32[]{:S(2)}) %collective-permute-start.6) | collective-permute-done | bytes 262176 | tf_op jit(solution)/shard_map/ppermute | solution.py:26
  42.0 0.7 copy-done.12
  42.7 3.0 %collective-permute-done.7 = bf16[512,256]{0,1:T(8,128)(2,1)} collective-permute-done((bf16[512,256]{0,1:T(8,128)(2,1)S(1)}, bf16[512,256]{0,1:T(8,128)(2,1)}, u32[]{:S(2)}, u32[]{:S(2)}) %collective-permute-start.7) | collective-permute-done | bytes 262176 | tf_op jit(solution)/shard_map/ppermute | solution.py:26
  45.6 5.9 %fusion.2 = f32[2048,256]{1,0:T(8,128)} fusion(s32[1024]{0:T(1024)S(1)} %broadcast_add_fusion.2, bf16[1024,256]{0,1:T(8,128)(2,1)S(1)} %fusion.29, f32[256]{0:T(256)S(1)} %copy-done.16, bf16[512,256]{0,1:T(8,128)(2,1)} %collective-permute-done.7, bf16[512,256]{0,1:T(8,128)(2,1)} %copy-done.12, bf16[512,256]{0,1:T(8,128)(2,1)S(1)} %collective-permute-done.5, ...), kind=kOutput, calls=%fused_computation.11 | convolution fusion | flops 2157707264 | bytes 3675136 | tf_op jit(solution)/shard_map/dot_general | solution.py:10
  51.6 3.0 %fusion.25 = f32[1024,256]{0,1:T(8,128)S(1)} fusion(s32[1024]{0:T(1024)S(1)} %broadcast_add_fusion.1, f32[256]{0:T(256)S(1)} %copy-done.16, bf16[512,256]{0,1:T(8,128)(2,1)} %collective-permute-done.7, bf16[512,256]{0,1:T(8,128)(2,1)S(1)} %copy-done.13, bf16[512,256]{0,1:T(8,128)(2,1)S(1)} %collective-permute-done.5, bf16[512,256]{0,1:T(8,128)(2,1)S(1)} %fusion.34), kind=kOutput, calls=%fused_computation.42 | convolution fusion | flops 1080295424 | bytes 2102272 | tf_op jit(solution)/shard_map/dot_general | solution.py:10
  54.6 1.7 %fusion.90 = (bf16[2048,128]{1,0:T(8,128)(2,1)S(1)}, f32[2048,128]{1,0:T(8,128)S(1)}) fusion(f32[1024,256]{0,1:T(8,128)S(1)} %fusion.25, bf16[1024,128]{0,1:T(8,128)(2,1)S(1)} %collective-permute-done.15, s32[1024]{0:T(1024)S(1)} %broadcast_add_fusion.1, f32[2048,256]{1,0:T(8,128)S(1)} %copy-done.18), kind=kOutput, calls=%fused_computation.140 | convolution fusion | flops 540278784 | bytes 3411968 | tf_op jit(solution)/shard_map/dot_general | solution.py:10
  56.3 2.5 %collective-permute-start.16 = (bf16[512,128]{1,0:T(8,128)(2,1)S(1)}, bf16[512,128]{1,0:T(8,128)(2,1)S(1)}, u32[]{:S(2)}, u32[]{:S(2)}) collective-permute-start(bf16[512,128]{1,0:T(8,128)(2,1)S(1)} %get-tuple-element.7), channel_id=1, source_target_pairs={{0,2},{2,0},{4,6},{6,4},{8,10},{10,8},{12,14},{14,12},{1,3},{3,1},... | collective-permute-start | bytes 393224 | tf_op jit(solution)/shard_map/ppermute | solution.py:26
  58.8 1.5 %collective-permute-start.18 = (bf16[512,128]{1,0:T(8,128)(2,1)S(1)}, bf16[512,128]{1,0:T(8,128)(2,1)S(1)}, u32[]{:S(2)}, u32[]{:S(2)}) collective-permute-start(bf16[512,128]{1,0:T(8,128)(2,1)S(1)} %get-tuple-element.8), channel_id=1, source_target_pairs={{0,6},{2,4},{4,2},{6,0},{8,14},{10,12},{12,10},{14,8},{1,7},{3,5},... | collective-permute-start | bytes 393224 | tf_op jit(solution)/shard_map/ppermute | solution.py:26
  60.3 1.8 %fusion.91 = (bf16[2048,128]{1,0:T(8,128)(2,1)S(1)}, f32[2048,128]{1,0:T(8,128)S(1)}) fusion(f32[1024,256]{0,1:T(8,128)S(1)} %fusion.25, bf16[1024,128]{0,1:T(8,128)(2,1)S(1)} %collective-permute-done.9, s32[1024]{0:T(1024)S(1)} %broadcast_add_fusion.1, f32[2048,256]{1,0:T(8,128)S(1)} %copy-done.18), kind=kOutput, calls=%fused_computation.141 | convolution fusion | flops 540278784 | bytes 3411968 | tf_op jit(solution)/shard_map/dot_general | solution.py:10
  62.2 2.0 %collective-permute-start.10 = (bf16[512,128]{1,0:T(8,128)(2,1)S(1)}, bf16[512,128]{1,0:T(8,128)(2,1)S(1)}, u32[]{:S(2)}, u32[]{:S(2)}) collective-permute-start(bf16[512,128]{1,0:T(8,128)(2,1)S(1)} %get-tuple-element.2), channel_id=1, source_target_pairs={{0,2},{2,0},{4,6},{6,4},{8,10},{10,8},{12,14},{14,12},{1,3},{3,1},... | collective-permute-start | bytes 393224 | tf_op jit(solution)/shard_map/ppermute | solution.py:26
  64.3 1.5 %collective-permute-start.12 = (bf16[512,128]{1,0:T(8,128)(2,1)S(1)}, bf16[512,128]{1,0:T(8,128)(2,1)S(1)}, u32[]{:S(2)}, u32[]{:S(2)}) collective-permute-start(bf16[512,128]{1,0:T(8,128)(2,1)S(1)} %get-tuple-element.3), channel_id=1, source_target_pairs={{0,6},{2,4},{4,2},{6,0},{8,14},{10,12},{12,10},{14,8},{1,7},{3,5},... | collective-permute-start | bytes 393224 | tf_op jit(solution)/shard_map/ppermute | solution.py:26
  65.8 0.7 collective-permute-done.18
  66.7 2.1 %collective-permute-done.10 = bf16[512,128]{1,0:T(8,128)(2,1)S(1)} collective-permute-done((bf16[512,128]{1,0:T(8,128)(2,1)S(1)}, bf16[512,128]{1,0:T(8,128)(2,1)S(1)}, u32[]{:S(2)}, u32[]{:S(2)}) %collective-permute-start.10) | collective-permute-done | bytes 131104 | tf_op jit(solution)/shard_map/ppermute | solution.py:26
  68.8 1.2 %collective-permute-done.11 = bf16[512,128]{1,0:T(8,128)(2,1)S(1)} collective-permute-done((bf16[512,128]{1,0:T(8,128)(2,1)S(1)}, bf16[512,128]{1,0:T(8,128)(2,1)S(1)}, u32[]{:S(2)}, u32[]{:S(2)}) %collective-permute-start.11) | collective-permute-done | bytes 131104 | tf_op jit(solution)/shard_map/ppermute | solution.py:26
  70.0 1.2 %collective-permute-done.12 = bf16[512,128]{1,0:T(8,128)(2,1)S(1)} collective-permute-done((bf16[512,128]{1,0:T(8,128)(2,1)S(1)}, bf16[512,128]{1,0:T(8,128)(2,1)S(1)}, u32[]{:S(2)}, u32[]{:S(2)}) %collective-permute-start.12) | collective-permute-done | bytes 131104 | tf_op jit(solution)/shard_map/ppermute | solution.py:26
  72.0 0.7 collective-permute-done.13
  73.4 0.4 convolution_convert_fusion
  73.8 1.3 %fusion.27 = bf16[1024,256]{1,0:T(8,128)(2,1)} fusion(s32[1024]{0:T(1024)S(1)} %bitcast.43, bf16[512,512]{1,0:T(8,128)(2,1)S(1)} %convolution_convert_fusion), kind=kOutput, calls=%fused_computation.45 | convolution fusion | flops 269221888 | bytes 790528 | tf_op jit(solution)/shard_map/dot_general | solution.py:10
  75.1 4.4 %all-to-all-start = ((bf16[8,128,256]{2,1,0:T(8,128)(2,1)}), bf16[8,128,256]{2,1,0:T(8,128)(2,1)S(1)}, u32[]{:S(2)}, u32[]{:S(2)}) async-start(bf16[8,128,256]{2,1,0:T(8,128)(2,1)} %bitcast.13), calls=%async_computation | async-start | bytes 1048576 | tf_op jit(solution)/shard_map/all_to_all | solution.py:135
  79.6 2.0 %fusion.13 = f32[2048,256]{1,0:T(8,128)} fusion(s32[2048]{0:T(1024)S(1)} %bitcast.31, bf16[512,512]{1,0:T(8,128)(2,1)S(1)} %convolution_convert_fusion), kind=kOutput, calls=%fused_computation.25 | convolution fusion | flops 537919488 | bytes 2367488 | tf_op jit(solution)/shard_map/dot_general | solution.py:10
  81.7 12.7 %all-to-all-done = bf16[8,128,256]{2,1,0:T(8,128)(2,1)S(1)} async-done(((bf16[8,128,256]{2,1,0:T(8,128)(2,1)}), bf16[8,128,256]{2,1,0:T(8,128)(2,1)S(1)}, u32[]{:S(2)}, u32[]{:S(2)}) %all-to-all-start) | async-done | bytes 524320 | tf_op jit(solution)/shard_map/all_to_all | solution.py:135
  94.3 2.7 %fusion.5 = f32[2048,256]{1,0:T(8,128)} fusion(bf16[1024,256]{1,0:T(8,128)(2,1)S(1)} %bitcast.30, s32[2048]{0:T(1024)S(1)} %broadcast_add_fusion), kind=kOutput, calls=%fused_computation.14 | convolution fusion | flops 1075838976 | bytes 2629632 | tf_op jit(solution)/shard_map/dot_general | solution.py:10
  97.0 4.6 %fusion.33 = bf16[512,256]{1,0:T(8,128)(2,1)S(1)} fusion(s32[2048]{0:T(1024)S(1)} %bitcast.42, f32[2048,256]{1,0:T(8,128)} %fusion.5, f32[2048,256]{1,0:T(8,128)} %fusion.13, f32[256]{0:T(256)S(1)} %copy-done.17, bf16[512,512]{1,0:T(8,128)(2,1)S(1)} %convolution_convert_fusion), kind=kOutput, calls=%fused_computation.53 | convolution fusion | flops 1079640064 | bytes 4736000 | tf_op jit(solution)/shard_map/dot_general | solution.py:10
  102.0 1.2 %collective-permute-done.20 = bf16[512,256]{1,0:T(8,128)(2,1)S(1)} collective-permute-done((bf16[512,256]{1,0:T(8,128)(2,1)S(1)}, bf16[512,256]{1,0:T(8,128)(2,1)S(1)}, u32[]{:S(2)}, u32[]{:S(2)}) %collective-permute-start.20) | collective-permute-done | bytes 262176 | tf_op jit(solution)/shard_map/ppermute | solution.py:22
  103.2 0.9 fusion.31
  (86 shorter events, 3.8 us)
Async XLA Ops:
  0.6 8.5 %copy-start = (bf16[512,256]{1,0:T(8,128)(2,1)S(1)}, bf16[512,256]{1,0:T(8,128)(2,1)}, u32[]{:S(2)}) copy-start(bf16[512,256]{1,0:T(8,128)(2,1)} %param.17) | copy-start | bytes 786436
  0.6 14.9 %collective-permute-start.1 = (s32[4096]{0:T(1024)}, s32[4096]{0:T(1024)}, u32[]{:S(2)}, u32[]{:S(2)}) collective-permute-start(s32[4096]{0:T(1024)} %bitcast.39), channel_id=1, source_target_pairs={{0,2},{2,0},{4,6},{6,4},{8,10},{10,8},{12,14},{14,12},{1,3},{3,1},... | collective-permute-start | bytes 49160 | tf_op jit(solution)/shard_map/ppermute | solution.py:26
  3.6 12.7 %collective-permute-start.2 = (s32[4096]{0:T(1024)}, s32[4096]{0:T(1024)}, u32[]{:S(2)}, u32[]{:S(2)}) collective-permute-start(s32[4096]{0:T(1024)} %bitcast.40), channel_id=1, source_target_pairs={{0,4},{2,6},{4,0},{6,2},{8,12},{10,14},{12,8},{14,10},{1,5},{3,7},... | collective-permute-start | bytes 49160 | tf_op jit(solution)/shard_map/ppermute | solution.py:26
  5.2 14.9 %collective-permute-start.3 = (s32[4096]{0:T(1024)}, s32[4096]{0:T(1024)}, u32[]{:S(2)}, u32[]{:S(2)}) collective-permute-start(s32[4096]{0:T(1024)} %bitcast.41), channel_id=1, source_target_pairs={{0,6},{2,4},{4,2},{6,0},{8,14},{10,12},{12,10},{14,8},{1,7},{3,5},... | collective-permute-start | bytes 49160 | tf_op jit(solution)/shard_map/ppermute | solution.py:26
  5.2 17.6 %collective-permute-start = (bf16[512,256]{1,0:T(8,128)(2,1)}, bf16[512,256]{1,0:T(8,128)(2,1)S(1)}, u32[]{:S(2)}, u32[]{:S(2)}) collective-permute-start(bf16[512,256]{1,0:T(8,128)(2,1)} %param.16), channel_id=1, source_target_pairs={{0,1},{1,0},{2,3},{3,2},{4,5},{5,4},{6,7},{7,6},{8,9},{9,8},{10,11... | collective-permute-start | bytes 786440 | tf_op jit(solution)/shard_map/ppermute | solution.py:22
  5.2 21.6 %collective-permute-start.4 = (bf16[1024,256]{1,0:T(8,128)(2,1)}, bf16[1024,256]{1,0:T(8,128)(2,1)}, u32[]{:S(2)}, u32[]{:S(2)}) collective-permute-start(bf16[1024,256]{1,0:T(8,128)(2,1)} %param.15), channel_id=1, source_target_pairs={{0,1},{1,0},{2,3},{3,2},{4,5},{5,4},{6,7},{7,6},{8,9},{9,8},{10,11... | collective-permute-start | bytes 1572872 | tf_op jit(solution)/shard_map/ppermute | solution.py:22
  5.7 3.5 %copy-start.6 = (bf16[1024,256]{1,0:T(8,128)(2,1)S(1)}, bf16[1024,256]{1,0:T(8,128)(2,1)}, u32[]{:S(2)}) copy-start(bf16[1024,256]{1,0:T(8,128)(2,1)} %param.15) | copy-start | bytes 1572868
  7.8 1.8 %copy-start.3 = (bf16[256,512]{1,0:T(8,128)(2,1)S(1)}, bf16[256,512]{1,0:T(8,128)(2,1)}, u32[]{:S(2)}) copy-start(bf16[256,512]{1,0:T(8,128)(2,1)} %param.20) | copy-start | bytes 786436
  7.8 2.5 %copy-start.1 = (bf16[512,256]{1,0:T(8,128)(2,1)S(1)}, bf16[512,256]{1,0:T(8,128)(2,1)}, u32[]{:S(2)}) copy-start(bf16[512,256]{1,0:T(8,128)(2,1)} %param.21) | copy-start | bytes 786436
  9.1 1.9 %copy-start.2 = (bf16[512,256]{1,0:T(8,128)(2,1)S(1)}, bf16[512,256]{1,0:T(8,128)(2,1)}, u32[]{:S(2)}) copy-start(bf16[512,256]{1,0:T(8,128)(2,1)} %param.22) | copy-start | bytes 786436
  9.2 3.5 %copy-start.11 = (s32[1,4096]{1,0:T(1,128)S(1)}, s32[1,4096]{1,0:T(1,128)}, u32[]{:S(2)}) copy-start(s32[1,4096]{1,0:T(1,128)} %param.25) | copy-start | bytes 49156
  15.5 11.2 %collective-permute-start.14 = (bf16[256,512]{1,0:T(8,128)(2,1)S(1)}, bf16[256,512]{1,0:T(8,128)(2,1)S(1)}, u32[]{:S(2)}, u32[]{:S(2)}) collective-permute-start(bf16[256,512]{1,0:T(8,128)(2,1)S(1)} %copy-done.3), channel_id=1, source_target_pairs={{0,1},{1,0},{2,3},{3,2},{4,5},{5,4},{6,7},{7,6},{8,9},{9,8},{10,11... | collective-permute-start | bytes 786440 | tf_op jit(solution)/shard_map/ppermute | solution.py:22
  16.3 5.5 %collective-permute-start.8 = (s32[4096]{0:T(1024)S(1)}, s32[4096]{0:T(1024)S(1)}, u32[]{:S(2)}, u32[]{:S(2)}) collective-permute-start(s32[4096]{0:T(1024)S(1)} %bitcast.38), channel_id=1, source_target_pairs={{0,8},{2,10},{4,12},{6,14},{8,0},{10,2},{12,4},{14,6},{1,9},{3,11}... | collective-permute-start | bytes 49160 | tf_op jit(solution)/shard_map/ppermute | solution.py:26
  23.1 8.5 %collective-permute-start.5 = (bf16[512,256]{0,1:T(8,128)(2,1)S(1)}, bf16[512,256]{0,1:T(8,128)(2,1)S(1)}, u32[]{:S(2)}, u32[]{:S(2)}) collective-permute-start(bf16[512,256]{0,1:T(8,128)(2,1)S(1)} %fusion.34), channel_id=1, source_target_pairs={{0,2},{2,0},{4,6},{6,4},{8,10},{10,8},{12,14},{14,12},{1,3},{3,1},... | collective-permute-start | bytes 786440 | tf_op jit(solution)/shard_map/ppermute | solution.py:26
  24.7 17.2 %collective-permute-start.6 = (bf16[512,256]{0,1:T(8,128)(2,1)S(1)}, bf16[512,256]{0,1:T(8,128)(2,1)S(1)}, u32[]{:S(2)}, u32[]{:S(2)}) collective-permute-start(bf16[512,256]{0,1:T(8,128)(2,1)S(1)} %fusion.34), channel_id=1, source_target_pairs={{0,4},{2,6},{4,0},{6,2},{8,12},{10,14},{12,8},{14,10},{1,5},{3,7},... | collective-permute-start | bytes 786440 | tf_op jit(solution)/shard_map/ppermute | solution.py:26
  26.3 19.3 %collective-permute-start.7 = (bf16[512,256]{0,1:T(8,128)(2,1)S(1)}, bf16[512,256]{0,1:T(8,128)(2,1)}, u32[]{:S(2)}, u32[]{:S(2)}) collective-permute-start(bf16[512,256]{0,1:T(8,128)(2,1)S(1)} %fusion.34), channel_id=1, source_target_pairs={{0,6},{2,4},{4,2},{6,0},{8,14},{10,12},{12,10},{14,8},{1,7},{3,5},... | collective-permute-start | bytes 786440 | tf_op jit(solution)/shard_map/ppermute | solution.py:26
  26.7 18.9 %copy-start.16 = (f32[256]{0:T(256)S(1)}, f32[256]{0:T(256)}, u32[]{:S(2)}) copy-start(f32[256]{0:T(256)} %param.19) | copy-start | bytes 3076
  28.3 32.1 %collective-permute-start.9 = (bf16[1024,128]{0,1:T(8,128)(2,1)S(1)}, bf16[1024,128]{0,1:T(8,128)(2,1)S(1)}, u32[]{:S(2)}, u32[]{:S(2)}) collective-permute-start(bf16[1024,128]{0,1:T(8,128)(2,1)S(1)} %get-tuple-element.5), channel_id=1, source_target_pairs={{0,8},{2,10},{4,12},{6,14},{8,0},{10,2},{12,4},{14,6},{1,9},{3,11}... | collective-permute-start | bytes 786440 | tf_op jit(solution)/shard_map/ppermute | solution.py:26
  30.5 24.0 %collective-permute-start.15 = (bf16[1024,128]{0,1:T(8,128)(2,1)S(1)}, bf16[1024,128]{0,1:T(8,128)(2,1)S(1)}, u32[]{:S(2)}, u32[]{:S(2)}) collective-permute-start(bf16[1024,128]{0,1:T(8,128)(2,1)S(1)} %get-tuple-element.6), channel_id=1, source_target_pairs={{0,8},{2,10},{4,12},{6,14},{8,0},{10,2},{12,4},{14,6},{1,9},{3,11}... | collective-permute-start | bytes 786440 | tf_op jit(solution)/shard_map/ppermute | solution.py:26
  41.9 0.7 copy-start.12
  45.6 5.9 %copy-start.13 = (bf16[512,256]{0,1:T(8,128)(2,1)S(1)}, bf16[512,256]{0,1:T(8,128)(2,1)}, u32[]{:S(2)}) copy-start(bf16[512,256]{0,1:T(8,128)(2,1)} %copy-done.12) | copy-start | bytes 786436
  51.6 3.0 %copy-start.18 = (f32[2048,256]{1,0:T(8,128)S(1)}, f32[2048,256]{1,0:T(8,128)}, u32[]{:S(2)}) copy-start(f32[2048,256]{1,0:T(8,128)} %fusion.2) | copy-start | bytes 6291460
  56.3 8.0 %collective-permute-start.16 = (bf16[512,128]{1,0:T(8,128)(2,1)S(1)}, bf16[512,128]{1,0:T(8,128)(2,1)S(1)}, u32[]{:S(2)}, u32[]{:S(2)}) collective-permute-start(bf16[512,128]{1,0:T(8,128)(2,1)S(1)} %get-tuple-element.7), channel_id=1, source_target_pairs={{0,2},{2,0},{4,6},{6,4},{8,10},{10,8},{12,14},{14,12},{1,3},{3,1},... | collective-permute-start | bytes 393224 | tf_op jit(solution)/shard_map/ppermute | solution.py:26
  58.8 7.0 %collective-permute-start.17 = (bf16[512,128]{1,0:T(8,128)(2,1)S(1)}, bf16[512,128]{1,0:T(8,128)(2,1)S(1)}, u32[]{:S(2)}, u32[]{:S(2)}) collective-permute-start(bf16[512,128]{1,0:T(8,128)(2,1)S(1)} %get-tuple-element.9), channel_id=1, source_target_pairs={{0,4},{2,6},{4,0},{6,2},{8,12},{10,14},{12,8},{14,10},{1,5},{3,7},... | collective-permute-start | bytes 393224 | tf_op jit(solution)/shard_map/ppermute | solution.py:26
  58.8 7.7 %collective-permute-start.18 = (bf16[512,128]{1,0:T(8,128)(2,1)S(1)}, bf16[512,128]{1,0:T(8,128)(2,1)S(1)}, u32[]{:S(2)}, u32[]{:S(2)}) collective-permute-start(bf16[512,128]{1,0:T(8,128)(2,1)S(1)} %get-tuple-element.8), channel_id=1, source_target_pairs={{0,6},{2,4},{4,2},{6,0},{8,14},{10,12},{12,10},{14,8},{1,7},{3,5},... | collective-permute-start | bytes 393224 | tf_op jit(solution)/shard_map/ppermute | solution.py:26
  62.2 6.6 %collective-permute-start.10 = (bf16[512,128]{1,0:T(8,128)(2,1)S(1)}, bf16[512,128]{1,0:T(8,128)(2,1)S(1)}, u32[]{:S(2)}, u32[]{:S(2)}) collective-permute-start(bf16[512,128]{1,0:T(8,128)(2,1)S(1)} %get-tuple-element.2), channel_id=1, source_target_pairs={{0,2},{2,0},{4,6},{6,4},{8,10},{10,8},{12,14},{14,12},{1,3},{3,1},... | collective-permute-start | bytes 393224 | tf_op jit(solution)/shard_map/ppermute | solution.py:26
  64.2 5.8 %collective-permute-start.11 = (bf16[512,128]{1,0:T(8,128)(2,1)S(1)}, bf16[512,128]{1,0:T(8,128)(2,1)S(1)}, u32[]{:S(2)}, u32[]{:S(2)}) collective-permute-start(bf16[512,128]{1,0:T(8,128)(2,1)S(1)} %get-tuple-element.4), channel_id=1, source_target_pairs={{0,4},{2,6},{4,0},{6,2},{8,12},{10,14},{12,8},{14,10},{1,5},{3,7},... | collective-permute-start | bytes 393224 | tf_op jit(solution)/shard_map/ppermute | solution.py:26
  64.3 7.0 %collective-permute-start.12 = (bf16[512,128]{1,0:T(8,128)(2,1)S(1)}, bf16[512,128]{1,0:T(8,128)(2,1)S(1)}, u32[]{:S(2)}, u32[]{:S(2)}) collective-permute-start(bf16[512,128]{1,0:T(8,128)(2,1)S(1)} %get-tuple-element.3), channel_id=1, source_target_pairs={{0,6},{2,4},{4,2},{6,0},{8,14},{10,12},{12,10},{14,8},{1,7},{3,5},... | collective-permute-start | bytes 393224 | tf_op jit(solution)/shard_map/ppermute | solution.py:26
  66.6 4.8 %collective-permute-start.19 = (bf16[512,128]{1,0:T(8,128)(2,1)S(1)}, bf16[512,128]{1,0:T(8,128)(2,1)S(1)}, u32[]{:S(2)}, u32[]{:S(2)}) collective-permute-start(bf16[512,128]{1,0:T(8,128)(2,1)S(1)} %fusion.45), channel_id=1, source_target_pairs={{0,1},{1,0},{2,3},{3,2},{4,5},{5,4},{6,7},{7,6},{8,9},{9,8},{10,11... | collective-permute-start | bytes 393224 | tf_op jit(solution)/shard_map/ppermute | solution.py:22
  71.3 1.4 %collective-permute-start.13 = (bf16[512,128]{1,0:T(8,128)(2,1)S(1)}, bf16[512,128]{1,0:T(8,128)(2,1)S(1)}, u32[]{:S(2)}, u32[]{:S(2)}) collective-permute-start(bf16[512,128]{1,0:T(8,128)(2,1)S(1)} %fusion.48), channel_id=1, source_target_pairs={{0,1},{1,0},{2,3},{3,2},{4,5},{5,4},{6,7},{7,6},{8,9},{9,8},{10,11... | collective-permute-start | bytes 393224 | tf_op jit(solution)/shard_map/ppermute | solution.py:22
  71.7 1.3 %copy-start.5 = (bf16[512,256]{1,0:T(8,128)(2,1)S(1)}, bf16[512,256]{1,0:T(8,128)(2,1)}, u32[]{:S(2)}) copy-start(bf16[512,256]{1,0:T(8,128)(2,1)} %param.16) | copy-start | bytes 786436
  72.0 1.4 %copy-start.7 = (bf16[512,256]{1,0:T(8,128)(2,1)S(1)}, bf16[512,256]{1,0:T(8,128)(2,1)}, u32[]{:S(2)}) copy-start(bf16[512,256]{1,0:T(8,128)(2,1)} %get-tuple-element.44) | copy-start | bytes 786436
  72.0 1.4 %copy-start.8 = (bf16[512,256]{1,0:T(8,128)(2,1)S(1)}, bf16[512,256]{1,0:T(8,128)(2,1)}, u32[]{:S(2)}) copy-start(bf16[512,256]{1,0:T(8,128)(2,1)} %get-tuple-element.45) | copy-start | bytes 786436
  73.0 0.8 copy-start.15
  73.3 6.2 %copy-start.9 = (bf16[256,512]{1,0:T(8,128)(2,1)S(1)}, bf16[256,512]{1,0:T(8,128)(2,1)}, u32[]{:S(2)}) copy-start(bf16[256,512]{1,0:T(8,128)(2,1)} %param.24) | copy-start | bytes 786436
  73.4 6.3 %copy-start.10 = (s32[16,128]{1,0:T(8,128)S(1)}, s32[16,128]{1,0:T(8,128)}, u32[]{:S(2)}) copy-start(s32[16,128]{1,0:T(8,128)} %param.28) | copy-start | bytes 24580
  75.1 19.2 %all-to-all-start = ((bf16[8,128,256]{2,1,0:T(8,128)(2,1)}), bf16[8,128,256]{2,1,0:T(8,128)(2,1)S(1)}, u32[]{:S(2)}, u32[]{:S(2)}) async-start(bf16[8,128,256]{2,1,0:T(8,128)(2,1)} %bitcast.13), calls=%async_computation | async-start | bytes 1048576 | tf_op jit(solution)/shard_map/all_to_all | solution.py:135
  79.5 22.4 %collective-permute-start.21 = (bf16[256,512]{1,0:T(8,128)(2,1)S(1)}, bf16[256,512]{1,0:T(8,128)(2,1)S(1)}, u32[]{:S(2)}, u32[]{:S(2)}) collective-permute-start(bf16[256,512]{1,0:T(8,128)(2,1)S(1)} %copy-done.9), channel_id=1, source_target_pairs={{0,1},{1,0},{2,3},{3,2},{4,5},{5,4},{6,7},{7,6},{8,9},{9,8},{10,11... | collective-permute-start | bytes 786440 | tf_op jit(solution)/shard_map/ppermute | solution.py:22
  94.3 2.7 %copy-start.14 = (s32[16,128]{1,0:T(8,128)S(1)}, s32[16,128]{1,0:T(8,128)}, u32[]{:S(2)}) copy-start(s32[16,128]{1,0:T(8,128)} %param.29) | copy-start | bytes 24580
  94.3 2.7 %copy-start.17 = (f32[256]{0:T(256)S(1)}, f32[256]{0:T(256)}, u32[]{:S(2)}) copy-start(f32[256]{0:T(256)} %param.23) | copy-start | bytes 3076
  101.6 1.6 %collective-permute-start.20 = (bf16[512,256]{1,0:T(8,128)(2,1)S(1)}, bf16[512,256]{1,0:T(8,128)(2,1)S(1)}, u32[]{:S(2)}, u32[]{:S(2)}) collective-permute-start(bf16[512,256]{1,0:T(8,128)(2,1)S(1)} %fusion.33), channel_id=1, source_target_pairs={{0,1},{1,0},{2,3},{3,2},{4,5},{5,4},{6,7},{7,6},{8,9},{9,8},{10,11... | collective-permute-start | bytes 786440 | tf_op jit(solution)/shard_map/ppermute | solution.py:22
  101.7 2.4 %copy-start.4 = (bf16[512,256]{1,0:T(8,128)(2,1)}, bf16[512,256]{1,0:T(8,128)(2,1)S(1)}, u32[]{:S(2)}) copy-start(bf16[512,256]{1,0:T(8,128)(2,1)S(1)} %slice.182) | copy-start | bytes 786436

commit v2 on v0

v2 whole, which is shorter than its diff:
```python
import functools

import jax
import jax.numpy as jnp
from jax import lax
from jax.experimental import pallas as pl
from jax.experimental.pallas import tpu as pltpu
from jax.sharding import PartitionSpec as P

BF16, F32, I32 = jnp.bfloat16, jnp.float32, jnp.int32
LANES = 128
STEP = 256
SMEM = pl.BlockSpec(memory_space=pltpu.SMEM)
VMEM = pl.BlockSpec(memory_space=pltpu.VMEM)
HBM = pl.BlockSpec(memory_space=pltpu.HBM)


def dot(a, b):
    return jnp.dot(a, b, preferred_element_type=F32)


def iota(shape, axis):
    return lax.broadcasted_iota(I32, shape, axis)


def silu_bf16(v):
    return (v / (1.0 + jnp.exp(-v))).astype(BF16)


def shape_of(shape, dtype):
    return jax.ShapeDtypeStruct(shape, dtype)


def position(axis):
    return lax.axis_index(axis).astype(I32).reshape(1)


def swap(x):
    return lax.ppermute(x, "feat", [(0, 1), (1, 0)])


def from_xor(x, bits, n_dom):
    return lax.ppermute(x, "dom", [(i, i ^ bits) for i in range(n_dom)])


def call(kernel, out_shape, *args, specs=None, outs=None, name, scratch=(), mib=32):
    return pl.pallas_call(
        kernel,
        out_shape=out_shape,
        in_specs=[VMEM] * len(args) if specs is None else specs,
        out_specs=jax.tree.map(lambda _: VMEM, out_shape) if outs is None else outs,
        scratch_shapes=scratch,
        compiler_params=pltpu.CompilerParams(vmem_limit_bytes=mib << 20),
        name=name,
    )(*args)


def halves_of(feat, size):
    own = pl.ds(pl.multiple_of(feat * size, size), size)
    other = pl.ds(pl.multiple_of((1 - feat) * size, size), size)
    return own, other


def fetch_lists(send_list, recv_list, n_dom):
    near, far = (1, 3), (2, 4)
    fetched = []
    for step in range(2):
        what = jnp.where(lax.axis_index("feat") == 1, send_list, recv_list) if step else recv_list
        pairs = [(2 * d, 2 * (d ^ near[step])) for d in range(n_dom)]
        pairs += [(2 * d + 1, 2 * (d ^ far[step]) + 1) for d in range(n_dom)]
        fetched.append(lax.ppermute(what, ("dom", "feat"), pairs))
    return jnp.concatenate(fetched, axis=1)


def start_copies(source, target, sems, first, pieces):
    rows = source.shape[0] // pieces
    copies = []
    for n in range(pieces):
        part = pl.ds(n * rows, rows)
        copies.append(pltpu.make_async_copy(source.at[part], target.at[part], sems.at[first + n]))
        copies[-1].start()
    return copies


def wait_copies(copies):
    for copy in copies:
        copy.wait()


def own_features_kernel(feat, grid, mesh, w_send, w_recv, grid_part, mesh_part, send_rest, recv_rest, *scratch):
    ws, g, wr, m, sems = scratch
    first = start_copies(w_send, ws, sems, 0, 4) + start_copies(grid, g, sems, 4, 4)
    second = start_copies(w_recv, wr, sems, 8, 4) + start_copies(mesh, m, sems, 12, 4)
    own, other = halves_of(feat[0], g.shape[1])
    wait_copies(first)
    grid_part[...] = dot(g[...], ws[own, :])
    send_rest[...] = ws[other, :]
    wait_copies(second)
    mesh_part[...] = dot(m[...], wr[own, :])
    recv_rest[...] = wr[other, :]


def other_features_kernel(part, rest, other, *outs):
    width = outs[0].shape[1]
    for c, out in enumerate(outs):
        lanes = slice(c * width, (c + 1) * width)
        out[...] = (part[:, lanes] + dot(other[...], rest[:, lanes])).astype(BF16)


def project(grid, mesh, w_send, w_recv, n_chunks):
    grid_other, mesh_other = swap(grid), swap(mesh)
    hidden, feats = w_send.shape[1], grid.shape[1]
    parts = call(
        own_features_kernel,
        [
            shape_of((grid.shape[0], hidden), F32),
            shape_of((mesh.shape[0], hidden), F32),
            shape_of((feats, hidden), BF16),
            shape_of((feats, hidden), BF16),
        ],
        position("feat"),
        *[pltpu.with_memory_space_constraint(x, pltpu.HBM) for x in (grid, mesh, w_send, w_recv)],
        specs=[SMEM] + [HBM] * 4,
        scratch=[pltpu.VMEM(x.shape, BF16) for x in (w_send, grid, w_recv, mesh)] + [pltpu.SemaphoreType.DMA((16,))],
        name="own_features",
        mib=16,
    )
    grid_part, mesh_part, send_rest, recv_rest = parts
    chunk = shape_of((grid.shape[0], hidden // n_chunks), BF16)
    chunks = call(
        other_features_kernel, [chunk] * n_chunks, grid_part, send_rest, grid_other, name="other_grid_features"
    )
    chunks, mesh_part = lax.optimization_barrier((chunks, mesh_part))
    (mesh_proj,) = call(
        other_features_kernel,
        [shape_of((mesh.shape[0], hidden), BF16)],
        mesh_part,
        recv_rest,
        mesh_other,
        name="other_mesh_features",
    )
    return chunks, mesh_proj, mesh_other


def across(row):
    return jnp.transpose(jnp.broadcast_to(row.astype(F32), (LANES, LANES))).astype(I32)


def goals_kernel(half, mesh_rows, me, feat, send_own, recv_own, mine, other, *outs):
    size = send_own.shape[1]
    cap = size // (2 * half)
    blocks = outs[0].shape[0] // LANES
    digit = 64

    def pick(from_second, step, block):
        at = pl.ds(pl.multiple_of(step * size + block * cap, cap), cap)
        return jnp.where(feat[0] == from_second, mine[:, at], other[:, at])

    def block(ref, n):
        return ref[:, pl.ds(pl.multiple_of(n * cap, cap), cap)]

    for sender, column, row in ((me[0], outs[0], outs[1]), (me[0] ^ half, outs[2], outs[3])):
        rows = (block(recv_own, sender), pick(0, 0, sender), pick(1, 0, sender), pick(0, 1, sender))
        ids = [block(send_own, me[0] ^ k) if column is outs[0] else pick(1, 1, me[0] ^ k) for k in range(half)]
        values = [jnp.where(r < mesh_rows, r + (k * mesh_rows + 1), 0) for k, r in enumerate(rows)]
        ids, values = jnp.concatenate(ids, axis=1), jnp.concatenate(values, axis=1)
        into_block = iota((blocks, ids.shape[1]), 0) == ids // LANES
        into_lane = (iota((LANES, ids.shape[1]), 0) == ids % LANES).astype(BF16)
        goal = jnp.full((blocks, LANES), -1.0, F32)
        for scale, part in ((digit, values // digit), (1, values % digit)):
            entries = jnp.where(into_block, part, 0).astype(F32).astype(BF16)
            goal += scale * lax.dot_general(entries, into_lane, (((1,), (1,)), ((), ())), preferred_element_type=F32)
        for b in range(blocks):
            part = slice(b * LANES, (b + 1) * LANES)
            found = goal[b : b + 1, :]
            column[part, :] = across(found)
            row[:, part] = jnp.broadcast_to(found, (row.shape[0], LANES)).astype(I32)


def add_terms(term, goal, tables, first):
    for k, table in enumerate(tables):
        hot = goal == iota((goal.shape[0], table.shape[0]), 1) + (first + k) * table.shape[0]
        term += dot(hot.astype(BF16), table[...])
    return term


def terms_kernel(first, n_tables, *refs):
    start_own, start_mirror, goal_own, goal_mirror, *tables = refs[: 4 + n_tables]
    for start, goal, out in zip((start_own, start_mirror), (goal_own, goal_mirror), refs[4 + n_tables :]):

        @pl.loop(0, out.shape[0] // STEP)
        def _(i):
            at = pl.ds(pl.multiple_of(i * STEP, STEP), STEP)
            begin = jnp.broadcast_to(start[...], (STEP, out.shape[1])) if start.shape[0] == 1 else start[at, :]
            out[at, :] = add_terms(begin, goal[at, :][:, :1], tables, first)


def own_sums_kernel(half, term_own, term_mirror, goal_own, goal_mirror, row_own, table, g0, g1, sums, mirror_out, hidden):
    grid_rows, width = g0.shape

    @pl.loop(0, grid_rows // STEP)
    def _(i):
        at = pl.ds(pl.multiple_of(i * STEP, STEP), STEP)
        mirror_out[at, :] = add_terms(term_mirror[at, :], goal_mirror[at, :][:, :1], (table,), half - 1)
        term = add_terms(term_own[at, :], goal_own[at, :][:, :1], (table,), half - 1)
        for c, g in enumerate((g0, g1)):
            part = slice(c * width, (c + 1) * width)
            hidden[at, part] = silu_bf16(g[at, :].astype(F32) + term[:, part])

    goal = row_own[:1, :]

    @pl.loop(0, sums.shape[0] // STEP)
    def _(i):
        hot = iota((STEP, grid_rows), 0) + i * STEP == goal
        sums[pl.ds(pl.multiple_of(i * STEP, STEP), STEP), :] = dot(hot.astype(BF16), hidden[...])


def far_sums_kernel(chunk, mirrored, term, row, sums, *outs):
    width = mirrored.shape[1]
    part = slice(chunk * width, (chunk + 1) * width)
    hidden = silu_bf16(mirrored[...].astype(F32) + term[:, part])
    goal = row[:1, :]
    for k, out in enumerate(outs):
        for at in range(0, out.shape[0], STEP):
            first = k * out.shape[0] + at
            hot = iota((STEP, goal.shape[1]), 0) + first == goal
            total = sums[first : first + STEP, part] + dot(hot.astype(BF16), hidden)
            out[at : at + STEP, :] = total.astype(out.dtype)


def sums_by_halves(grid_chunks, mesh_rproj, bias, send_grid, recv_row, fetched, n_dom):
    half = n_dom // 2
    mesh_rows, hidden = mesh_rproj.shape
    grid_rows, width = grid_chunks[0].shape
    tables = [mesh_rproj] + [from_xor(mesh_rproj, k, n_dom) for k in range(1, half)]
    mirrored = [from_xor(grid_chunks[0], half, n_dom)]
    fetched, later = lax.optimization_barrier((fetched, grid_chunks[1]))
    mirrored.append(from_xor(later, half, n_dom))
    column, row = shape_of((grid_rows, LANES), I32), shape_of((8, grid_rows), I32)
    goal_own, row_own, goal_mirror, row_mirror = call(
        functools.partial(goals_kernel, half, mesh_rows),
        [column, row, column, row],
        position("dom"),
        position("feat"),
        send_grid,
        recv_row,
        fetched,
        swap(fetched),
        specs=[SMEM] * 2 + [VMEM] * 4,
        name="goals",
    )
    term = shape_of((grid_rows, hidden), F32)
    terms = (bias[None, :], bias[None, :])
    for first, some in ((0, tables[:2]), (2, tables[2:3])):
        terms = call(
            functools.partial(terms_kernel, first, len(some)),
            [term, term],
            *terms,
            goal_own,
            goal_mirror,
            *some,
            name="mesh_terms",
        )
    sums, term_mirror = call(
        functools.partial(own_sums_kernel, half),
        [shape_of((half * mesh_rows, hidden), F32), term],
        *terms,
        goal_own,
        goal_mirror,
        row_own,
        tables[3],
        *grid_chunks,
        scratch=[pltpu.VMEM((grid_rows, hidden), BF16)],
        name="own_sums",
    )
    chunks = []
    for c in range(2):
        parts = call(
            functools.partial(far_sums_kernel, c),
            [shape_of((mesh_rows, width), BF16 if k else F32) for k in range(half)],
            mirrored[c],
            term_mirror,
            row_mirror,
            sums,
            name="far_sums",
        )
        result = parts[0]
        for k in range(1, half):
            result += from_xor(parts[k], k, n_dom).astype(F32)
        chunks.append(result.astype(BF16))
    return chunks


def sums_by_all_to_all(grid_chunks, mesh_rproj, bias, send_grid, recv_row, fetched, n_dom):
    def rows_of(table, index):
        hot = index[0][:, None] == iota((index.shape[1], table.shape[0]), 1)
        return dot(hot.astype(BF16), table)

    packed = rows_of(grid_chunks[0], send_grid).astype(BF16)
    arrived = lax.all_to_all(packed, "dom", split_axis=0, concat_axis=0, tiled=True)
    hidden = silu_bf16(arrived.astype(F32) + rows_of(mesh_rproj, recv_row) + bias[None, :])
    into = iota((mesh_rproj.shape[0], recv_row.shape[1]), 0) == recv_row
    return [dot(into.astype(BF16), hidden).astype(BF16)]


def encode_kernel(n_chunks, feat, *refs):
    chunks, others = refs[:n_chunks], refs[n_chunks : 2 * n_chunks]
    w_own, w_other, mesh_own, mesh_other, w_send, halo_rows = refs[2 * n_chunks : 2 * n_chunks + 6]
    full_out, send_out, halo_out, update, full, send_proj, halo, sem = refs[2 * n_chunks + 6 :]
    width, feats = chunks[0].shape[1], mesh_own.shape[1]
    total = 0.0
    for c, (mine, other) in enumerate(zip(chunks, others)):
        rows = slice(c * width, (c + 1) * width)
        total += dot(mine[...], w_own[rows, :]) + dot(other[...], w_other[rows, :])
    update[...] = total
    own, rest = halves_of(feat[0], feats)
    full[:, own] = (mesh_own[...].astype(F32) + update[:, own]).astype(BF16)
    full[:, rest] = (mesh_other[...].astype(F32) + update[:, rest]).astype(BF16)
    sent = start_copies(full, full_out, sem, 0, 2)
    send_proj[...] = dot(full[...], w_send[...]).astype(BF16)
    sent += start_copies(send_proj, send_out, sem, 2, 1)
    for at in range(0, halo.shape[0], LANES):
        rows = slice(at, at + LANES)
        hot = across(halo_rows[:, rows])[:, :1] == iota((LANES, send_proj.shape[0]), 1)
        halo[rows, :] = dot(hot.astype(BF16), send_proj[...]).astype(BF16)
        if rows.stop % STEP == 0:
            done = slice(rows.stop - STEP, rows.stop)
            sent.append(pltpu.make_async_copy(halo.at[done], halo_out.at[done], sem.at[len(sent)]))
            sent[-1].start()
    wait_copies(sent)


def near_edges_kernel(feat, full, send_proj, w_recv, bias, src, dst, w_own, w_other, near, src_at, dst_row, w_out, encoded):
    feats = encoded.shape[1]
    own, _ = halves_of(feat[0], feats)
    encoded[...] = full[:, own]
    recv_proj = dot(full[...], w_recv[...]).astype(BF16)
    for b in range(src.shape[0]):
        rows = slice(b * LANES, (b + 1) * LANES)
        src_at[rows, :] = across(src[b : b + 1, :])
        dst_row[:, rows] = dst[b : b + 1, :]
        dst_at = across(dst[b : b + 1, :])[:, :1]
        term = dot((src_at[rows, :1] == iota((LANES, send_proj.shape[0]), 1)).astype(BF16), send_proj[...])
        term += dot((dst_at == iota((LANES, send_proj.shape[0]), 1)).astype(BF16), recv_proj)
        near[rows, :] = term + bias[...]
    w_out[: w_own.shape[0], :] = w_own[:, own]
    w_out[w_own.shape[0] :, :] = w_other[:, own]


def edge_sums_kernel(halo_rows, near, src_at, dst_row, out, halo, sem):
    arrival = start_copies(halo_rows, halo, sem, 0, 8)
    mesh_rows = out.shape[0]
    total = jnp.zeros(out.shape, F32)
    wait_copies(arrival)
    for at in range(0, near.shape[0], STEP):
        rows = slice(at, at + STEP)
        hot = src_at[rows, :1] - mesh_rows == iota((STEP, halo.shape[0]), 1)
        hidden = silu_bf16(near[rows, :] + dot(hot.astype(BF16), halo[...]))
        into = iota((mesh_rows, STEP), 0) == dst_row[:, rows]
        total += dot(into.astype(BF16), hidden)
    out[...] = total.astype(BF16)


def output_kernel(encoded, mine, other, w_out, out):
    hidden = mine.shape[1]
    update = dot(mine[...], w_out[:hidden, :]) + dot(other[...], w_out[hidden:, :])
    out[...] = (encoded[...].astype(F32) + update).astype(BF16)


def shards(
    grid_lat,
    mesh_lat,
    w_grid_send,
    w_grid_recv,
    g2m_bias,
    w_grid_out,
    w_edge_send,
    w_edge_recv,
    edge_bias,
    w_edge_out,
    send_grid,
    recv_row,
    halo_rows,
    edge_src,
    edge_dst,
):
    n_dom = lax.axis_size("dom")
    mesh_rows, feats = mesh_lat.shape
    hidden = w_grid_send.shape[1]
    halves = n_dom == 8
    grid_chunks, mesh_rproj, mesh_other = project(grid_lat, mesh_lat, w_grid_send, w_grid_recv, 2 if halves else 1)
    grid_chunks, mesh_rproj, send_grid, recv_row, w_grid_out, w_edge_out = lax.optimization_barrier(
        (grid_chunks, mesh_rproj, send_grid, recv_row, w_grid_out, w_edge_out)
    )
    fetched = fetch_lists(send_grid, recv_row, n_dom) if halves else None
    sums = sums_by_halves if halves else sums_by_all_to_all
    chunks = sums(grid_chunks, mesh_rproj, g2m_bias, send_grid, recv_row, fetched, n_dom)

    feat = position("feat")
    full, send_proj, halo_out = call(
        functools.partial(encode_kernel, len(chunks)),
        [
            pltpu.HBM((mesh_rows, 2 * feats), BF16),
            pltpu.HBM((mesh_rows, hidden), BF16),
            pltpu.HBM((halo_rows.shape[1], hidden), BF16),
        ],
        feat,
        *chunks,
        *[swap(chunk) for chunk in chunks],
        w_grid_out,
        swap(w_grid_out),
        mesh_lat,
        mesh_other,
        w_edge_send,
        halo_rows,
        specs=[SMEM] + [VMEM] * (2 * len(chunks) + 6),
        scratch=[
            pltpu.VMEM((mesh_rows, 2 * feats), F32),
            pltpu.VMEM((mesh_rows, 2 * feats), BF16),
            pltpu.VMEM((mesh_rows, hidden), BF16),
            pltpu.VMEM((halo_rows.shape[1], hidden), BF16),
            pltpu.SemaphoreType.DMA((3 + halo_rows.shape[1] // STEP,)),
        ],
        outs=[HBM] * 3,
        name="encode",
    )
    halo_in = lax.all_to_all(halo_out, "dom", split_axis=0, concat_axis=0, tiled=True)
    edges = edge_src.shape[0] * edge_src.shape[1]
    near, src_at, dst_row, w_out, mesh_encoded = call(
        near_edges_kernel,
        [
            shape_of((edges, hidden), F32),
            shape_of((edges, LANES), I32),
            shape_of((1, edges), I32),
            shape_of((2 * w_edge_out.shape[0], feats), BF16),
            shape_of((mesh_rows, feats), BF16),
        ],
        feat,
        full,
        send_proj,
        w_edge_recv,
        edge_bias[None, :],
        edge_src,
        edge_dst,
        w_edge_out,
        swap(w_edge_out),
        specs=[SMEM] + [VMEM] * 8,
        name="near_edges",
    )
    proc_sum = call(
        edge_sums_kernel,
        shape_of((mesh_rows, hidden), BF16),
        pltpu.with_memory_space_constraint(halo_in, pltpu.HBM),
        near,
        src_at,
        dst_row,
        specs=[HBM] + [VMEM] * 3,
        scratch=[pltpu.VMEM(halo_in.shape, BF16), pltpu.SemaphoreType.DMA((8,))],
        name="edge_sums",
    )
    mesh_out = call(
        output_kernel,
        shape_of((mesh_rows, feats), BF16),
        mesh_encoded,
        proc_sum,
        swap(proc_sum),
        w_out,
        name="output",
    )
    return (mesh_encoded, mesh_out)


def solution(mesh):
    rows = P(("member", "dom"), "feat")
    columns, lists = P(None, "feat"), P("dom", None)
    placed = (rows, rows, columns, columns, P("feat"), P("feat", None), columns, columns, P("feat"), P("feat", None))
    return jax.shard_map(
        shards,
        mesh=mesh,
        in_specs=placed + (lists,) * 5,
        out_specs=(rows, rows),
        check_vma=False,
    )
```

time: 170 us -> 83.9 us (0.49)
  blocking collectives: 78.1 us -> 0 us
  matrix products: 33.4 us -> 0 us
  Pallas kernels: 0 us -> 25.1 us
  starting transfers between devices: 0.34 us -> 23 us
  between operations: 13.9 us -> 0.92 us
  waiting for transfers between devices: 37.5 us -> 30.7 us
  other arithmetic: 3.83 us -> 0.17 us
  local copies, waits for them, and re-layouts: 1.93 us -> 3.69 us
    all_to_all x2 -> x0, blocking collectives: 75.9 us -> none  [the longest x1 55.4 us: shards(): lax.all_to_all(packed, 'dom', split_axis=0, concat_axis=0, tiled=True)]
    dot_general x8 -> x0, matrix products: 33.4 us -> none  [the longest x5 20.3 us: pick_rows(): jnp.dot(selector, table, preferred_element_type=jnp.float32)]
    pallas_call x0 -> x13, Pallas kernels: none -> 25.1 us  [call(): pl.pallas_call(kernel, out_shape=out_shape, in_specs=[VMEM] * len(args) i...]
    ppermute x0 -> x21, waiting for transfers between devices: none -> 23.7 us  [the longest x11 18.2 us: from_xor(): return lax.ppermute(x, 'dom', [(i, i ^ bits) for i in range(n_dom)])]
    reduce_scatter x2 -> x0, waiting for transfers between devices: 19.8 us -> none  [the longest x1 9.91 us: shards(): lax.psum_scatter(proc_partial, 'feat', scatter_dimension=1, tiled=True)]
    ppermute x0 -> x21, starting transfers between devices: none -> 18.6 us  [the longest x11 13 us: from_xor(): return lax.ppermute(x, 'dom', [(i, i ^ bits) for i in range(n_dom)])]
    all_gather x2 -> x0, waiting for transfers between devices: 17.7 us -> none  [the longest x1 9.07 us: shards(): slot_full = lax.all_gather(arrived, 'feat', axis=1, tiled=True)]
    all_to_all x0 -> x1, waiting for transfers between devices: none -> 7.01 us  [shards(): lax.all_to_all(halo_out, 'dom', split_axis=0, concat_axis=0, tiled=True)]
  transfers between devices with their start and end apart: 4 -> 22, of which waited for: 4 -> 11; matrix products, arithmetic and copies ran while one was open for 0% -> 0% of each run, Pallas kernels for 0% -> 21%
where the time goes in v2:
time: 83.9 us; the launch traced here: 83.5 us
  waiting for transfers between devices  30.7 us (37%)
  Pallas kernels  25.1 us (30%)
  starting transfers between devices  23 us (27%)
  local copies, waits for them, and re-layouts  3.69 us (4%)
  between operations  0.92 us (1%)
    pallas_call x13, Pallas kernels, call(): pl.pallas_call(kernel, out_shape=out_shape, in_specs=[VMEM] * len(args) i...  25.1 us
    ppermute x11, waiting for transfers between devices, from_xor(): return lax.ppermute(x, 'dom', [(i, i ^ bits) for i in range(n_dom)])  18.2 us
    ppermute x11, starting transfers between devices, from_xor(): return lax.ppermute(x, 'dom', [(i, i ^ bits) for i in range(n_dom)])  13 us
    all_to_all x1, waiting for transfers between devices, shards(): lax.all_to_all(halo_out, 'dom', split_axis=0, concat_axis=0, tiled=True)  7.01 us
    ppermute x8, waiting for transfers between devices, swap(): return lax.ppermute(x, 'feat', [(0, 1), (1, 0)])  5.44 us
    ppermute x2, starting transfers between devices, fetch_lists(): fetched.append(lax.ppermute(what, ('dom', 'feat'), pairs))  4.54 us
    all_to_all x1, starting transfers between devices, shards(): lax.all_to_all(halo_out, 'dom', split_axis=0, concat_axis=0, tiled=True)  4.35 us
    unnamed x36, local copies, waits for them, and re-layouts  3.69 us
  transfers between devices with their start and end apart: 22, of which 11 were waited for; matrix products, arithmetic and copies ran while one was open for 0% of the time, Pallas kernels for 21%

profile of v2, /device:TPU:0, one launch (start us, length us, event | category | flops | bytes accessed | tf_op | source)
XLA Modules:
  0.0 83.5 jit_solution(2033697232687272390)
XLA Ops:
  0.6 0.5 collective-permute-start
  1.1 0.1 collective-permute-start.1
  1.2 2.0 %own_features.1 = (f32[1024,256]{1,0:T(8,128)S(1)}, f32[512,256]{1,0:T(8,128)S(1)}, bf16[256,256]{1,0:T(8,128)(2,1)S(1)}, bf16[256,256]{1,0:T(8,128)(2,1)S(1)}) custom-call(s32[1]{0:T(128)} %bitcast.feat, bf16[1024,256]{1,0:T(8,128)(2,1)} %grid.1, bf16[512,256]{1,0:T(8,128)(2,1)} %refs_6_.1, bf16[512,256]{1,0:T(8,128)(2,1)} %w_send.1, bf16[512,256]{1,0:T(8,128)(2,1)} %w_recv.2), custom_call_target="tpu_custom_call" | custom-call | tf_op jit(solution)/shard_map/own_features/pallas_call | solution.py:47
  3.3 0.4 other_grid_features.1
  3.7 0.2 other_mesh_features.1.refs_4_
  4.0 4.0 %collective-permute-start.4 = (s32[1,4096]{1,0:T(1,128)S(1)}, s32[1,4096]{1,0:T(1,128)S(1)}, u32[]{:S(2)}, u32[]{:S(2)}) collective-permute-start(s32[1,4096]{1,0:T(1,128)S(1)} %broadcast_select_fusion), channel_id=1, source_target_pairs={{0,6},{2,4},{4,2},{6,0},{8,14},{10,12},{12,10},{14,8},{1,9},{3,11}... | collective-permute-start | bytes 49160 | tf_op jit(solution)/shard_map/ppermute | solution.py:71
  8.0 0.5 collective-permute-start.3
  8.6 1.5 %collective-permute-start.6 = (bf16[512,256]{1,0:T(8,128)(2,1)S(1)}, bf16[512,256]{1,0:T(8,128)(2,1)S(1)}, u32[]{:S(2)}, u32[]{:S(2)}) collective-permute-start(bf16[512,256]{1,0:T(8,128)(2,1)S(1)} %other_mesh_features.1.refs_4_), channel_id=1, source_target_pairs={{0,2},{2,0},{4,6},{6,4},{8,10},{10,8},{12,14},{14,12},{1,3},{3,1},... | collective-permute-start | bytes 786440 | tf_op jit(solution)/shard_map/ppermute | solution.py:43
  10.0 0.5 collective-permute-start.7
  10.5 1.5 %collective-permute-start.8 = (bf16[512,256]{1,0:T(8,128)(2,1)S(1)}, bf16[512,256]{1,0:T(8,128)(2,1)S(1)}, u32[]{:S(2)}, u32[]{:S(2)}) collective-permute-start(bf16[512,256]{1,0:T(8,128)(2,1)S(1)} %other_mesh_features.1.refs_4_), channel_id=1, source_target_pairs={{0,6},{2,4},{4,2},{6,0},{8,14},{10,12},{12,10},{14,8},{1,7},{3,5},... | collective-permute-start | bytes 786440 | tf_op jit(solution)/shard_map/ppermute | solution.py:43
  12.1 2.6 %collective-permute-start.2 = (bf16[1024,128]{1,0:T(8,128)(2,1)S(1)}, bf16[1024,128]{1,0:T(8,128)(2,1)S(1)}, u32[]{:S(2)}, u32[]{:S(2)}) collective-permute-start(bf16[1024,128]{1,0:T(8,128)(2,1)S(1)} %get-tuple-element.55.g0), channel_id=1, source_target_pairs={{0,8},{2,10},{4,12},{6,14},{8,0},{10,2},{12,4},{14,6},{1,9},{3,11}... | collective-permute-start | bytes 786440 | tf_op jit(solution)/shard_map/ppermute | solution.py:43
  14.6 1.2 %collective-permute-done.5.other = s32[1,8192]{1,0:T(1,128)S(1)} collective-permute-done((s32[1,8192]{1,0:T(1,128)S(1)}, s32[1,8192]{1,0:T(1,128)S(1)}, u32[]{:S(2)}, u32[]{:S(2)}) %collective-permute-start.5) | collective-permute-done | bytes 32800 | tf_op jit(solution)/shard_map/ppermute | solution.py:39
  15.8 0.4 collective-permute-start.12
  16.2 0.9 %goals.1 = (s32[1024,128]{1,0:T(8,128)S(1)}, s32[8,1024]{1,0:T(8,128)S(1)}, s32[1024,128]{1,0:T(8,128)S(1)}, s32[8,1024]{1,0:T(8,128)S(1)}) custom-call(s32[1]{0:T(128)} %bitcast.2.me, s32[1]{0:T(128)} %bitcast.feat, s32[1,4096]{1,0:T(1,128)S(1)} %copy-done.11, s32[1,4096]{1,0:T(1,128)S(1)} %copy-done.12, s32[1,8192]{1,0:T(1,128)S(1)} %pad_add_fusion.mine, ...), custom_call_target="tpu_custom_call" | custom-call | tf_op jit(solution)/shard_map/goals/pallas_call | solution.py:47
  17.1 0.3 collective-permute-done.6.refs_5_
  17.4 3.0 %mesh_terms.2 = (f32[1024,256]{1,0:T(8,128)S(1)}, f32[1024,256]{1,0:T(8,128)S(1)}) custom-call(f32[1,256]{1,0:T(1,128)S(1)} %bitcast.6, f32[1,256]{1,0:T(1,128)S(1)} %bitcast.7, s32[1024,128]{1,0:T(8,128)S(1)} %get-tuple-element.60.refs_2_.goal_own, s32[1024,128]{1,0:T(8,128)S(1)} %get-tuple-element.61.refs_3_.goal_mirror, ...), custom_call_target="tpu_custom_call" | custom-call | tf_op jit(solution)/shard_map/mesh_terms/pallas_call | solution.py:47
  20.4 7.5 %collective-permute-done.7.refs_4_ = bf16[512,256]{1,0:T(8,128)(2,1)S(1)} collective-permute-done((bf16[512,256]{1,0:T(8,128)(2,1)S(1)}, bf16[512,256]{1,0:T(8,128)(2,1)S(1)}, u32[]{:S(2)}, u32[]{:S(2)}) %collective-permute-start.7) | collective-permute-done | bytes 262176 | tf_op jit(solution)/shard_map/ppermute | solution.py:43
  27.9 2.2 %mesh_terms.3 = (f32[1024,256]{1,0:T(8,128)S(1)}, f32[1024,256]{1,0:T(8,128)S(1)}) custom-call(f32[1024,256]{1,0:T(8,128)S(1)} %get-tuple-element.63.refs_0_, f32[1024,256]{1,0:T(8,128)S(1)} %get-tuple-element.64.refs_1_, s32[1024,128]{1,0:T(8,128)S(1)} %get-tuple-element.60.refs_2_.goal_own, s32[1024,128]{1,0:T(8,128)S(1)} %get-tuple-element.61.refs_3_.goal_mirror, ...), custom_call_target="tpu_custom_call" | custom-call | tf_op jit(solution)/shard_map/mesh_terms/pallas_call | solution.py:47
  30.1 1.9 %collective-permute-done.8.table = bf16[512,256]{1,0:T(8,128)(2,1)S(1)} collective-permute-done((bf16[512,256]{1,0:T(8,128)(2,1)S(1)}, bf16[512,256]{1,0:T(8,128)(2,1)S(1)}, u32[]{:S(2)}, u32[]{:S(2)}) %collective-permute-start.8) | collective-permute-done | bytes 262176 | tf_op jit(solution)/shard_map/ppermute | solution.py:43
  32.0 4.0 %own_sums.1 = (f32[2048,256]{1,0:T(8,128)S(1)}, f32[1024,256]{1,0:T(8,128)S(1)}) custom-call(f32[1024,256]{1,0:T(8,128)S(1)} %get-tuple-element.65.term_own, f32[1024,256]{1,0:T(8,128)S(1)} %get-tuple-element.66.term_mirror, s32[1024,128]{1,0:T(8,128)S(1)} %get-tuple-element.60.refs_2_.goal_own, s32[1024,128]{1,0:T(8,128)S(1)} %get-tuple-element.61.refs_3_.goal_mirror, ...), custom_call_target="tpu_custom_call" | custom-call | tf_op jit(solution)/shard_map/own_sums/pallas_call | solution.py:47
  36.0 1.4 %far_sums.2 = (f32[512,128]{1,0:T(8,128)S(1)}, bf16[512,128]{1,0:T(8,128)(2,1)S(1)}, bf16[512,128]{1,0:T(8,128)(2,1)S(1)}, bf16[512,128]{1,0:T(8,128)(2,1)S(1)}) custom-call(bf16[1024,128]{1,0:T(8,128)(2,1)S(1)} %collective-permute-done.2.mirrored, f32[1024,256]{1,0:T(8,128)S(1)} %get-tuple-element.68.term, s32[8,1024]{1,0:T(8,128)S(1)} %get-tuple-element.69.row, ...), custom_call_target="tpu_custom_call" | custom-call | tf_op jit(solution)/shard_map/far_sums/pallas_call | solution.py:47
  37.4 0.6 collective-permute-start.10
  38.0 3.4 %collective-permute-start.11 = (bf16[512,128]{1,0:T(8,128)(2,1)S(1)}, bf16[512,128]{1,0:T(8,128)(2,1)S(1)}, u32[]{:S(2)}, u32[]{:S(2)}) collective-permute-start(bf16[512,128]{1,0:T(8,128)(2,1)S(1)} %get-tuple-element.74), channel_id=1, source_target_pairs={{0,6},{2,4},{4,2},{6,0},{8,14},{10,12},{12,10},{14,8},{1,7},{3,5},... | collective-permute-start | bytes 393224 | tf_op jit(solution)/shard_map/ppermute | solution.py:43
  41.4 0.1 collective-permute-start.18
  41.5 1.4 %far_sums.3 = (f32[512,128]{1,0:T(8,128)S(1)}, bf16[512,128]{1,0:T(8,128)(2,1)S(1)}, bf16[512,128]{1,0:T(8,128)(2,1)S(1)}, bf16[512,128]{1,0:T(8,128)(2,1)S(1)}) custom-call(bf16[1024,128]{1,0:T(8,128)(2,1)S(1)} %collective-permute-done.12.mirrored, f32[1024,256]{1,0:T(8,128)S(1)} %get-tuple-element.68.term, s32[8,1024]{1,0:T(8,128)S(1)} %get-tuple-element.69.row, ...), custom_call_target="tpu_custom_call" | custom-call | tf_op jit(solution)/shard_map/far_sums/pallas_call | solution.py:47
  42.9 2.0 %collective-permute-start.13 = (bf16[512,128]{1,0:T(8,128)(2,1)S(1)}, bf16[512,128]{1,0:T(8,128)(2,1)S(1)}, u32[]{:S(2)}, u32[]{:S(2)}) collective-permute-start(bf16[512,128]{1,0:T(8,128)(2,1)S(1)} %get-tuple-element.77), channel_id=1, source_target_pairs={{0,2},{2,0},{4,6},{6,4},{8,10},{10,8},{12,14},{14,12},{1,3},{3,1},... | collective-permute-start | bytes 393224 | tf_op jit(solution)/shard_map/ppermute | solution.py:43
  44.9 0.1 collective-permute-start.14
  44.9 2.3 %collective-permute-done.11 = bf16[512,128]{1,0:T(8,128)(2,1)S(1)} collective-permute-done((bf16[512,128]{1,0:T(8,128)(2,1)S(1)}, bf16[512,128]{1,0:T(8,128)(2,1)S(1)}, u32[]{:S(2)}, u32[]{:S(2)}) %collective-permute-start.11) | collective-permute-done | bytes 131104 | tf_op jit(solution)/shard_map/ppermute | solution.py:43
  47.2 0.5 collective-permute-start.15
  47.7 2.8 %collective-permute-done.9 = bf16[512,128]{1,0:T(8,128)(2,1)S(1)} collective-permute-done((bf16[512,128]{1,0:T(8,128)(2,1)S(1)}, bf16[512,128]{1,0:T(8,128)(2,1)S(1)}, u32[]{:S(2)}, u32[]{:S(2)}) %collective-permute-start.9) | collective-permute-done | bytes 131104 | tf_op jit(solution)/shard_map/ppermute | solution.py:43
  50.5 0.1 add_convert_fusion.1.refs_0_
  50.6 0.1 collective-permute-start.16
  50.7 3.5 %collective-permute-done.13 = bf16[512,128]{1,0:T(8,128)(2,1)S(1)} collective-permute-done((bf16[512,128]{1,0:T(8,128)(2,1)S(1)}, bf16[512,128]{1,0:T(8,128)(2,1)S(1)}, u32[]{:S(2)}, u32[]{:S(2)}) %collective-permute-start.13) | collective-permute-done | bytes 131104 | tf_op jit(solution)/shard_map/ppermute | solution.py:43
  54.2 0.1 collective-permute-start.17
  54.3 1.3 %collective-permute-done.17.refs_3_ = bf16[512,128]{1,0:T(8,128)(2,1)S(1)} collective-permute-done((bf16[512,128]{1,0:T(8,128)(2,1)S(1)}, bf16[512,128]{1,0:T(8,128)(2,1)S(1)}, u32[]{:S(2)}, u32[]{:S(2)}) %collective-permute-start.17) | collective-permute-done | bytes 131104 | tf_op jit(solution)/shard_map/ppermute | solution.py:39
  55.7 2.5 %encode.1 = (bf16[512,512]{1,0:T(8,128)(2,1)}, bf16[512,256]{1,0:T(8,128)(2,1)}, bf16[1024,256]{1,0:T(8,128)(2,1)}) custom-call(s32[1]{0:T(128)} %bitcast.feat, bf16[512,128]{1,0:T(8,128)(2,1)S(1)} %add_convert_fusion.1.refs_0_, bf16[512,128]{1,0:T(8,128)(2,1)S(1)} %add_convert_fusion.refs_1_, bf16[512,128]{1,0:T(8,128)(2,1)S(1)} %collective-permute-done.16.refs_2_, ...), custom_call_target="tpu_custom_call" | custom-call | tf_op jit(solution)/shard_map/encode/pallas_call | solution.py:47
  58.1 4.3 %all-to-all-start = ((bf16[8,128,256]{2,1,0:T(8,128)(2,1)}), bf16[8,128,256]{2,1,0:T(8,128)(2,1)}, u32[]{:S(2)}, u32[]{:S(2)}) async-start(bf16[8,128,256]{2,1,0:T(8,128)(2,1)} %bitcast.9), calls=%async_computation | async-start | bytes 1048576 | tf_op jit(solution)/shard_map/all_to_all | solution.py:427
  62.5 0.2 collective-permute-start.19
  62.7 1.4 %collective-permute-done.19.w_other = bf16[256,512]{1,0:T(8,128)(2,1)S(1)} collective-permute-done((bf16[256,512]{1,0:T(8,128)(2,1)S(1)}, bf16[256,512]{1,0:T(8,128)(2,1)S(1)}, u32[]{:S(2)}, u32[]{:S(2)}) %collective-permute-start.19) | collective-permute-done | bytes 262176 | tf_op jit(solution)/shard_map/ppermute | solution.py:39
  64.1 1.0 %copy-done.1 = bf16[512,512]{1,0:T(8,128)(2,1)S(1)} copy-done((bf16[512,512]{1,0:T(8,128)(2,1)S(1)}, bf16[512,512]{1,0:T(8,128)(2,1)}, u32[]{:S(2)}) %copy-start.1) | copy-done | bytes 524312
  65.2 0.9 %copy-done.4 = bf16[256,512]{1,0:T(8,128)(2,1)S(1)} copy-done((bf16[256,512]{1,0:T(8,128)(2,1)S(1)}, bf16[256,512]{1,0:T(8,128)(2,1)}, u32[]{:S(2)}) %copy-start.4) | copy-done | bytes 262168
  66.1 0.9 %copy-done.6 = bf16[512,256]{1,0:T(8,128)(2,1)S(1)} copy-done((bf16[512,256]{1,0:T(8,128)(2,1)S(1)}, bf16[512,256]{1,0:T(8,128)(2,1)}, u32[]{:S(2)}) %copy-start.6) | copy-done | bytes 262168
  67.1 2.6 %near_edges.1 = (f32[2048,256]{1,0:T(8,128)S(1)}, s32[2048,128]{1,0:T(8,128)S(1)}, s32[1,2048]{1,0:T(1,128)S(1)}, bf16[512,256]{1,0:T(8,128)(2,1)S(1)}, bf16[512,256]{1,0:T(8,128)(2,1)}) custom-call(s32[1]{0:T(128)} %bitcast.feat, bf16[512,512]{1,0:T(8,128)(2,1)S(1)} %copy-done.1, bf16[512,256]{1,0:T(8,128)(2,1)S(1)} %copy-done.6, ...), custom_call_target="tpu_custom_call" | custom-call | tf_op jit(solution)/shard_map/near_edges/pallas_call | solution.py:47
  69.7 0.7 copy-done.7
  70.4 7.0 %all-to-all-done = bf16[8,128,256]{2,1,0:T(8,128)(2,1)} async-done(((bf16[8,128,256]{2,1,0:T(8,128)(2,1)}), bf16[8,128,256]{2,1,0:T(8,128)(2,1)}, u32[]{:S(2)}, u32[]{:S(2)}) %all-to-all-start) | async-done | bytes 524320 | tf_op jit(solution)/shard_map/all_to_all | solution.py:427
  77.4 3.5 %edge_sums.1.mine = bf16[512,256]{1,0:T(8,128)(2,1)S(1)} custom-call(bf16[1024,256]{1,0:T(8,128)(2,1)} %bitcast.5.halo_rows, f32[2048,256]{1,0:T(8,128)S(1)} %get-tuple-element.86.near, s32[2048,128]{1,0:T(8,128)S(1)} %get-tuple-element.87.src_at, s32[1,2048]{1,0:T(1,128)S(1)} %get-tuple-element.88.dst_row), custom_call_target="tpu_custom_call" | custom-call | tf_op jit(solution)/shard_map/edge_sums/pallas_call | solution.py:47
  81.0 1.5 %collective-permute-done.20.other = bf16[512,256]{1,0:T(8,128)(2,1)S(1)} collective-permute-done((bf16[512,256]{1,0:T(8,128)(2,1)S(1)}, bf16[512,256]{1,0:T(8,128)(2,1)S(1)}, u32[]{:S(2)}, u32[]{:S(2)}) %collective-permute-start.20) | collective-permute-done | bytes 262176 | tf_op jit(solution)/shard_map/ppermute | solution.py:39
  82.5 1.0 %output.1 = bf16[512,256]{1,0:T(8,128)(2,1)} custom-call(bf16[512,256]{1,0:T(8,128)(2,1)S(1)} %copy-done.5, bf16[512,256]{1,0:T(8,128)(2,1)S(1)} %edge_sums.1.mine, bf16[512,256]{1,0:T(8,128)(2,1)S(1)} %collective-permute-done.20.other, bf16[512,256]{1,0:T(8,128)(2,1)S(1)} %copy-done.8), custom_call_target="tpu_custom_call" | custom-call | tf_op jit(solution)/shard_map/output/pallas_call | solution.py:47
  (49 shorter events, 0.3 us)
Async XLA Ops:
  0.6 2.6 %collective-permute-start = (bf16[1024,256]{1,0:T(8,128)(2,1)}, bf16[1024,256]{1,0:T(8,128)(2,1)S(1)}, u32[]{:S(2)}, u32[]{:S(2)}) collective-permute-start(bf16[1024,256]{1,0:T(8,128)(2,1)} %grid.1), channel_id=1, source_target_pairs={{0,1},{1,0},{2,3},{3,2},{4,5},{5,4},{6,7},{7,6},{8,9},{9,8},{10,11... | collective-permute-start | bytes 1572872 | tf_op jit(solution)/shard_map/ppermute | solution.py:39
  1.1 2.6 %collective-permute-start.1 = (bf16[512,256]{1,0:T(8,128)(2,1)}, bf16[512,256]{1,0:T(8,128)(2,1)S(1)}, u32[]{:S(2)}, u32[]{:S(2)}) collective-permute-start(bf16[512,256]{1,0:T(8,128)(2,1)} %refs_6_.1), channel_id=1, source_target_pairs={{0,1},{1,0},{2,3},{3,2},{4,5},{5,4},{6,7},{7,6},{8,9},{9,8},{10,11... | collective-permute-start | bytes 786440 | tf_op jit(solution)/shard_map/ppermute | solution.py:39
  1.2 2.7 %copy-start.11 = (s32[1,4096]{1,0:T(1,128)S(1)}, s32[1,4096]{1,0:T(1,128)}, u32[]{:S(2)}) copy-start(s32[1,4096]{1,0:T(1,128)} %send_own) | copy-start | bytes 49156
  1.2 2.7 %copy-start.12 = (s32[1,4096]{1,0:T(1,128)S(1)}, s32[1,4096]{1,0:T(1,128)}, u32[]{:S(2)}) copy-start(s32[1,4096]{1,0:T(1,128)} %recv_own) | copy-start | bytes 49156
  1.2 16.2 %copy-start.16 = (f32[256]{0:T(256)S(1)}, f32[256]{0:T(256)}, u32[]{:S(2)}) copy-start(f32[256]{0:T(256)} %param.19) | copy-start | bytes 3076
  4.0 8.0 %collective-permute-start.4 = (s32[1,4096]{1,0:T(1,128)S(1)}, s32[1,4096]{1,0:T(1,128)S(1)}, u32[]{:S(2)}, u32[]{:S(2)}) collective-permute-start(s32[1,4096]{1,0:T(1,128)S(1)} %broadcast_select_fusion), channel_id=1, source_target_pairs={{0,6},{2,4},{4,2},{6,0},{8,14},{10,12},{12,10},{14,8},{1,9},{3,11}... | collective-permute-start | bytes 49160 | tf_op jit(solution)/shard_map/ppermute | solution.py:71
  8.0 6.6 %collective-permute-start.3 = (s32[1,4096]{1,0:T(1,128)S(1)}, s32[1,4096]{1,0:T(1,128)S(1)}, u32[]{:S(2)}, u32[]{:S(2)}) collective-permute-start(s32[1,4096]{1,0:T(1,128)S(1)} %copy-done.12), channel_id=1, source_target_pairs={{0,2},{2,0},{4,6},{6,4},{8,10},{10,8},{12,14},{14,12},{1,5},{3,7},... | collective-permute-start | bytes 49160 | tf_op jit(solution)/shard_map/ppermute | solution.py:71
  8.6 8.8 %collective-permute-start.6 = (bf16[512,256]{1,0:T(8,128)(2,1)S(1)}, bf16[512,256]{1,0:T(8,128)(2,1)S(1)}, u32[]{:S(2)}, u32[]{:S(2)}) collective-permute-start(bf16[512,256]{1,0:T(8,128)(2,1)S(1)} %other_mesh_features.1.refs_4_), channel_id=1, source_target_pairs={{0,2},{2,0},{4,6},{6,4},{8,10},{10,8},{12,14},{14,12},{1,3},{3,1},... | collective-permute-start | bytes 786440 | tf_op jit(solution)/shard_map/ppermute | solution.py:43
  10.0 17.9 %collective-permute-start.7 = (bf16[512,256]{1,0:T(8,128)(2,1)S(1)}, bf16[512,256]{1,0:T(8,128)(2,1)S(1)}, u32[]{:S(2)}, u32[]{:S(2)}) collective-permute-start(bf16[512,256]{1,0:T(8,128)(2,1)S(1)} %other_mesh_features.1.refs_4_), channel_id=1, source_target_pairs={{0,4},{2,6},{4,0},{6,2},{8,12},{10,14},{12,8},{14,10},{1,5},{3,7},... | collective-permute-start | bytes 786440 | tf_op jit(solution)/shard_map/ppermute | solution.py:43
  10.5 21.5 %collective-permute-start.8 = (bf16[512,256]{1,0:T(8,128)(2,1)S(1)}, bf16[512,256]{1,0:T(8,128)(2,1)S(1)}, u32[]{:S(2)}, u32[]{:S(2)}) collective-permute-start(bf16[512,256]{1,0:T(8,128)(2,1)S(1)} %other_mesh_features.1.refs_4_), channel_id=1, source_target_pairs={{0,6},{2,4},{4,2},{6,0},{8,14},{10,12},{12,10},{14,8},{1,7},{3,5},... | collective-permute-start | bytes 786440 | tf_op jit(solution)/shard_map/ppermute | solution.py:43
  12.1 24.0 %collective-permute-start.2 = (bf16[1024,128]{1,0:T(8,128)(2,1)S(1)}, bf16[1024,128]{1,0:T(8,128)(2,1)S(1)}, u32[]{:S(2)}, u32[]{:S(2)}) collective-permute-start(bf16[1024,128]{1,0:T(8,128)(2,1)S(1)} %get-tuple-element.55.g0), channel_id=1, source_target_pairs={{0,8},{2,10},{4,12},{6,14},{8,0},{10,2},{12,4},{14,6},{1,9},{3,11}... | collective-permute-start | bytes 786440 | tf_op jit(solution)/shard_map/ppermute | solution.py:43
  14.6 1.2 %collective-permute-start.5 = (s32[1,8192]{1,0:T(1,128)S(1)}, s32[1,8192]{1,0:T(1,128)S(1)}, u32[]{:S(2)}, u32[]{:S(2)}) collective-permute-start(s32[1,8192]{1,0:T(1,128)S(1)} %pad_add_fusion.mine), channel_id=1, source_target_pairs={{0,1},{1,0},{2,3},{3,2},{4,5},{5,4},{6,7},{7,6},{8,9},{9,8},{10,11... | collective-permute-start | bytes 98312 | tf_op jit(solution)/shard_map/ppermute | solution.py:39
  15.8 25.6 %collective-permute-start.12 = (bf16[1024,128]{1,0:T(8,128)(2,1)S(1)}, bf16[1024,128]{1,0:T(8,128)(2,1)S(1)}, u32[]{:S(2)}, u32[]{:S(2)}) collective-permute-start(bf16[1024,128]{1,0:T(8,128)(2,1)S(1)} %get-tuple-element.75.g1), channel_id=1, source_target_pairs={{0,8},{2,10},{4,12},{6,14},{8,0},{10,2},{12,4},{14,6},{1,9},{3,11}... | collective-permute-start | bytes 786440 | tf_op jit(solution)/shard_map/ppermute | solution.py:43
  36.0 5.4 %copy-start.9 = (bf16[256,512]{1,0:T(8,128)(2,1)S(1)}, bf16[256,512]{1,0:T(8,128)(2,1)}, u32[]{:S(2)}) copy-start(bf16[256,512]{1,0:T(8,128)(2,1)} %refs_4_) | copy-start | bytes 786436
  37.4 7.5 %collective-permute-start.10 = (bf16[512,128]{1,0:T(8,128)(2,1)S(1)}, bf16[512,128]{1,0:T(8,128)(2,1)S(1)}, u32[]{:S(2)}, u32[]{:S(2)}) collective-permute-start(bf16[512,128]{1,0:T(8,128)(2,1)S(1)} %get-tuple-element.73), channel_id=1, source_target_pairs={{0,4},{2,6},{4,0},{6,2},{8,12},{10,14},{12,8},{14,10},{1,5},{3,7},... | collective-permute-start | bytes 393224 | tf_op jit(solution)/shard_map/ppermute | solution.py:43
  38.0 9.2 %collective-permute-start.11 = (bf16[512,128]{1,0:T(8,128)(2,1)S(1)}, bf16[512,128]{1,0:T(8,128)(2,1)S(1)}, u32[]{:S(2)}, u32[]{:S(2)}) collective-permute-start(bf16[512,128]{1,0:T(8,128)(2,1)S(1)} %get-tuple-element.74), channel_id=1, source_target_pairs={{0,6},{2,4},{4,2},{6,0},{8,14},{10,12},{12,10},{14,8},{1,7},{3,5},... | collective-permute-start | bytes 393224 | tf_op jit(solution)/shard_map/ppermute | solution.py:43
  41.4 14.3 %copy-start = (bf16[512,256]{1,0:T(8,128)(2,1)S(1)}, bf16[512,256]{1,0:T(8,128)(2,1)}, u32[]{:S(2)}) copy-start(bf16[512,256]{1,0:T(8,128)(2,1)} %refs_6_.1) | copy-start | bytes 786436
  41.4 14.3 %copy-start.10 = (bf16[512,256]{1,0:T(8,128)(2,1)S(1)}, bf16[512,256]{1,0:T(8,128)(2,1)}, u32[]{:S(2)}) copy-start(bf16[512,256]{1,0:T(8,128)(2,1)} %refs_8_.1) | copy-start | bytes 786436
  41.4 14.3 %copy-start.15 = (s32[1,1024]{1,0:T(1,128)S(1)}, s32[1,1024]{1,0:T(1,128)}, u32[]{:S(2)}) copy-start(s32[1,1024]{1,0:T(1,128)} %refs_9_.1) | copy-start | bytes 12292
  41.4 9.1 %collective-permute-start.9 = (bf16[512,128]{1,0:T(8,128)(2,1)S(1)}, bf16[512,128]{1,0:T(8,128)(2,1)S(1)}, u32[]{:S(2)}, u32[]{:S(2)}) collective-permute-start(bf16[512,128]{1,0:T(8,128)(2,1)S(1)} %get-tuple-element.72), channel_id=1, source_target_pairs={{0,2},{2,0},{4,6},{6,4},{8,10},{10,8},{12,14},{14,12},{1,3},{3,1},... | collective-permute-start | bytes 393224 | tf_op jit(solution)/shard_map/ppermute | solution.py:43
  41.4 12.9 %collective-permute-start.18 = (bf16[256,512]{1,0:T(8,128)(2,1)S(1)}, bf16[256,512]{1,0:T(8,128)(2,1)S(1)}, u32[]{:S(2)}, u32[]{:S(2)}) collective-permute-start(bf16[256,512]{1,0:T(8,128)(2,1)S(1)} %copy-done.9), channel_id=1, source_target_pairs={{0,1},{1,0},{2,3},{3,2},{4,5},{5,4},{6,7},{7,6},{8,9},{9,8},{10,11... | collective-permute-start | bytes 786440 | tf_op jit(solution)/shard_map/ppermute | solution.py:39
  42.9 11.3 %collective-permute-start.13 = (bf16[512,128]{1,0:T(8,128)(2,1)S(1)}, bf16[512,128]{1,0:T(8,128)(2,1)S(1)}, u32[]{:S(2)}, u32[]{:S(2)}) collective-permute-start(bf16[512,128]{1,0:T(8,128)(2,1)S(1)} %get-tuple-element.77), channel_id=1, source_target_pairs={{0,2},{2,0},{4,6},{6,4},{8,10},{10,8},{12,14},{14,12},{1,3},{3,1},... | collective-permute-start | bytes 393224 | tf_op jit(solution)/shard_map/ppermute | solution.py:43
  44.9 9.3 %collective-permute-start.14 = (bf16[512,128]{1,0:T(8,128)(2,1)S(1)}, bf16[512,128]{1,0:T(8,128)(2,1)S(1)}, u32[]{:S(2)}, u32[]{:S(2)}) collective-permute-start(bf16[512,128]{1,0:T(8,128)(2,1)S(1)} %get-tuple-element.78), channel_id=1, source_target_pairs={{0,4},{2,6},{4,0},{6,2},{8,12},{10,14},{12,8},{14,10},{1,5},{3,7},... | collective-permute-start | bytes 393224 | tf_op jit(solution)/shard_map/ppermute | solution.py:43
  47.2 6.9 %collective-permute-start.15 = (bf16[512,128]{1,0:T(8,128)(2,1)S(1)}, bf16[512,128]{1,0:T(8,128)(2,1)S(1)}, u32[]{:S(2)}, u32[]{:S(2)}) collective-permute-start(bf16[512,128]{1,0:T(8,128)(2,1)S(1)} %get-tuple-element.79), channel_id=1, source_target_pairs={{0,6},{2,4},{4,2},{6,0},{8,14},{10,12},{12,10},{14,8},{1,7},{3,5},... | collective-permute-start | bytes 393224 | tf_op jit(solution)/shard_map/ppermute | solution.py:43
  50.5 12.0 %copy-start.3 = (bf16[256,512]{1,0:T(8,128)(2,1)S(1)}, bf16[256,512]{1,0:T(8,128)(2,1)}, u32[]{:S(2)}) copy-start(bf16[256,512]{1,0:T(8,128)(2,1)} %w_own) | copy-start | bytes 786436
  50.5 13.6 %copy-start.2 = (bf16[512,256]{1,0:T(8,128)(2,1)S(1)}, bf16[512,256]{1,0:T(8,128)(2,1)}, u32[]{:S(2)}) copy-start(bf16[512,256]{1,0:T(8,128)(2,1)} %w_recv.3) | copy-start | bytes 786436
  50.5 13.6 %copy-start.13 = (s32[16,128]{1,0:T(8,128)S(1)}, s32[16,128]{1,0:T(8,128)}, u32[]{:S(2)}) copy-start(s32[16,128]{1,0:T(8,128)} %src.1) | copy-start | bytes 24580
  50.5 13.6 %copy-start.14 = (s32[16,128]{1,0:T(8,128)S(1)}, s32[16,128]{1,0:T(8,128)}, u32[]{:S(2)}) copy-start(s32[16,128]{1,0:T(8,128)} %dst.1) | copy-start | bytes 24580
  50.5 13.6 %copy-start.17 = (f32[256]{0:T(256)S(1)}, f32[256]{0:T(256)}, u32[]{:S(2)}) copy-start(f32[256]{0:T(256)} %param.23) | copy-start | bytes 3076
  50.6 3.7 %collective-permute-start.16 = (bf16[512,128]{1,0:T(8,128)(2,1)S(1)}, bf16[512,128]{1,0:T(8,128)(2,1)S(1)}, u32[]{:S(2)}, u32[]{:S(2)}) collective-permute-start(bf16[512,128]{1,0:T(8,128)(2,1)S(1)} %add_convert_fusion.1.refs_0_), channel_id=1, source_target_pairs={{0,1},{1,0},{2,3},{3,2},{4,5},{5,4},{6,7},{7,6},{8,9},{9,8},{10,11... | collective-permute-start | bytes 393224 | tf_op jit(solution)/shard_map/ppermute | solution.py:39
  54.2 1.4 %collective-permute-start.17 = (bf16[512,128]{1,0:T(8,128)(2,1)S(1)}, bf16[512,128]{1,0:T(8,128)(2,1)S(1)}, u32[]{:S(2)}, u32[]{:S(2)}) collective-permute-start(bf16[512,128]{1,0:T(8,128)(2,1)S(1)} %add_convert_fusion.refs_1_), channel_id=1, source_target_pairs={{0,1},{1,0},{2,3},{3,2},{4,5},{5,4},{6,7},{7,6},{8,9},{9,8},{10,11... | collective-permute-start | bytes 393224 | tf_op jit(solution)/shard_map/ppermute | solution.py:39
  58.1 19.2 %all-to-all-start = ((bf16[8,128,256]{2,1,0:T(8,128)(2,1)}), bf16[8,128,256]{2,1,0:T(8,128)(2,1)}, u32[]{:S(2)}, u32[]{:S(2)}) async-start(bf16[8,128,256]{2,1,0:T(8,128)(2,1)} %bitcast.9), calls=%async_computation | async-start | bytes 1048576 | tf_op jit(solution)/shard_map/all_to_all | solution.py:427
  62.5 1.6 %collective-permute-start.19 = (bf16[256,512]{1,0:T(8,128)(2,1)S(1)}, bf16[256,512]{1,0:T(8,128)(2,1)S(1)}, u32[]{:S(2)}, u32[]{:S(2)}) collective-permute-start(bf16[256,512]{1,0:T(8,128)(2,1)S(1)} %copy-done.3), channel_id=1, source_target_pairs={{0,1},{1,0},{2,3},{3,2},{4,5},{5,4},{6,7},{7,6},{8,9},{9,8},{10,11... | collective-permute-start | bytes 786440 | tf_op jit(solution)/shard_map/ppermute | solution.py:39
  64.1 1.0 %copy-start.1 = (bf16[512,512]{1,0:T(8,128)(2,1)S(1)}, bf16[512,512]{1,0:T(8,128)(2,1)}, u32[]{:S(2)}) copy-start(bf16[512,512]{1,0:T(8,128)(2,1)} %get-tuple-element.81.full) | copy-start | bytes 1572868
  65.2 0.9 %copy-start.4 = (bf16[256,512]{1,0:T(8,128)(2,1)S(1)}, bf16[256,512]{1,0:T(8,128)(2,1)}, u32[]{:S(2)}) copy-start(bf16[256,512]{1,0:T(8,128)(2,1)} %w_own) | copy-start | bytes 786436
  66.1 0.9 %copy-start.6 = (bf16[512,256]{1,0:T(8,128)(2,1)S(1)}, bf16[512,256]{1,0:T(8,128)(2,1)}, u32[]{:S(2)}) copy-start(bf16[512,256]{1,0:T(8,128)(2,1)} %get-tuple-element.82.send_proj) | copy-start | bytes 786436
  69.7 0.7 copy-start.7
  70.4 12.2 %copy-start.5 = (bf16[512,256]{1,0:T(8,128)(2,1)S(1)}, bf16[512,256]{1,0:T(8,128)(2,1)}, u32[]{:S(2)}) copy-start(bf16[512,256]{1,0:T(8,128)(2,1)} %get-tuple-element.44.encoded) | copy-start | bytes 786436
  77.4 5.2 %copy-start.8 = (bf16[512,256]{1,0:T(8,128)(2,1)S(1)}, bf16[512,256]{1,0:T(8,128)(2,1)}, u32[]{:S(2)}) copy-start(bf16[512,256]{1,0:T(8,128)(2,1)} %copy-done.7) | copy-start | bytes 786436
  80.9 1.6 %collective-permute-start.20 = (bf16[512,256]{1,0:T(8,128)(2,1)S(1)}, bf16[512,256]{1,0:T(8,128)(2,1)S(1)}, u32[]{:S(2)}, u32[]{:S(2)}) collective-permute-start(bf16[512,256]{1,0:T(8,128)(2,1)S(1)} %edge_sums.1.mine), channel_id=1, source_target_pairs={{0,1},{1,0},{2,3},{3,2},{4,5},{5,4},{6,7},{7,6},{8,9},{9,8},{10,11... | collective-permute-start | bytes 786440 | tf_op jit(solution)/shard_map/ppermute | solution.py:39

commit v3 on v0

v3 whole, which is shorter than its diff:
```python
import functools

import jax
import jax.numpy as jnp
from jax import lax
from jax.experimental import pallas as pl
from jax.experimental.pallas import tpu as pltpu
from jax.sharding import PartitionSpec as P

BF16, F32, I32 = jnp.bfloat16, jnp.float32, jnp.int32
LANES = 128
STEP = 256
MIB = 24
SMEM = pl.BlockSpec(memory_space=pltpu.SMEM)
VMEM = pl.BlockSpec(memory_space=pltpu.VMEM)
HBM = pl.BlockSpec(memory_space=pltpu.HBM)


def dot(a, b):
    return jnp.dot(a, b, preferred_element_type=F32)


def iota(shape, axis):
    return lax.broadcasted_iota(I32, shape, axis)


def silu_bf16(v):
    return (v / (1.0 + jnp.exp(-v))).astype(BF16)


def shape_of(shape, dtype):
    return jax.ShapeDtypeStruct(shape, dtype)


def position(axis):
    return lax.axis_index(axis).astype(I32).reshape(1)


def swap(x):
    return lax.ppermute(x, "feat", [(0, 1), (1, 0)])


def from_xor(x, bits, n_dom):
    return lax.ppermute(x, "dom", [(i, i ^ bits) for i in range(n_dom)])


def call(kernel, out_shape, *args, specs=None, outs=None, name, scratch=(), mib=MIB):
    return pl.pallas_call(
        kernel,
        out_shape=out_shape,
        in_specs=[VMEM] * len(args) if specs is None else specs,
        out_specs=jax.tree.map(lambda _: VMEM, out_shape) if outs is None else outs,
        scratch_shapes=scratch,
        compiler_params=pltpu.CompilerParams(vmem_limit_bytes=mib << 20),
        name=name,
    )(*args)


def halves_of(feat, size):
    own = pl.ds(pl.multiple_of(feat * size, size), size)
    other = pl.ds(pl.multiple_of((1 - feat) * size, size), size)
    return own, other


def start_copies(source, target, sems, first, pieces):
    rows = source.shape[0] // pieces
    copies = []
    for n in range(pieces):
        part = pl.ds(n * rows, rows)
        copies.append(pltpu.make_async_copy(source.at[part], target.at[part], sems.at[first + n]))
        copies[-1].start()
    return copies


def wait_copies(copies):
    for copy in copies:
        copy.wait()


def own_features_kernel(feat, grid, mesh, w_send, w_recv, grid_part, mesh_part, send_rest, recv_rest, *scratch):
    ws, g, wr, m, sems = scratch
    first = start_copies(w_send, ws, sems, 0, 4) + start_copies(grid, g, sems, 4, 4)
    second = start_copies(w_recv, wr, sems, 8, 4) + start_copies(mesh, m, sems, 12, 4)
    own, other = halves_of(feat[0], g.shape[1])
    wait_copies(first)
    grid_part[...] = dot(g[...], ws[own, :])
    send_rest[...] = ws[other, :]
    wait_copies(second)
    mesh_part[...] = dot(m[...], wr[own, :])
    recv_rest[...] = wr[other, :]


def other_features_kernel(part, rest, other, *outs):
    width = outs[0].shape[1]
    for c, out in enumerate(outs):
        lanes = slice(c * width, (c + 1) * width)
        out[...] = (part[:, lanes] + dot(other[...], rest[:, lanes])).astype(BF16)


def project(grid, mesh, w_send, w_recv, n_chunks):
    grid_other, mesh_other = swap(grid), swap(mesh)
    hidden, feats = w_send.shape[1], grid.shape[1]
    parts = call(
        own_features_kernel,
        [
            shape_of((grid.shape[0], hidden), F32),
            shape_of((mesh.shape[0], hidden), F32),
            shape_of((feats, hidden), BF16),
            shape_of((feats, hidden), BF16),
        ],
        position("feat"),
        *[pltpu.with_memory_space_constraint(x, pltpu.HBM) for x in (grid, mesh, w_send, w_recv)],
        specs=[SMEM] + [HBM] * 4,
        scratch=[pltpu.VMEM(x.shape, BF16) for x in (w_send, grid, w_recv, mesh)] + [pltpu.SemaphoreType.DMA((16,))],
        name="own_features",
        mib=16,
    )
    grid_part, mesh_part, send_rest, recv_rest = parts
    chunk = shape_of((grid.shape[0], hidden // n_chunks), BF16)
    chunks = call(
        other_features_kernel, [chunk] * n_chunks, grid_part, send_rest, grid_other, name="other_grid_features"
    )
    chunks, mesh_part = lax.optimization_barrier((chunks, mesh_part))
    (mesh_proj,) = call(
        other_features_kernel,
        [shape_of((mesh.shape[0], hidden), BF16)],
        mesh_part,
        recv_rest,
        mesh_other,
        name="other_mesh_features",
    )
    return chunks, mesh_proj, mesh_other


def across(row):
    return jnp.transpose(jnp.broadcast_to(row.astype(F32), (LANES, LANES))).astype(I32)


def slots_of(ref, n, cap):
    return ref[:, pl.ds(pl.multiple_of(n * cap, cap), cap)]


def one_hot_rows(row, width, at):
    return (across(row[:, at : at + LANES])[:, :1] == iota((LANES, width), 1)).astype(BF16)


def pack_own_kernel(bits, me, send, g0, g1, *outs):
    width, cap = g0.shape[1], outs[0].shape[0]
    for k, out in zip(bits, outs):
        ids = slots_of(send, me[0] ^ k, cap)
        for at in range(0, cap, LANES):
            hot = one_hot_rows(ids, g0.shape[0], at)
            out[at : at + LANES, :width] = dot(hot, g0[...]).astype(BF16)
            out[at : at + LANES, width:] = dot(hot, g1[...]).astype(BF16)


def prepare_kernel(half, me, send_mirror, recv, mesh_proj, bias, pick, into, term):
    cap = pick.shape[0] // half
    for k in range(half):
        ids, rows = slots_of(send_mirror, me[0] ^ k, cap), slots_of(recv, me[0] ^ k ^ half, cap)
        first = k * cap
        into[:, first : first + cap] = (iota((into.shape[0], cap), 0) == rows).astype(BF16)
        for at in range(0, cap, LANES):
            here = slice(first + at, first + at + LANES)
            pick[here, :] = one_hot_rows(ids, pick.shape[1], at)
            term[here, :] = dot(one_hot_rows(rows, mesh_proj.shape[0], at), mesh_proj[...]) + bias[...]


def add_slots(total, grid, rows, mesh_proj, bias):
    hot = [one_hot_rows(rows, mesh_proj.shape[0], at) for at in range(0, rows.shape[1], LANES)]
    term = dot(jnp.concatenate(hot, axis=0), mesh_proj[...])
    into = (iota((mesh_proj.shape[0], rows.shape[1]), 0) == rows).astype(BF16)
    return total + dot(into, silu_bf16(grid + term + bias[...]))


def local_sums_kernel(cap, me, send, recv, g0, g1, mesh_proj, bias, out):
    ids, rows = slots_of(send, me[0], cap), slots_of(recv, me[0], cap)
    hot = jnp.concatenate([one_hot_rows(ids, g0.shape[0], at) for at in range(0, cap, LANES)], axis=0)
    grid = jnp.concatenate([dot(hot, g0[...]), dot(hot, g1[...])], axis=1)
    out[...] = add_slots(0.0, grid, rows, mesh_proj, bias)


def arrived_sums_kernel(cap, me, recv, mesh_proj, bias, start, *refs):
    *blocks, out = refs
    total = start[...]
    for k, block in enumerate(blocks, 1):
        total = add_slots(total, block[...].astype(F32), slots_of(recv, me[0] ^ k, cap), mesh_proj, bias)
    out[...] = total


def pack_mirror_kernel(pick, mirrored, *outs):
    cap = outs[0].shape[0]
    for k, out in enumerate(outs, 1):
        out[...] = dot(pick[k * cap : (k + 1) * cap, :], mirrored[...]).astype(BF16)


def mirror_sums_kernel(chunk, first, pick, mirrored, into, term, total, *refs):
    *blocks, out = refs
    width = out.shape[1]
    lanes = slice(chunk * width, (chunk + 1) * width)
    cap = into.shape[1] // 4
    if first:
        blocks = [dot(pick[:cap, :], mirrored[...])]
        sums = total[:, lanes]
    else:
        sums = total[...]
    for k, block in enumerate(blocks, 0 if first else 1):
        rows = slice(k * cap, (k + 1) * cap)
        hidden = silu_bf16(block[...].astype(F32) + term[rows, lanes])
        sums += dot(into[:, rows], hidden)
    out[...] = sums.astype(out.dtype)


def sums_by_halves(grid_chunks, mesh_rproj, bias, send_grid, recv_row, n_dom, select, lists):
    half = n_dom // 2
    mesh_rows, hidden = mesh_rproj.shape
    grid_rows, width = grid_chunks[0].shape
    cap = send_grid.shape[1] // n_dom
    me, bias = position("dom"), bias[None, :]

    def pack_own(*bits):
        blocks = call(
            functools.partial(pack_own_kernel, bits),
            [shape_of((cap, hidden), BF16)] * len(bits),
            me,
            send_grid,
            *grid_chunks,
            specs=[SMEM] + [VMEM] * 3,
            name="pack_own",
        )
        return blocks

    packed = pack_own(3, 2)
    packed, first = lax.optimization_barrier((packed, grid_chunks[0]))
    arrived = {k: from_xor(block, k, n_dom) for k, block in zip((3, 2), packed)}
    mirrored = [from_xor(first, half, n_dom)]
    send_mirror = from_xor(send_grid, half, n_dom)
    own = call(
        functools.partial(local_sums_kernel, cap),
        shape_of((mesh_rows, hidden), F32),
        me,
        send_grid,
        recv_row,
        *grid_chunks,
        mesh_rproj,
        bias,
        specs=[SMEM] + [VMEM] * 6,
        name="local_sums",
    )
    own, packed, lists = lax.optimization_barrier((own, pack_own(1), lists))
    arrived[1] = from_xor(packed[0], 1, n_dom)
    selections = select(me, *lists)
    send_mirror, later, selections = lax.optimization_barrier((send_mirror, grid_chunks[1], selections))
    mirrored.append(from_xor(later, half, n_dom))
    arrived = [arrived[k] for k in range(1, half)]
    pick, into, term = call(
        functools.partial(prepare_kernel, half),
        [
            shape_of((half * cap, grid_rows), BF16),
            shape_of((mesh_rows, half * cap), BF16),
            shape_of((half * cap, hidden), F32),
        ],
        me,
        send_mirror,
        recv_row,
        mesh_rproj,
        bias,
        specs=[SMEM] + [VMEM] * 4,
        name="prepare",
    )
    arrived, mirrored[1] = lax.optimization_barrier((arrived, mirrored[1]))
    own = call(
        functools.partial(arrived_sums_kernel, cap),
        shape_of((mesh_rows, hidden), F32),
        me,
        recv_row,
        mesh_rproj,
        bias,
        own,
        *arrived,
        specs=[SMEM] + [VMEM] * (4 + len(arrived)),
        name="arrived_sums",
    )
    chunks = []
    for c in range(2):
        blocks = call(
            pack_mirror_kernel, [shape_of((cap, width), BF16)] * (half - 1), pick, mirrored[c], name="pack_mirror"
        )
        blocks = [from_xor(block, k, n_dom) for k, block in enumerate(blocks, 1)]
        total = call(
            functools.partial(mirror_sums_kernel, c, True),
            shape_of((mesh_rows, width), F32),
            pick,
            mirrored[c],
            into,
            term,
            own,
            name="own_mirror_sums",
        )
        chunks.append(
            call(
                functools.partial(mirror_sums_kernel, c, False),
                shape_of((mesh_rows, width), BF16),
                pick,
                mirrored[c],
                into,
                term,
                total,
                *blocks,
                name="mirror_sums",
            )
        )
    return chunks, selections


def sums_by_all_to_all(grid_chunks, mesh_rproj, bias, send_grid, recv_row, n_dom, select, lists):
    def rows_of(table, index):
        hot = index[0][:, None] == iota((index.shape[1], table.shape[0]), 1)
        return dot(hot.astype(BF16), table)

    packed = rows_of(grid_chunks[0], send_grid).astype(BF16)
    arrived = lax.all_to_all(packed, "dom", split_axis=0, concat_axis=0, tiled=True)
    hidden = silu_bf16(arrived.astype(F32) + rows_of(mesh_rproj, recv_row) + bias[None, :])
    into = iota((mesh_rproj.shape[0], recv_row.shape[1]), 0) == recv_row
    return [dot(into.astype(BF16), hidden).astype(BF16)], select(position("dom"), *lists)


def list_rows(ref, me, k, blocks):
    size = ref.shape[1] // blocks
    return slots_of(ref, me ^ k, size) if blocks > 1 else ref[...]


def select_kernel(blocks, me, halo_rows, src, dst, halo_pick, near_src, near_dst, far_src, into):
    mesh_rows = into.shape[0]
    size = halo_pick.shape[0] // blocks
    for k in range(blocks):
        rows = list_rows(halo_rows, me[0], k, blocks)
        for a in range(0, size, LANES):
            halo_pick[k * size + a : k * size + a + LANES, :] = one_hot_rows(rows, mesh_rows, a)
    for b in range(src.shape[0]):
        rows = slice(b * LANES, (b + 1) * LANES)
        senders, receivers = src[b : b + 1, :], dst[b : b + 1, :]
        far = senders - mesh_rows
        if blocks > 1:
            far = jnp.where(far < 0, far, ((far // size) ^ me[0]) * size + far % size)
        near_src[rows, :] = one_hot_rows(senders, mesh_rows, 0)
        near_dst[rows, :] = one_hot_rows(receivers, mesh_rows, 0)
        far_src[rows, :] = one_hot_rows(far, far_src.shape[1], 0)
        into[:, rows] = (iota((mesh_rows, LANES), 0) == receivers).astype(BF16)


def encode_base_kernel(n_chunks, feat, *refs):
    chunks, others = refs[:n_chunks], refs[n_chunks : 2 * n_chunks]
    mesh_own, mesh_other, w_own, w_other, w2_own, w2_other, base, w2 = refs[2 * n_chunks :]
    feats = mesh_own.shape[1]
    own, rest = halves_of(feat[0], feats)
    base[:, own] = mesh_own[...].astype(F32)
    base[:, rest] = mesh_other[...].astype(F32)
    at = 0
    for mine, other in zip(chunks, others):
        rows = slice(at, at + mine.shape[1])
        base[...] += dot(mine[...], w_own[rows, :]) + dot(other[...], w_other[rows, :])
        at += mine.shape[1]
    w2[: w2_own.shape[0], :] = w2_own[:, own]
    w2[w2_own.shape[0] :, :] = w2_other[:, own]


def encode_kernel(first, base, mine, other, w_own, w_other, w_send, pick, full, send_proj, *halo):
    rows = slice(first, first + mine.shape[1])
    full[...] = (base[...] + dot(mine[...], w_own[rows, :]) + dot(other[...], w_other[rows, :])).astype(BF16)
    send_proj[...] = dot(full[...], w_send[...]).astype(BF16)
    size = halo[0].shape[0]
    for k, out in enumerate(halo):
        out[...] = dot(pick[k * size : (k + 1) * size, :], send_proj[...]).astype(BF16)


def near_edges_kernel(feat, full, send_proj, w_recv, bias, near_src, near_dst, near, encoded):
    own, _ = halves_of(feat[0], encoded.shape[1])
    encoded[...] = full[:, own]
    recv_proj = dot(full[...], w_recv[...]).astype(BF16)
    for at in range(0, near.shape[0], STEP):
        rows = slice(at, at + STEP)
        near[rows, :] = dot(near_src[rows, :], send_proj[...]) + dot(near_dst[rows, :], recv_proj) + bias[...]


def edge_sums_kernel(near, far_pick, into, *refs):
    *halo, out, table = refs
    size = halo[0].shape[0]
    for k, block in enumerate(halo):
        table[k * size : (k + 1) * size, :] = block[...]
    total = jnp.zeros(out.shape, F32)
    for at in range(0, near.shape[0], STEP):
        rows = slice(at, at + STEP)
        hidden = silu_bf16(near[rows, :] + dot(far_pick[rows, :], table[...]))
        total += dot(into[:, rows], hidden)
    out[...] = total.astype(BF16)


def own_output_kernel(encoded, mine, w_out, out):
    out[...] = encoded[...].astype(F32) + dot(mine[...], w_out[: mine.shape[1], :])


def output_kernel(part, other, w_out, out):
    out[...] = (part[...] + dot(other[...], w_out[other.shape[1] :, :])).astype(BF16)


def shards(
    grid_lat,
    mesh_lat,
    w_grid_send,
    w_grid_recv,
    g2m_bias,
    w_grid_out,
    w_edge_send,
    w_edge_recv,
    edge_bias,
    w_edge_out,
    send_grid,
    recv_row,
    halo_rows,
    edge_src,
    edge_dst,
):
    n_dom = lax.axis_size("dom")
    mesh_rows, feats = mesh_lat.shape
    hidden = w_grid_send.shape[1]
    halves = n_dom == 8
    grid_chunks, mesh_rproj, mesh_other = project(grid_lat, mesh_lat, w_grid_send, w_grid_recv, 2 if halves else 1)
    grid_chunks, mesh_rproj, send_grid, recv_row, w_other, w2_other = lax.optimization_barrier(
        (grid_chunks, mesh_rproj, send_grid, recv_row, swap(w_grid_out), swap(w_edge_out))
    )
    me, feat = position("dom"), position("feat")
    blocks = n_dom if halves else 1
    n_halo, edges = halo_rows.shape[1], edge_src.shape[0] * edge_src.shape[1]
    def select(me, halo_rows, src, dst):
        return call(
            functools.partial(select_kernel, blocks),
            [
                shape_of((n_halo, mesh_rows), BF16),
                shape_of((edges, mesh_rows), BF16),
                shape_of((edges, mesh_rows), BF16),
                shape_of((edges, n_halo), BF16),
                shape_of((mesh_rows, edges), BF16),
            ],
            me,
            halo_rows,
            src,
            dst,
            specs=[SMEM] + [VMEM] * 3,
            name="select",
        )

    sums = sums_by_halves if halves else sums_by_all_to_all
    lists = (halo_rows, edge_src, edge_dst)
    chunks, selections = sums(grid_chunks, mesh_rproj, g2m_bias, send_grid, recv_row, n_dom, select, lists)
    pick, near_src, near_dst, far_src, into = selections
    *early, last = chunks
    base, w_out = call(
        functools.partial(encode_base_kernel, len(early)),
        [shape_of((mesh_rows, 2 * feats), F32), shape_of((2 * w_edge_out.shape[0], feats), BF16)],
        feat,
        *early,
        *[swap(chunk) for chunk in early],
        mesh_lat,
        mesh_other,
        w_grid_out,
        w_other,
        w_edge_out,
        w2_other,
        specs=[SMEM] + [VMEM] * (2 * len(early) + 6),
        name="encode_base",
    )
    full, send_proj, *halo = call(
        functools.partial(encode_kernel, hidden - last.shape[1]),
        [shape_of((mesh_rows, 2 * feats), BF16), shape_of((mesh_rows, hidden), BF16)]
        + [shape_of((n_halo // blocks, hidden), BF16)] * blocks,
        base,
        last,
        swap(last),
        w_grid_out,
        w_other,
        w_edge_send,
        pick,
        name="encode",
    )
    if halves:
        arrived = {k: from_xor(halo[k], k, n_dom) for k in (6, 7, 4, 5, 3, 2, 1)}
        halo = [halo[0]] + [arrived[k] for k in range(1, n_dom)]
    else:
        halo = [lax.all_to_all(halo[0], "dom", split_axis=0, concat_axis=0, tiled=True)]
    near, mesh_encoded = call(
        near_edges_kernel,
        [shape_of((edges, hidden), F32), shape_of((mesh_rows, feats), BF16)],
        feat,
        full,
        send_proj,
        w_edge_recv,
        edge_bias[None, :],
        near_src,
        near_dst,
        specs=[SMEM] + [VMEM] * 6,
        name="near_edges",
    )
    proc_sum = call(
        edge_sums_kernel,
        shape_of((mesh_rows, hidden), BF16),
        near,
        far_src,
        into,
        *halo,
        scratch=[pltpu.VMEM((n_halo, hidden), BF16)],
        name="edge_sums",
    )
    part = call(
        own_output_kernel, shape_of((mesh_rows, feats), F32), mesh_encoded, proc_sum, w_out, name="own_output"
    )
    mesh_out = call(
        output_kernel, shape_of((mesh_rows, feats), BF16), part, swap(proc_sum), w_out, name="output"
    )
    return (mesh_encoded, mesh_out)


def solution(mesh):
    rows = P(("member", "dom"), "feat")
    columns, lists = P(None, "feat"), P("dom", None)
    placed = (rows, rows, columns, columns, P("feat"), P("feat", None), columns, columns, P("feat"), P("feat", None))
    return jax.shard_map(
        shards,
        mesh=mesh,
        in_specs=placed + (lists,) * 5,
        out_specs=(rows, rows),
        check_vma=False,
    )
```

time: 170 us -> 76.8 us (0.45)
  blocking collectives: 78.1 us -> 0 us
  matrix products: 33.4 us -> 0 us
  starting transfers between devices: 0.34 us -> 30.5 us
  Pallas kernels: 0 us -> 27.1 us
  waiting for transfers between devices: 37.5 us -> 17.9 us
  between operations: 13.9 us -> 1.02 us
  other arithmetic: 3.83 us -> 0 us
  local copies, waits for them, and re-layouts: 1.93 us -> 0.08 us
    all_to_all x2 -> x0, blocking collectives: 75.9 us -> none  [the longest x1 55.4 us: shards(): lax.all_to_all(packed, 'dom', split_axis=0, concat_axis=0, tiled=True)]
    dot_general x8 -> x0, matrix products: 33.4 us -> none  [the longest x5 20.3 us: pick_rows(): jnp.dot(selector, table, preferred_element_type=jnp.float32)]
    ppermute x0 -> x26, starting transfers between devices: none -> 30.5 us  [the longest x19 29.2 us: from_xor(): return lax.ppermute(x, 'dom', [(i, i ^ bits) for i in range(n_dom)])]
    pallas_call x0 -> x21, Pallas kernels: none -> 27.1 us  [call(): pl.pallas_call(kernel, out_shape=out_shape, in_specs=[VMEM] * len(args) i...]
    reduce_scatter x2 -> x0, waiting for transfers between devices: 19.8 us -> none  [the longest x1 9.91 us: shards(): lax.psum_scatter(proc_partial, 'feat', scatter_dimension=1, tiled=True)]
    ppermute x0 -> x26, waiting for transfers between devices: none -> 17.9 us  [the longest x19 15.8 us: from_xor(): return lax.ppermute(x, 'dom', [(i, i ^ bits) for i in range(n_dom)])]
    all_gather x2 -> x0, waiting for transfers between devices: 17.7 us -> none  [the longest x1 9.07 us: shards(): slot_full = lax.all_gather(arrived, 'feat', axis=1, tiled=True)]
    convert_element_type x2 -> x0, other arithmetic: 2.89 us -> none  [the longest x1 1.8 us: shards(): (mesh_encoded.astype(jnp.float32) + proc_update).astype(jnp.bfloat16)]
  transfers between devices with their start and end apart: 4 -> 26, of which waited for: 4 -> 7; matrix products, arithmetic and copies ran while one was open for 0% -> 0% of each run, Pallas kernels for 0% -> 28%
where the time goes in v3:
time: 76.8 us; the launch traced here: 76.7 us
  starting transfers between devices  30.5 us (40%)
  Pallas kernels  27.1 us (35%)
  waiting for transfers between devices  17.9 us (23%)
  between operations  1.02 us (1%)
    ppermute x19, starting transfers between devices, from_xor(): return lax.ppermute(x, 'dom', [(i, i ^ bits) for i in range(n_dom)])  29.2 us
    pallas_call x21, Pallas kernels, call(): pl.pallas_call(kernel, out_shape=out_shape, in_specs=[VMEM] * len(args) i...  27.1 us
    ppermute x19, waiting for transfers between devices, from_xor(): return lax.ppermute(x, 'dom', [(i, i ^ bits) for i in range(n_dom)])  15.8 us
    ppermute x7, waiting for transfers between devices, swap(): return lax.ppermute(x, 'feat', [(0, 1), (1, 0)])  2.16 us
  transfers between devices with their start and end apart: 26, of which 7 were waited for; matrix products, arithmetic and copies ran while one was open for 0% of the time, Pallas kernels for 28%

profile of v3, /device:TPU:0, one launch (start us, length us, event | category | flops | bytes accessed | tf_op | source)
XLA Modules:
  0.0 76.7 jit_solution(14915332518872036442)
XLA Ops:
  0.6 0.5 collective-permute-start
  1.1 0.1 collective-permute-start.1
  1.2 0.4 collective-permute-start.3
  1.7 0.1 collective-permute-start.2
  1.7 2.0 %own_features.1 = (f32[1024,256]{1,0:T(8,128)S(1)}, f32[512,256]{1,0:T(8,128)S(1)}, bf16[256,256]{1,0:T(8,128)(2,1)S(1)}, bf16[256,256]{1,0:T(8,128)(2,1)S(1)}) custom-call(s32[1]{0:T(128)} %bitcast.feat, bf16[1024,256]{1,0:T(8,128)(2,1)} %grid.1, bf16[512,256]{1,0:T(8,128)(2,1)} %refs_2_.1, bf16[512,256]{1,0:T(8,128)(2,1)} %w_send.2, bf16[512,256]{1,0:T(8,128)(2,1)} %w_recv.2), custom_call_target="tpu_custom_call" | custom-call | tf_op jit(solution)/shard_map/own_features/pallas_call | solution.py:48
  3.8 0.4 other_grid_features.1
  4.3 0.2 other_mesh_features.1.mesh_proj
  4.6 1.5 %pack_own.3 = (bf16[512,256]{1,0:T(8,128)(2,1)S(1)}, bf16[512,256]{1,0:T(8,128)(2,1)S(1)}) custom-call(s32[1]{0:T(128)} %bitcast.1.me, s32[1,4096]{1,0:T(1,128)S(1)} %copy-done.7, bf16[1024,128]{1,0:T(8,128)(2,1)S(1)} %get-tuple-element.93.g0, bf16[1024,128]{1,0:T(8,128)(2,1)S(1)} %get-tuple-element.100.g1), custom_call_target="tpu_custom_call" | custom-call | tf_op jit(solution)/shard_map/pack_own/pallas_call | solution.py:48
  6.1 4.1 %collective-permute-start.5 = (bf16[1024,128]{1,0:T(8,128)(2,1)S(1)}, bf16[1024,128]{1,0:T(8,128)(2,1)S(1)}, u32[]{:S(2)}, u32[]{:S(2)}) collective-permute-start(bf16[1024,128]{1,0:T(8,128)(2,1)S(1)} %get-tuple-element.93.g0), channel_id=1, source_target_pairs={{0,8},{2,10},{4,12},{6,14},{8,0},{10,2},{12,4},{14,6},{1,9},{3,11}... | collective-permute-start | bytes 786440 | tf_op jit(solution)/shard_map/ppermute | solution.py:44
  10.2 0.1 collective-permute-start.4
  10.2 0.9 %pack_own.2 = bf16[512,256]{1,0:T(8,128)(2,1)S(1)} custom-call(s32[1]{0:T(128)} %bitcast.1.me, s32[1,4096]{1,0:T(1,128)S(1)} %copy-done.7, bf16[1024,128]{1,0:T(8,128)(2,1)S(1)} %get-tuple-element.93.g0, bf16[1024,128]{1,0:T(8,128)(2,1)S(1)} %get-tuple-element.100.g1), custom_call_target="tpu_custom_call" | custom-call | tf_op jit(solution)/shard_map/pack_own/pallas_call | solution.py:48
  11.2 1.6 %local_sums.1.start = f32[512,256]{1,0:T(8,128)S(1)} custom-call(s32[1]{0:T(128)} %bitcast.1.me, s32[1,4096]{1,0:T(1,128)S(1)} %copy-done.7, s32[1,4096]{1,0:T(1,128)S(1)} %copy-done.6, bf16[1024,128]{1,0:T(8,128)(2,1)S(1)} %get-tuple-element.93.g0, bf16[1024,128]{1,0:T(8,128)(2,1)S(1)} %get-tuple-element.100.g1, ...), custom_call_target="tpu_custom_call" | custom-call | tf_op jit(solution)/shard_map/local_sums/pallas_call | solution.py:48
  12.8 1.8 %collective-permute-start.6 = (bf16[512,256]{1,0:T(8,128)(2,1)S(1)}, bf16[512,256]{1,0:T(8,128)(2,1)S(1)}, u32[]{:S(2)}, u32[]{:S(2)}) collective-permute-start(bf16[512,256]{1,0:T(8,128)(2,1)S(1)} %pack_own.2), channel_id=1, source_target_pairs={{0,2},{2,0},{4,6},{6,4},{8,10},{10,8},{12,14},{14,12},{1,3},{3,1},... | collective-permute-start | bytes 786440 | tf_op jit(solution)/shard_map/ppermute | solution.py:44
  14.6 1.6 %collective-permute-start.7 = (bf16[512,256]{1,0:T(8,128)(2,1)S(1)}, bf16[512,256]{1,0:T(8,128)(2,1)S(1)}, u32[]{:S(2)}, u32[]{:S(2)}) collective-permute-start(bf16[512,256]{1,0:T(8,128)(2,1)S(1)} %get-tuple-element.98), channel_id=1, source_target_pairs={{0,4},{2,6},{4,0},{6,2},{8,12},{10,14},{12,8},{14,10},{1,5},{3,7},... | collective-permute-start | bytes 786440 | tf_op jit(solution)/shard_map/ppermute | solution.py:44
  16.2 0.1 collective-permute-start.8
  16.4 3.5 %select.1 = (bf16[1024,512]{1,0:T(8,128)(2,1)S(1)}, bf16[2048,512]{1,0:T(8,128)(2,1)S(1)}, bf16[2048,512]{1,0:T(8,128)(2,1)S(1)}, bf16[2048,1024]{1,0:T(8,128)(2,1)S(1)}, bf16[512,2048]{1,0:T(8,128)(2,1)S(1)}) custom-call(s32[1]{0:T(128)} %bitcast.1.me, s32[1,1024]{1,0:T(1,128)S(1)} %copy-done.11, s32[16,128]{1,0:T(8,128)S(1)} %copy-done.9, ...), custom_call_target="tpu_custom_call" | custom-call | tf_op jit(solution)/shard_map/select/pallas_call | solution.py:48
  19.9 3.2 %collective-permute-done.4.send_mirror = s32[1,4096]{1,0:T(1,128)S(1)} collective-permute-done((s32[1,4096]{1,0:T(1,128)S(1)}, s32[1,4096]{1,0:T(1,128)S(1)}, u32[]{:S(2)}, u32[]{:S(2)}) %collective-permute-start.4) | collective-permute-done | bytes 16416 | tf_op jit(solution)/shard_map/ppermute | solution.py:44
  23.1 2.8 %prepare.1 = (bf16[2048,1024]{1,0:T(8,128)(2,1)S(1)}, bf16[512,2048]{1,0:T(8,128)(2,1)S(1)}, f32[2048,256]{1,0:T(8,128)S(1)}) custom-call(s32[1]{0:T(128)} %bitcast.1.me, s32[1,4096]{1,0:T(1,128)S(1)} %collective-permute-done.4.send_mirror, s32[1,4096]{1,0:T(1,128)S(1)} %copy-done.6, bf16[512,256]{1,0:T(8,128)(2,1)S(1)} %other_mesh_features.1.mesh_proj, ...), custom_call_target="tpu_custom_call" | custom-call | tf_op jit(solution)/shard_map/prepare/pallas_call | solution.py:48
  26.0 1.0 %pack_mirror.2 = (bf16[512,128]{1,0:T(8,128)(2,1)S(1)}, bf16[512,128]{1,0:T(8,128)(2,1)S(1)}, bf16[512,128]{1,0:T(8,128)(2,1)S(1)}) custom-call(bf16[2048,1024]{1,0:T(8,128)(2,1)S(1)} %get-tuple-element.90.pick, bf16[1024,128]{1,0:T(8,128)(2,1)S(1)} %collective-permute-done.5.mirrored), custom_call_target="tpu_custom_call" | custom-call | tf_op jit(solution)/shard_map/pack_mirror/pallas_call | solution.py:48
  26.9 1.8 %collective-permute-start.10 = (bf16[512,128]{1,0:T(8,128)(2,1)S(1)}, bf16[512,128]{1,0:T(8,128)(2,1)S(1)}, u32[]{:S(2)}, u32[]{:S(2)}) collective-permute-start(bf16[512,128]{1,0:T(8,128)(2,1)S(1)} %get-tuple-element.104), channel_id=1, source_target_pairs={{0,2},{2,0},{4,6},{6,4},{8,10},{10,8},{12,14},{14,12},{1,3},{3,1},... | collective-permute-start | bytes 393224 | tf_op jit(solution)/shard_map/ppermute | solution.py:44
  28.7 4.1 %collective-permute-start.11 = (bf16[512,128]{1,0:T(8,128)(2,1)S(1)}, bf16[512,128]{1,0:T(8,128)(2,1)S(1)}, u32[]{:S(2)}, u32[]{:S(2)}) collective-permute-start(bf16[512,128]{1,0:T(8,128)(2,1)S(1)} %get-tuple-element.105), channel_id=1, source_target_pairs={{0,4},{2,6},{4,0},{6,2},{8,12},{10,14},{12,8},{14,10},{1,5},{3,7},... | collective-permute-start | bytes 393224 | tf_op jit(solution)/shard_map/ppermute | solution.py:44
  32.8 7.0 %collective-permute-done.8.refs_2_ = bf16[512,256]{1,0:T(8,128)(2,1)S(1)} collective-permute-done((bf16[512,256]{1,0:T(8,128)(2,1)S(1)}, bf16[512,256]{1,0:T(8,128)(2,1)S(1)}, u32[]{:S(2)}, u32[]{:S(2)}) %collective-permute-start.8) | collective-permute-done | bytes 262176 | tf_op jit(solution)/shard_map/ppermute | solution.py:44
  39.8 1.0 %pack_mirror.3 = (bf16[512,128]{1,0:T(8,128)(2,1)S(1)}, bf16[512,128]{1,0:T(8,128)(2,1)S(1)}, bf16[512,128]{1,0:T(8,128)(2,1)S(1)}) custom-call(bf16[2048,1024]{1,0:T(8,128)(2,1)S(1)} %get-tuple-element.90.pick, bf16[1024,128]{1,0:T(8,128)(2,1)S(1)} %collective-permute-done.9.mirrored), custom_call_target="tpu_custom_call" | custom-call | tf_op jit(solution)/shard_map/pack_mirror/pallas_call | solution.py:48
  40.8 1.7 %collective-permute-start.14 = (bf16[512,128]{1,0:T(8,128)(2,1)S(1)}, bf16[512,128]{1,0:T(8,128)(2,1)S(1)}, u32[]{:S(2)}, u32[]{:S(2)}) collective-permute-start(bf16[512,128]{1,0:T(8,128)(2,1)S(1)} %get-tuple-element.111), channel_id=1, source_target_pairs={{0,2},{2,0},{4,6},{6,4},{8,10},{10,8},{12,14},{14,12},{1,3},{3,1},... | collective-permute-start | bytes 393224 | tf_op jit(solution)/shard_map/ppermute | solution.py:44
  42.5 1.8 %collective-permute-start.16 = (bf16[512,128]{1,0:T(8,128)(2,1)S(1)}, bf16[512,128]{1,0:T(8,128)(2,1)S(1)}, u32[]{:S(2)}, u32[]{:S(2)}) collective-permute-start(bf16[512,128]{1,0:T(8,128)(2,1)S(1)} %get-tuple-element.113), channel_id=1, source_target_pairs={{0,6},{2,4},{4,2},{6,0},{8,14},{10,12},{12,10},{14,8},{1,7},{3,5},... | collective-permute-start | bytes 393224 | tf_op jit(solution)/shard_map/ppermute | solution.py:44
  44.4 1.9 %arrived_sums.1.total = f32[512,256]{1,0:T(8,128)S(1)} custom-call(s32[1]{0:T(128)} %bitcast.1.me, s32[1,4096]{1,0:T(1,128)S(1)} %copy-done.6, bf16[512,256]{1,0:T(8,128)(2,1)S(1)} %other_mesh_features.1.mesh_proj, f32[1,256]{1,0:T(1,128)S(1)} %bitcast.6, f32[512,256]{1,0:T(8,128)S(1)} %local_sums.1.start, ...), custom_call_target="tpu_custom_call" | custom-call | tf_op jit(solution)/shard_map/arrived_sums/pallas_call | solution.py:48
  46.2 0.9 %own_mirror_sums.3.total = f32[512,128]{1,0:T(8,128)S(1)} custom-call(bf16[2048,1024]{1,0:T(8,128)(2,1)S(1)} %get-tuple-element.90.pick, bf16[1024,128]{1,0:T(8,128)(2,1)S(1)} %collective-permute-done.9.mirrored, bf16[512,2048]{1,0:T(8,128)(2,1)S(1)} %get-tuple-element.94.into, f32[2048,256]{1,0:T(8,128)S(1)} %get-tuple-element.95.term, ...), custom_call_target="tpu_custom_call" | custom-call | tf_op jit(solution)/shard_map/own_mirror_sums/pallas_call | solution.py:48
  47.1 0.9 %own_mirror_sums.2.total = f32[512,128]{1,0:T(8,128)S(1)} custom-call(bf16[2048,1024]{1,0:T(8,128)(2,1)S(1)} %get-tuple-element.90.pick, bf16[1024,128]{1,0:T(8,128)(2,1)S(1)} %collective-permute-done.5.mirrored, bf16[512,2048]{1,0:T(8,128)(2,1)S(1)} %get-tuple-element.94.into, f32[2048,256]{1,0:T(8,128)S(1)} %get-tuple-element.95.term, ...), custom_call_target="tpu_custom_call" | custom-call | tf_op jit(solution)/shard_map/own_mirror_sums/pallas_call | solution.py:48
  48.0 0.6 mirror_sums.2.refs_0_
  48.7 0.1 collective-permute-start.13
  48.8 0.6 collective-permute-done.16.refs_2_
  49.5 0.6 mirror_sums.3.mine
  50.1 0.1 collective-permute-start.17
  50.3 0.4 encode_base.1
  50.7 0.9 %collective-permute-done.17.other = bf16[512,128]{1,0:T(8,128)(2,1)S(1)} collective-permute-done((bf16[512,128]{1,0:T(8,128)(2,1)S(1)}, bf16[512,128]{1,0:T(8,128)(2,1)S(1)}, u32[]{:S(2)}, u32[]{:S(2)}) %collective-permute-start.17) | collective-permute-done | bytes 131104 | tf_op jit(solution)/shard_map/ppermute | solution.py:40
  51.6 1.2 %encode.1 = (bf16[512,512]{1,0:T(8,128)(2,1)S(1)}, bf16[512,256]{1,0:T(8,128)(2,1)S(1)}, bf16[128,256]{1,0:T(8,128)(2,1)S(1)}, bf16[128,256]{1,0:T(8,128)(2,1)S(...) custom-call(f32[512,512]{1,0:T(8,128)S(1)} %get-tuple-element.109.ba, ...), custom_call_target="tpu_custom_call" | custom-call | tf_op jit(solution)/shard_map/encode/pallas_call | solution.py:48
  52.8 1.6 %collective-permute-start.18 = (bf16[128,256]{1,0:T(8,128)(2,1)S(1)}, bf16[128,256]{1,0:T(8,128)(2,1)S(1)}, u32[]{:S(2)}, u32[]{:S(2)}) collective-permute-start(bf16[128,256]{1,0:T(8,128)(2,1)S(1)} %get-tuple-element.124), channel_id=1, source_target_pairs={{0,2},{2,0},{4,6},{6,4},{8,10},{10,8},{12,14},{14,12},{1,3},{3,1},... | collective-permute-start | bytes 196616 | tf_op jit(solution)/shard_map/ppermute | solution.py:44
  54.3 2.0 %collective-permute-start.20 = (bf16[128,256]{1,0:T(8,128)(2,1)S(1)}, bf16[128,256]{1,0:T(8,128)(2,1)S(1)}, u32[]{:S(2)}, u32[]{:S(2)}) collective-permute-start(bf16[128,256]{1,0:T(8,128)(2,1)S(1)} %get-tuple-element.126), channel_id=1, source_target_pairs={{0,6},{2,4},{4,2},{6,0},{8,14},{10,12},{12,10},{14,8},{1,7},{3,5},... | collective-permute-start | bytes 196616 | tf_op jit(solution)/shard_map/ppermute | solution.py:44
  56.3 3.2 %collective-permute-start.21 = (bf16[128,256]{1,0:T(8,128)(2,1)S(1)}, bf16[128,256]{1,0:T(8,128)(2,1)S(1)}, u32[]{:S(2)}, u32[]{:S(2)}) collective-permute-start(bf16[128,256]{1,0:T(8,128)(2,1)S(1)} %get-tuple-element.127), channel_id=1, source_target_pairs={{0,8},{2,10},{4,12},{6,14},{8,0},{10,2},{12,4},{14,6},{1,9},{3,11}... | collective-permute-start | bytes 196616 | tf_op jit(solution)/shard_map/ppermute | solution.py:44
  59.5 0.9 %collective-permute-start.22 = (bf16[128,256]{1,0:T(8,128)(2,1)S(1)}, bf16[128,256]{1,0:T(8,128)(2,1)S(1)}, u32[]{:S(2)}, u32[]{:S(2)}) collective-permute-start(bf16[128,256]{1,0:T(8,128)(2,1)S(1)} %get-tuple-element.128), channel_id=1, source_target_pairs={{0,10},{2,8},{4,14},{6,12},{8,2},{10,0},{12,6},{14,4},{1,11},{3,9}... | collective-permute-start | bytes 196616 | tf_op jit(solution)/shard_map/ppermute | solution.py:44
  60.4 4.4 %collective-permute-start.23 = (bf16[128,256]{1,0:T(8,128)(2,1)S(1)}, bf16[128,256]{1,0:T(8,128)(2,1)S(1)}, u32[]{:S(2)}, u32[]{:S(2)}) collective-permute-start(bf16[128,256]{1,0:T(8,128)(2,1)S(1)} %get-tuple-element.129), channel_id=1, source_target_pairs={{0,12},{2,14},{4,8},{6,10},{8,4},{10,6},{12,0},{14,2},{1,13},{3,15... | collective-permute-start | bytes 196616 | tf_op jit(solution)/shard_map/ppermute | solution.py:44
  64.8 2.1 %near_edges.1 = (f32[2048,256]{1,0:T(8,128)S(1)}, bf16[512,256]{1,0:T(8,128)(2,1)}) custom-call(s32[1]{0:T(128)} %bitcast.feat, bf16[512,512]{1,0:T(8,128)(2,1)S(1)} %get-tuple-element.115.full, bf16[512,256]{1,0:T(8,128)(2,1)S(1)} %get-tuple-element.116.send_proj, bf16[512,256]{1,0:T(8,128)(2,1)S(1)} %copy-done.3, f32[1,256]{1,0:T(1,128)S(1)} %bitcast.7, ...), custom_call_target="tpu_custom_call" | custom-call | tf_op jit(solution)/shard_map/near_edges/pallas_call | solution.py:48
  66.9 3.0 %collective-permute-done.22.refs_5_ = bf16[128,256]{1,0:T(8,128)(2,1)S(1)} collective-permute-done((bf16[128,256]{1,0:T(8,128)(2,1)S(1)}, bf16[128,256]{1,0:T(8,128)(2,1)S(1)}, u32[]{:S(2)}, u32[]{:S(2)}) %collective-permute-start.22) | collective-permute-done | bytes 65568 | tf_op jit(solution)/shard_map/ppermute | solution.py:44
  69.9 2.0 %collective-permute-done.24.refs_7_ = bf16[128,256]{1,0:T(8,128)(2,1)S(1)} collective-permute-done((bf16[128,256]{1,0:T(8,128)(2,1)S(1)}, bf16[128,256]{1,0:T(8,128)(2,1)S(1)}, u32[]{:S(2)}, u32[]{:S(2)}) %collective-permute-start.24) | collective-permute-done | bytes 65568 | tf_op jit(solution)/shard_map/ppermute | solution.py:44
  71.9 2.3 %edge_sums.1.mine = bf16[512,256]{1,0:T(8,128)(2,1)S(1)} custom-call(f32[2048,256]{1,0:T(8,128)S(1)} %get-tuple-element.120.near, bf16[2048,1024]{1,0:T(8,128)(2,1)S(1)} %get-tuple-element.121.far_pick, bf16[512,2048]{1,0:T(8,128)(2,1)S(1)} %get-tuple-element.122.into, bf16[128,256]{1,0:T(8,128)(2,1)S(1)} %get-tuple-element.123.refs_0_, ...), custom_call_target="tpu_custom_call" | custom-call | tf_op jit(solution)/shard_map/edge_sums/pallas_call | solution.py:48
  74.2 0.2 own_output.1.part
  74.4 1.3 %collective-permute-done.25.other = bf16[512,256]{1,0:T(8,128)(2,1)S(1)} collective-permute-done((bf16[512,256]{1,0:T(8,128)(2,1)S(1)}, bf16[512,256]{1,0:T(8,128)(2,1)S(1)}, u32[]{:S(2)}, u32[]{:S(2)}) %collective-permute-start.25) | collective-permute-done | bytes 262176 | tf_op jit(solution)/shard_map/ppermute | solution.py:40
  75.7 0.9 %output.1 = bf16[512,256]{1,0:T(8,128)(2,1)} custom-call(f32[512,256]{1,0:T(8,128)S(1)} %own_output.1.part, bf16[512,256]{1,0:T(8,128)(2,1)S(1)} %collective-permute-done.25.other, bf16[512,256]{1,0:T(8,128)(2,1)S(1)} %get-tuple-element.131.w_out), custom_call_target="tpu_custom_call" | custom-call | tf_op jit(solution)/shard_map/output/pallas_call | solution.py:48
  (51 shorter events, 0.3 us)
Async XLA Ops:
  0.6 3.2 %collective-permute-start = (bf16[1024,256]{1,0:T(8,128)(2,1)}, bf16[1024,256]{1,0:T(8,128)(2,1)S(1)}, u32[]{:S(2)}, u32[]{:S(2)}) collective-permute-start(bf16[1024,256]{1,0:T(8,128)(2,1)} %grid.1), channel_id=1, source_target_pairs={{0,1},{1,0},{2,3},{3,2},{4,5},{5,4},{6,7},{7,6},{8,9},{9,8},{10,11... | collective-permute-start | bytes 1572872 | tf_op jit(solution)/shard_map/ppermute | solution.py:40
  1.1 3.1 %collective-permute-start.1 = (bf16[512,256]{1,0:T(8,128)(2,1)}, bf16[512,256]{1,0:T(8,128)(2,1)S(1)}, u32[]{:S(2)}, u32[]{:S(2)}) collective-permute-start(bf16[512,256]{1,0:T(8,128)(2,1)} %refs_2_.1), channel_id=1, source_target_pairs={{0,1},{1,0},{2,3},{3,2},{4,5},{5,4},{6,7},{7,6},{8,9},{9,8},{10,11... | collective-permute-start | bytes 786440 | tf_op jit(solution)/shard_map/ppermute | solution.py:40
  1.2 3.3 %collective-permute-start.3 = (bf16[256,512]{1,0:T(8,128)(2,1)}, bf16[256,512]{1,0:T(8,128)(2,1)S(1)}, u32[]{:S(2)}, u32[]{:S(2)}) collective-permute-start(bf16[256,512]{1,0:T(8,128)(2,1)} %refs_6_.1), channel_id=1, source_target_pairs={{0,1},{1,0},{2,3},{3,2},{4,5},{5,4},{6,7},{7,6},{8,9},{9,8},{10,11... | collective-permute-start | bytes 786440 | tf_op jit(solution)/shard_map/ppermute | solution.py:40
  1.7 2.9 %collective-permute-start.2 = (bf16[256,512]{1,0:T(8,128)(2,1)}, bf16[256,512]{1,0:T(8,128)(2,1)S(1)}, u32[]{:S(2)}, u32[]{:S(2)}) collective-permute-start(bf16[256,512]{1,0:T(8,128)(2,1)} %w_own.1), channel_id=1, source_target_pairs={{0,1},{1,0},{2,3},{3,2},{4,5},{5,4},{6,7},{7,6},{8,9},{9,8},{10,11... | collective-permute-start | bytes 786440 | tf_op jit(solution)/shard_map/ppermute | solution.py:40
  1.7 2.8 %copy-start.7 = (s32[1,4096]{1,0:T(1,128)S(1)}, s32[1,4096]{1,0:T(1,128)}, u32[]{:S(2)}) copy-start(s32[1,4096]{1,0:T(1,128)} %send.2) | copy-start | bytes 49156
  3.8 7.4 %copy-start.6 = (s32[1,4096]{1,0:T(1,128)S(1)}, s32[1,4096]{1,0:T(1,128)}, u32[]{:S(2)}) copy-start(s32[1,4096]{1,0:T(1,128)} %recv.2) | copy-start | bytes 49156
  3.8 7.4 %copy-start.8 = (f32[256]{0:T(256)S(1)}, f32[256]{0:T(256)}, u32[]{:S(2)}) copy-start(f32[256]{0:T(256)} %param.19) | copy-start | bytes 3076
  4.2 12.1 %copy-start.9 = (s32[16,128]{1,0:T(8,128)S(1)}, s32[16,128]{1,0:T(8,128)}, u32[]{:S(2)}) copy-start(s32[16,128]{1,0:T(8,128)} %src) | copy-start | bytes 24580
  4.3 12.1 %copy-start.10 = (s32[16,128]{1,0:T(8,128)S(1)}, s32[16,128]{1,0:T(8,128)}, u32[]{:S(2)}) copy-start(s32[16,128]{1,0:T(8,128)} %dst) | copy-start | bytes 24580
  4.3 12.1 %copy-start.11 = (s32[1,1024]{1,0:T(1,128)S(1)}, s32[1,1024]{1,0:T(1,128)}, u32[]{:S(2)}) copy-start(s32[1,1024]{1,0:T(1,128)} %halo_rows) | copy-start | bytes 12292
  6.1 19.9 %collective-permute-start.5 = (bf16[1024,128]{1,0:T(8,128)(2,1)S(1)}, bf16[1024,128]{1,0:T(8,128)(2,1)S(1)}, u32[]{:S(2)}, u32[]{:S(2)}) collective-permute-start(bf16[1024,128]{1,0:T(8,128)(2,1)S(1)} %get-tuple-element.93.g0), channel_id=1, source_target_pairs={{0,8},{2,10},{4,12},{6,14},{8,0},{10,2},{12,4},{14,6},{1,9},{3,11}... | collective-permute-start | bytes 786440 | tf_op jit(solution)/shard_map/ppermute | solution.py:44
  10.2 13.0 %collective-permute-start.4 = (s32[1,4096]{1,0:T(1,128)S(1)}, s32[1,4096]{1,0:T(1,128)S(1)}, u32[]{:S(2)}, u32[]{:S(2)}) collective-permute-start(s32[1,4096]{1,0:T(1,128)S(1)} %copy-done.7), channel_id=1, source_target_pairs={{0,8},{2,10},{4,12},{6,14},{8,0},{10,2},{12,4},{14,6},{1,9},{3,11}... | collective-permute-start | bytes 49160 | tf_op jit(solution)/shard_map/ppermute | solution.py:44
  12.8 15.9 %collective-permute-start.6 = (bf16[512,256]{1,0:T(8,128)(2,1)S(1)}, bf16[512,256]{1,0:T(8,128)(2,1)S(1)}, u32[]{:S(2)}, u32[]{:S(2)}) collective-permute-start(bf16[512,256]{1,0:T(8,128)(2,1)S(1)} %pack_own.2), channel_id=1, source_target_pairs={{0,2},{2,0},{4,6},{6,4},{8,10},{10,8},{12,14},{14,12},{1,3},{3,1},... | collective-permute-start | bytes 786440 | tf_op jit(solution)/shard_map/ppermute | solution.py:44
  14.6 18.1 %collective-permute-start.7 = (bf16[512,256]{1,0:T(8,128)(2,1)S(1)}, bf16[512,256]{1,0:T(8,128)(2,1)S(1)}, u32[]{:S(2)}, u32[]{:S(2)}) collective-permute-start(bf16[512,256]{1,0:T(8,128)(2,1)S(1)} %get-tuple-element.98), channel_id=1, source_target_pairs={{0,4},{2,6},{4,0},{6,2},{8,12},{10,14},{12,8},{14,10},{1,5},{3,7},... | collective-permute-start | bytes 786440 | tf_op jit(solution)/shard_map/ppermute | solution.py:44
  16.2 23.6 %collective-permute-start.8 = (bf16[512,256]{1,0:T(8,128)(2,1)S(1)}, bf16[512,256]{1,0:T(8,128)(2,1)S(1)}, u32[]{:S(2)}, u32[]{:S(2)}) collective-permute-start(bf16[512,256]{1,0:T(8,128)(2,1)S(1)} %get-tuple-element.99), channel_id=1, source_target_pairs={{0,6},{2,4},{4,2},{6,0},{8,14},{10,12},{12,10},{14,8},{1,7},{3,5},... | collective-permute-start | bytes 786440 | tf_op jit(solution)/shard_map/ppermute | solution.py:44
  23.1 16.7 %collective-permute-start.9 = (bf16[1024,128]{1,0:T(8,128)(2,1)S(1)}, bf16[1024,128]{1,0:T(8,128)(2,1)S(1)}, u32[]{:S(2)}, u32[]{:S(2)}) collective-permute-start(bf16[1024,128]{1,0:T(8,128)(2,1)S(1)} %get-tuple-element.100.g1), channel_id=1, source_target_pairs={{0,8},{2,10},{4,12},{6,14},{8,0},{10,2},{12,4},{14,6},{1,9},{3,11}... | collective-permute-start | bytes 786440 | tf_op jit(solution)/shard_map/ppermute | solution.py:44
  26.9 15.6 %collective-permute-start.10 = (bf16[512,128]{1,0:T(8,128)(2,1)S(1)}, bf16[512,128]{1,0:T(8,128)(2,1)S(1)}, u32[]{:S(2)}, u32[]{:S(2)}) collective-permute-start(bf16[512,128]{1,0:T(8,128)(2,1)S(1)} %get-tuple-element.104), channel_id=1, source_target_pairs={{0,2},{2,0},{4,6},{6,4},{8,10},{10,8},{12,14},{14,12},{1,3},{3,1},... | collective-permute-start | bytes 393224 | tf_op jit(solution)/shard_map/ppermute | solution.py:44
  28.7 19.3 %collective-permute-start.11 = (bf16[512,128]{1,0:T(8,128)(2,1)S(1)}, bf16[512,128]{1,0:T(8,128)(2,1)S(1)}, u32[]{:S(2)}, u32[]{:S(2)}) collective-permute-start(bf16[512,128]{1,0:T(8,128)(2,1)S(1)} %get-tuple-element.105), channel_id=1, source_target_pairs={{0,4},{2,6},{4,0},{6,2},{8,12},{10,14},{12,8},{14,10},{1,5},{3,7},... | collective-permute-start | bytes 393224 | tf_op jit(solution)/shard_map/ppermute | solution.py:44
  32.8 15.2 %collective-permute-start.12 = (bf16[512,128]{1,0:T(8,128)(2,1)S(1)}, bf16[512,128]{1,0:T(8,128)(2,1)S(1)}, u32[]{:S(2)}, u32[]{:S(2)}) collective-permute-start(bf16[512,128]{1,0:T(8,128)(2,1)S(1)} %get-tuple-element.106), channel_id=1, source_target_pairs={{0,6},{2,4},{4,2},{6,0},{8,14},{10,12},{12,10},{14,8},{1,7},{3,5},... | collective-permute-start | bytes 393224 | tf_op jit(solution)/shard_map/ppermute | solution.py:44
  40.8 8.0 %collective-permute-start.14 = (bf16[512,128]{1,0:T(8,128)(2,1)S(1)}, bf16[512,128]{1,0:T(8,128)(2,1)S(1)}, u32[]{:S(2)}, u32[]{:S(2)}) collective-permute-start(bf16[512,128]{1,0:T(8,128)(2,1)S(1)} %get-tuple-element.111), channel_id=1, source_target_pairs={{0,2},{2,0},{4,6},{6,4},{8,10},{10,8},{12,14},{14,12},{1,3},{3,1},... | collective-permute-start | bytes 393224 | tf_op jit(solution)/shard_map/ppermute | solution.py:44
  42.5 6.3 %collective-permute-start.15 = (bf16[512,128]{1,0:T(8,128)(2,1)S(1)}, bf16[512,128]{1,0:T(8,128)(2,1)S(1)}, u32[]{:S(2)}, u32[]{:S(2)}) collective-permute-start(bf16[512,128]{1,0:T(8,128)(2,1)S(1)} %get-tuple-element.112), channel_id=1, source_target_pairs={{0,4},{2,6},{4,0},{6,2},{8,12},{10,14},{12,8},{14,10},{1,5},{3,7},... | collective-permute-start | bytes 393224 | tf_op jit(solution)/shard_map/ppermute | solution.py:44
  42.5 6.9 %collective-permute-start.16 = (bf16[512,128]{1,0:T(8,128)(2,1)S(1)}, bf16[512,128]{1,0:T(8,128)(2,1)S(1)}, u32[]{:S(2)}, u32[]{:S(2)}) collective-permute-start(bf16[512,128]{1,0:T(8,128)(2,1)S(1)} %get-tuple-element.113), channel_id=1, source_target_pairs={{0,6},{2,4},{4,2},{6,0},{8,14},{10,12},{12,10},{14,8},{1,7},{3,5},... | collective-permute-start | bytes 393224 | tf_op jit(solution)/shard_map/ppermute | solution.py:44
  48.7 1.6 %copy-start = (bf16[512,256]{1,0:T(8,128)(2,1)S(1)}, bf16[512,256]{1,0:T(8,128)(2,1)}, u32[]{:S(2)}) copy-start(bf16[512,256]{1,0:T(8,128)(2,1)} %refs_2_.1) | copy-start | bytes 786436
  48.7 1.6 %copy-start.1 = (bf16[256,512]{1,0:T(8,128)(2,1)S(1)}, bf16[256,512]{1,0:T(8,128)(2,1)}, u32[]{:S(2)}) copy-start(bf16[256,512]{1,0:T(8,128)(2,1)} %w_own.1) | copy-start | bytes 786436
  48.7 1.5 %copy-start.5 = (bf16[256,512]{1,0:T(8,128)(2,1)S(1)}, bf16[256,512]{1,0:T(8,128)(2,1)}, u32[]{:S(2)}) copy-start(bf16[256,512]{1,0:T(8,128)(2,1)} %refs_6_.1) | copy-start | bytes 786436
  48.7 2.8 %copy-start.2 = (bf16[512,256]{1,0:T(8,128)(2,1)S(1)}, bf16[512,256]{1,0:T(8,128)(2,1)}, u32[]{:S(2)}) copy-start(bf16[512,256]{1,0:T(8,128)(2,1)} %w_send.3) | copy-start | bytes 786436
  48.7 1.5 %collective-permute-start.13 = (bf16[512,128]{1,0:T(8,128)(2,1)S(1)}, bf16[512,128]{1,0:T(8,128)(2,1)S(1)}, u32[]{:S(2)}, u32[]{:S(2)}) collective-permute-start(bf16[512,128]{1,0:T(8,128)(2,1)S(1)} %mirror_sums.2.refs_0_), channel_id=1, source_target_pairs={{0,1},{1,0},{2,3},{3,2},{4,5},{5,4},{6,7},{7,6},{8,9},{9,8},{10,11... | collective-permute-start | bytes 393224 | tf_op jit(solution)/shard_map/ppermute | solution.py:40
  50.1 14.7 %copy-start.3 = (bf16[512,256]{1,0:T(8,128)(2,1)S(1)}, bf16[512,256]{1,0:T(8,128)(2,1)}, u32[]{:S(2)}) copy-start(bf16[512,256]{1,0:T(8,128)(2,1)} %w_recv.3) | copy-start | bytes 786436
  50.1 14.7 %copy-start.12 = (f32[256]{0:T(256)S(1)}, f32[256]{0:T(256)}, u32[]{:S(2)}) copy-start(f32[256]{0:T(256)} %param.23) | copy-start | bytes 3076
  50.1 1.4 %collective-permute-start.17 = (bf16[512,128]{1,0:T(8,128)(2,1)S(1)}, bf16[512,128]{1,0:T(8,128)(2,1)S(1)}, u32[]{:S(2)}, u32[]{:S(2)}) collective-permute-start(bf16[512,128]{1,0:T(8,128)(2,1)S(1)} %mirror_sums.3.mine), channel_id=1, source_target_pairs={{0,1},{1,0},{2,3},{3,2},{4,5},{5,4},{6,7},{7,6},{8,9},{9,8},{10,11... | collective-permute-start | bytes 393224 | tf_op jit(solution)/shard_map/ppermute | solution.py:40
  52.8 7.6 %collective-permute-start.18 = (bf16[128,256]{1,0:T(8,128)(2,1)S(1)}, bf16[128,256]{1,0:T(8,128)(2,1)S(1)}, u32[]{:S(2)}, u32[]{:S(2)}) collective-permute-start(bf16[128,256]{1,0:T(8,128)(2,1)S(1)} %get-tuple-element.124), channel_id=1, source_target_pairs={{0,2},{2,0},{4,6},{6,4},{8,10},{10,8},{12,14},{14,12},{1,3},{3,1},... | collective-permute-start | bytes 196616 | tf_op jit(solution)/shard_map/ppermute | solution.py:44
  54.3 10.5 %collective-permute-start.19 = (bf16[128,256]{1,0:T(8,128)(2,1)S(1)}, bf16[128,256]{1,0:T(8,128)(2,1)S(1)}, u32[]{:S(2)}, u32[]{:S(2)}) collective-permute-start(bf16[128,256]{1,0:T(8,128)(2,1)S(1)} %get-tuple-element.125), channel_id=1, source_target_pairs={{0,4},{2,6},{4,0},{6,2},{8,12},{10,14},{12,8},{14,10},{1,5},{3,7},... | collective-permute-start | bytes 196616 | tf_op jit(solution)/shard_map/ppermute | solution.py:44
  54.3 12.6 %collective-permute-start.20 = (bf16[128,256]{1,0:T(8,128)(2,1)S(1)}, bf16[128,256]{1,0:T(8,128)(2,1)S(1)}, u32[]{:S(2)}, u32[]{:S(2)}) collective-permute-start(bf16[128,256]{1,0:T(8,128)(2,1)S(1)} %get-tuple-element.126), channel_id=1, source_target_pairs={{0,6},{2,4},{4,2},{6,0},{8,14},{10,12},{12,10},{14,8},{1,7},{3,5},... | collective-permute-start | bytes 196616 | tf_op jit(solution)/shard_map/ppermute | solution.py:44
  56.3 10.6 %collective-permute-start.21 = (bf16[128,256]{1,0:T(8,128)(2,1)S(1)}, bf16[128,256]{1,0:T(8,128)(2,1)S(1)}, u32[]{:S(2)}, u32[]{:S(2)}) collective-permute-start(bf16[128,256]{1,0:T(8,128)(2,1)S(1)} %get-tuple-element.127), channel_id=1, source_target_pairs={{0,8},{2,10},{4,12},{6,14},{8,0},{10,2},{12,4},{14,6},{1,9},{3,11}... | collective-permute-start | bytes 196616 | tf_op jit(solution)/shard_map/ppermute | solution.py:44
  59.5 10.4 %collective-permute-start.22 = (bf16[128,256]{1,0:T(8,128)(2,1)S(1)}, bf16[128,256]{1,0:T(8,128)(2,1)S(1)}, u32[]{:S(2)}, u32[]{:S(2)}) collective-permute-start(bf16[128,256]{1,0:T(8,128)(2,1)S(1)} %get-tuple-element.128), channel_id=1, source_target_pairs={{0,10},{2,8},{4,14},{6,12},{8,2},{10,0},{12,6},{14,4},{1,11},{3,9}... | collective-permute-start | bytes 196616 | tf_op jit(solution)/shard_map/ppermute | solution.py:44
  60.4 9.5 %collective-permute-start.23 = (bf16[128,256]{1,0:T(8,128)(2,1)S(1)}, bf16[128,256]{1,0:T(8,128)(2,1)S(1)}, u32[]{:S(2)}, u32[]{:S(2)}) collective-permute-start(bf16[128,256]{1,0:T(8,128)(2,1)S(1)} %get-tuple-element.129), channel_id=1, source_target_pairs={{0,12},{2,14},{4,8},{6,10},{8,4},{10,6},{12,0},{14,2},{1,13},{3,15... | collective-permute-start | bytes 196616 | tf_op jit(solution)/shard_map/ppermute | solution.py:44
  64.8 7.1 %collective-permute-start.24 = (bf16[128,256]{1,0:T(8,128)(2,1)S(1)}, bf16[128,256]{1,0:T(8,128)(2,1)S(1)}, u32[]{:S(2)}, u32[]{:S(2)}) collective-permute-start(bf16[128,256]{1,0:T(8,128)(2,1)S(1)} %get-tuple-element.130), channel_id=1, source_target_pairs={{0,14},{2,12},{4,10},{6,8},{8,6},{10,4},{12,2},{14,0},{1,15},{3,13... | collective-permute-start | bytes 196616 | tf_op jit(solution)/shard_map/ppermute | solution.py:44
  71.9 2.4 %copy-start.4 = (bf16[512,256]{1,0:T(8,128)(2,1)S(1)}, bf16[512,256]{1,0:T(8,128)(2,1)}, u32[]{:S(2)}) copy-start(bf16[512,256]{1,0:T(8,128)(2,1)} %get-tuple-element.65.encoded) | copy-start | bytes 786436
  74.1 1.6 %collective-permute-start.25 = (bf16[512,256]{1,0:T(8,128)(2,1)S(1)}, bf16[512,256]{1,0:T(8,128)(2,1)S(1)}, u32[]{:S(2)}, u32[]{:S(2)}) collective-permute-start(bf16[512,256]{1,0:T(8,128)(2,1)S(1)} %edge_sums.1.mine), channel_id=1, source_target_pairs={{0,1},{1,0},{2,3},{3,2},{4,5},{5,4},{6,7},{7,6},{8,9},{9,8},{10,11... | collective-permute-start | bytes 786440 | tf_op jit(solution)/shard_map/ppermute | solution.py:40

commit v4 on v3

--- a/solution.py
+++ b/solution.py
@@ -10,6 +10,7 @@
 BF16, F32, I32 = jnp.bfloat16, jnp.float32, jnp.int32
 LANES = 128
 STEP = 256
+DIGIT = 64
 MIB = 24
 SMEM = pl.BlockSpec(memory_space=pltpu.SMEM)
 VMEM = pl.BlockSpec(memory_space=pltpu.VMEM)
@@ -77,10 +78,11 @@
         copy.wait()
 
 
-def own_features_kernel(feat, grid, mesh, w_send, w_recv, grid_part, mesh_part, send_rest, recv_rest, *scratch):
-    ws, g, wr, m, sems = scratch
+def own_features_kernel(feat, grid, mesh, w_send, w_recv, send, grid_part, mesh_part, send_rest, recv_rest, list_out, *scratch):
+    ws, g, wr, m, ids, sems = scratch
     first = start_copies(w_send, ws, sems, 0, 4) + start_copies(grid, g, sems, 4, 4)
     second = start_copies(w_recv, wr, sems, 8, 4) + start_copies(mesh, m, sems, 12, 4)
+    second += start_copies(send, ids, sems, 16, 1)
     own, other = halves_of(feat[0], g.shape[1])
     wait_copies(first)
     grid_part[...] = dot(g[...], ws[own, :])
@@ -88,6 +90,8 @@
     wait_copies(second)
     mesh_part[...] = dot(m[...], wr[own, :])
     recv_rest[...] = wr[other, :]
+    rows = jnp.concatenate([ids[:, a : a + LANES] for a in range(0, ids.shape[1], LANES)], axis=0)
+    list_out[...] = jnp.concatenate([rows // DIGIT, rows % DIGIT], axis=0).astype(F32).astype(BF16)
 
 
 def other_features_kernel(part, rest, other, *outs):
@@ -97,7 +101,14 @@
         out[...] = (part[:, lanes] + dot(other[...], rest[:, lanes])).astype(BF16)
 
 
-def project(grid, mesh, w_send, w_recv, n_chunks):
+def with_list_kernel(part, rest, other, digits, *outs):
+    *chunks, first = outs
+    other_features_kernel(part, rest, other, *chunks)
+    first[: part.shape[0], :] = chunks[0][...]
+    first[part.shape[0] :, :] = digits[...]
+
+
+def project(grid, mesh, w_send, w_recv, send, n_chunks):
     grid_other, mesh_other = swap(grid), swap(mesh)
     hidden, feats = w_send.shape[1], grid.shape[1]
     parts = call(
@@ -107,19 +118,31 @@
             shape_of((mesh.shape[0], hidden), F32),
             shape_of((feats, hidden), BF16),
             shape_of((feats, hidden), BF16),
+            shape_of((2 * send.shape[1] // LANES, LANES), BF16),
         ],
         position("feat"),
-        *[pltpu.with_memory_space_constraint(x, pltpu.HBM) for x in (grid, mesh, w_send, w_recv)],
-        specs=[SMEM] + [HBM] * 4,
-        scratch=[pltpu.VMEM(x.shape, BF16) for x in (w_send, grid, w_recv, mesh)] + [pltpu.SemaphoreType.DMA((16,))],
+        *[pltpu.with_memory_space_constraint(x, pltpu.HBM) for x in (grid, mesh, w_send, w_recv, send)],
+        specs=[SMEM] + [HBM] * 5,
+        scratch=[pltpu.VMEM(x.shape, x.dtype) for x in (w_send, grid, w_recv, mesh, send)]
+        + [pltpu.SemaphoreType.DMA((17,))],
         name="own_features",
         mib=16,
     )
-    grid_part, mesh_part, send_rest, recv_rest = parts
+    grid_part, mesh_part, send_rest, recv_rest, digits = parts
     chunk = shape_of((grid.shape[0], hidden // n_chunks), BF16)
-    chunks = call(
-        other_features_kernel, [chunk] * n_chunks, grid_part, send_rest, grid_other, name="other_grid_features"
-    )
+    if n_chunks > 1:
+        first = shape_of((grid.shape[0] + digits.shape[0], chunk.shape[1]), BF16)
+        chunks = call(
+            with_list_kernel,
+            [chunk] * n_chunks + [first],
+            grid_part,
+            send_rest,
+            grid_other,
+            digits,
+            name="other_grid_features",
+        )
+    else:
+        chunks = call(other_features_kernel, [chunk], grid_part, send_rest, grid_other, name="other_grid_features")
     chunks, mesh_part = lax.optimization_barrier((chunks, mesh_part))
     (mesh_proj,) = call(
         other_features_kernel,
@@ -154,16 +177,35 @@
             out[at : at + LANES, width:] = dot(hot, g1[...]).astype(BF16)
 
 
-def prepare_kernel(half, me, send_mirror, recv, mesh_proj, bias, pick, into, term):
-    cap = pick.shape[0] // half
+def prepare_kernel(half, me, recv, mesh_proj, bias, into, term):
+    cap = term.shape[0] // half
     for k in range(half):
-        ids, rows = slots_of(send_mirror, me[0] ^ k, cap), slots_of(recv, me[0] ^ k ^ half, cap)
+        rows = slots_of(recv, me[0] ^ k ^ half, cap)
         first = k * cap
         into[:, first : first + cap] = (iota((into.shape[0], cap), 0) == rows).astype(BF16)
         for at in range(0, cap, LANES):
             here = slice(first + at, first + at + LANES)
-            pick[here, :] = one_hot_rows(ids, pick.shape[1], at)
             term[here, :] = dot(one_hot_rows(rows, mesh_proj.shape[0], at), mesh_proj[...]) + bias[...]
+
+
+def aside_kernel(half, cap, blocks, me, send, recv, g0, g1, mesh_proj, bias, halo_rows, src, dst, *outs):
+    packed, sums, into, term, *selections = outs
+    pack_own_kernel((1,), me, send, g0, g1, packed)
+    local_sums_kernel(cap, me, send, recv, g0, g1, mesh_proj, bias, sums)
+    prepare_kernel(half, me, recv, mesh_proj, bias, into, term)
+    select_kernel(blocks, me, halo_rows, src, dst, *selections)
+
+
+def pick_kernel(half, me, mirrored, pick, ids):
+    cap, grid_rows = pick.shape[0] // half, pick.shape[1]
+    lines = ids.shape[0]
+    digits = mirrored[grid_rows:, :].astype(F32).astype(I32)
+    ids[...] = digits[:lines, :] * DIGIT + digits[lines:, :]
+    for k in range(half):
+        for n in range(cap // LANES):
+            row = ids[pl.ds((me[0] ^ k) * (cap // LANES) + n, 1), :]
+            first = k * cap + n * LANES
+            pick[first : first + LANES, :] = one_hot_rows(row, grid_rows, 0)
 
 
 def add_slots(total, grid, rows, mesh_proj, bias):
@@ -182,6 +224,7 @@
 
 def arrived_sums_kernel(cap, me, recv, mesh_proj, bias, start, *refs):
     *blocks, out = refs
+    blocks.reverse()
     total = start[...]
     for k, block in enumerate(blocks, 1):
         total = add_slots(total, block[...].astype(F32), slots_of(recv, me[0] ^ k, cap), mesh_proj, bias)
@@ -191,7 +234,7 @@
 def pack_mirror_kernel(pick, mirrored, *outs):
     cap = outs[0].shape[0]
     for k, out in enumerate(outs, 1):
-        out[...] = dot(pick[k * cap : (k + 1) * cap, :], mirrored[...]).astype(BF16)
+        out[...] = dot(pick[k * cap : (k + 1) * cap, :], mirrored[: pick.shape[1], :]).astype(BF16)
 
 
 def mirror_sums_kernel(chunk, first, pick, mirrored, into, term, total, *refs):
@@ -200,9 +243,10 @@
     lanes = slice(chunk * width, (chunk + 1) * width)
     cap = into.shape[1] // 4
     if first:
-        blocks = [dot(pick[:cap, :], mirrored[...])]
+        blocks = [dot(pick[:cap, :], mirrored[: pick.shape[1], :])]
         sums = total[:, lanes]
     else:
+        blocks.reverse()
         sums = total[...]
     for k, block in enumerate(blocks, 0 if first else 1):
         rows = slice(k * cap, (k + 1) * cap)
@@ -214,6 +258,7 @@
 def sums_by_halves(grid_chunks, mesh_rproj, bias, send_grid, recv_row, n_dom, select, lists):
     half = n_dom // 2
     mesh_rows, hidden = mesh_rproj.shape
+    *grid_chunks, with_list = grid_chunks
     grid_rows, width = grid_chunks[0].shape
     cap = send_grid.shape[1] // n_dom
     me, bias = position("dom"), bias[None, :]
@@ -231,44 +276,42 @@
         return blocks
 
     packed = pack_own(3, 2)
-    packed, first = lax.optimization_barrier((packed, grid_chunks[0]))
+    packed, with_list, grid_chunks = lax.optimization_barrier((packed, with_list, grid_chunks))
     arrived = {k: from_xor(block, k, n_dom) for k, block in zip((3, 2), packed)}
-    mirrored = [from_xor(first, half, n_dom)]
-    send_mirror = from_xor(send_grid, half, n_dom)
-    own = call(
-        functools.partial(local_sums_kernel, cap),
-        shape_of((mesh_rows, hidden), F32),
+    mirrored = [from_xor(with_list, half, n_dom)]
+    selection_shapes, blocks = select
+    packed, own, into, term, *selections = call(
+        functools.partial(aside_kernel, half, cap, blocks),
+        [
+            shape_of((cap, hidden), BF16),
+            shape_of((mesh_rows, hidden), F32),
+            shape_of((mesh_rows, half * cap), BF16),
+            shape_of((half * cap, hidden), F32),
+            *selection_shapes,
+        ],
         me,
         send_grid,
         recv_row,
         *grid_chunks,
         mesh_rproj,
         bias,
-        specs=[SMEM] + [VMEM] * 6,
-        name="local_sums",
-    )
-    own, packed, lists = lax.optimization_barrier((own, pack_own(1), lists))
-    arrived[1] = from_xor(packed[0], 1, n_dom)
-    selections = select(me, *lists)
-    send_mirror, later, selections = lax.optimization_barrier((send_mirror, grid_chunks[1], selections))
-    mirrored.append(from_xor(later, half, n_dom))
+        *lists,
+        specs=[SMEM] + [VMEM] * (6 + len(lists)),
+        name="aside",
+    )
+    arrived[1] = from_xor(packed, 1, n_dom)
     arrived = [arrived[k] for k in range(1, half)]
-    pick, into, term = call(
-        functools.partial(prepare_kernel, half),
-        [
-            shape_of((half * cap, grid_rows), BF16),
-            shape_of((mesh_rows, half * cap), BF16),
-            shape_of((half * cap, hidden), F32),
-        ],
+    mirrored.append(from_xor(grid_chunks[1], half, n_dom))
+    own, into, term, selections, mirrored[0] = lax.optimization_barrier((own, into, term, selections, mirrored[0]))
+    pick = call(
+        functools.partial(pick_kernel, half),
+        shape_of((half * cap, grid_rows), BF16),
         me,
-        send_mirror,
-        recv_row,
-        mesh_rproj,
-        bias,
-        specs=[SMEM] + [VMEM] * 4,
-        name="prepare",
-    )
-    arrived, mirrored[1] = lax.optimization_barrier((arrived, mirrored[1]))
+        mirrored[0],
+        specs=[SMEM, VMEM],
+        scratch=[pltpu.VMEM((send_grid.shape[1] // LANES, LANES), I32)],
+        name="pick",
+    )
     own = call(
         functools.partial(arrived_sums_kernel, cap),
         shape_of((mesh_rows, hidden), F32),
@@ -277,7 +320,7 @@
         mesh_rproj,
         bias,
         own,
-        *arrived,
+        *arrived[::-1],
         specs=[SMEM] + [VMEM] * (4 + len(arrived)),
         name="arrived_sums",
     )
@@ -306,7 +349,7 @@
                 into,
                 term,
                 total,
-                *blocks,
+                *blocks[::-1],
                 name="mirror_sums",
             )
         )
@@ -322,7 +365,16 @@
     arrived = lax.all_to_all(packed, "dom", split_axis=0, concat_axis=0, tiled=True)
     hidden = silu_bf16(arrived.astype(F32) + rows_of(mesh_rproj, recv_row) + bias[None, :])
     into = iota((mesh_rproj.shape[0], recv_row.shape[1]), 0) == recv_row
-    return [dot(into.astype(BF16), hidden).astype(BF16)], select(position("dom"), *lists)
+    selection_shapes, blocks = select
+    selections = call(
+        functools.partial(select_kernel, blocks),
+        selection_shapes,
+        position("dom"),
+        *lists,
+        specs=[SMEM] + [VMEM] * len(lists),
+        name="select",
+    )
+    return [dot(into.astype(BF16), hidden).astype(BF16)], selections
 
 
 def list_rows(ref, me, k, blocks):
@@ -385,6 +437,7 @@
 
 def edge_sums_kernel(near, far_pick, into, *refs):
     *halo, out, table = refs
+    halo.reverse()
     size = halo[0].shape[0]
     for k, block in enumerate(halo):
         table[k * size : (k + 1) * size, :] = block[...]
@@ -425,31 +478,25 @@
     mesh_rows, feats = mesh_lat.shape
     hidden = w_grid_send.shape[1]
     halves = n_dom == 8
-    grid_chunks, mesh_rproj, mesh_other = project(grid_lat, mesh_lat, w_grid_send, w_grid_recv, 2 if halves else 1)
+    grid_chunks, mesh_rproj, mesh_other = project(
+        grid_lat, mesh_lat, w_grid_send, w_grid_recv, send_grid, 2 if halves else 1
+    )
     grid_chunks, mesh_rproj, send_grid, recv_row, w_other, w2_other = lax.optimization_barrier(
         (grid_chunks, mesh_rproj, send_grid, recv_row, swap(w_grid_out), swap(w_edge_out))
     )
     me, feat = position("dom"), position("feat")
     blocks = n_dom if halves else 1
     n_halo, edges = halo_rows.shape[1], edge_src.shape[0] * edge_src.shape[1]
-    def select(me, halo_rows, src, dst):
-        return call(
-            functools.partial(select_kernel, blocks),
-            [
-                shape_of((n_halo, mesh_rows), BF16),
-                shape_of((edges, mesh_rows), BF16),
-                shape_of((edges, mesh_rows), BF16),
-                shape_of((edges, n_halo), BF16),
-                shape_of((mesh_rows, edges), BF16),
-            ],
-            me,
-            halo_rows,
-            src,
-            dst,
-            specs=[SMEM] + [VMEM] * 3,
-            name="select",
-        )
-
+    select = (
+        [
+            shape_of((n_halo, mesh_rows), BF16),
+            shape_of((edges, mesh_rows), BF16),
+            shape_of((edges, mesh_rows), BF16),
+            shape_of((edges, n_halo), BF16),
+            shape_of((mesh_rows, edges), BF16),
+        ],
+        blocks,
+    )
     sums = sums_by_halves if halves else sums_by_all_to_all
     lists = (halo_rows, edge_src, edge_dst)
     chunks, selections = sums(grid_chunks, mesh_rproj, g2m_bias, send_grid, recv_row, n_dom, select, lists)
@@ -507,7 +554,7 @@
         near,
         far_src,
         into,
-        *halo,
+        *halo[::-1],
         scratch=[pltpu.VMEM((n_halo, hidden), BF16)],
         name="edge_sums",
     )

time: 76.8 us -> 71.4 us (0.930)
  Pallas kernels: 27.1 us -> 25.1 us
  starting transfers between devices: 30.5 us -> 28.6 us
  waiting for transfers between devices: 17.9 us -> 16.5 us
    ppermute x19 -> x18, starting transfers between devices: 29.2 us -> 26.8 us  [from_xor(): return lax.ppermute(x, 'dom', [(i, i ^ bits) for i in range(n_dom)])]
    pallas_call x21 -> x19, Pallas kernels: 27.1 us -> 25.1 us  [call(): pl.pallas_call(kernel, out_shape=out_shape, in_specs=[VMEM] * len(args) i...]
    ppermute x19 -> x18, waiting for transfers between devices: 15.8 us -> 14.7 us  [from_xor(): return lax.ppermute(x, 'dom', [(i, i ^ bits) for i in range(n_dom)])]
  transfers between devices with their start and end apart: 26 -> 25, of which waited for: 7 -> 9; matrix products, arithmetic and copies ran while one was open for 0% -> 0% of each run, Pallas kernels for 28% -> 27%
where the time goes in v4:
time: 71.4 us; the launch traced here: 71.2 us
  starting transfers between devices  28.6 us (40%)
  Pallas kernels  25.1 us (35%)
  waiting for transfers between devices  16.5 us (23%)
  between operations  0.96 us (1%)
    ppermute x18, starting transfers between devices, from_xor(): return lax.ppermute(x, 'dom', [(i, i ^ bits) for i in range(n_dom)])  26.8 us
    pallas_call x19, Pallas kernels, call(): pl.pallas_call(kernel, out_shape=out_shape, in_specs=[VMEM] * len(args) i...  25.1 us
    ppermute x18, waiting for transfers between devices, from_xor(): return lax.ppermute(x, 'dom', [(i, i ^ bits) for i in range(n_dom)])  14.7 us
    ppermute x7, waiting for transfers between devices, swap(): return lax.ppermute(x, 'feat', [(0, 1), (1, 0)])  1.83 us
    ppermute x7, starting transfers between devices, swap(): return lax.ppermute(x, 'feat', [(0, 1), (1, 0)])  1.79 us
  transfers between devices with their start and end apart: 25, of which 9 were waited for; matrix products, arithmetic and copies ran while one was open for 0% of the time, Pallas kernels for 27%

profile of v4, /device:TPU:0, one launch (start us, length us, event | category | flops | bytes accessed | tf_op | source)
XLA Modules:
  0.0 71.2 jit_solution(14862034230030100263)
XLA Ops:
  0.6 0.5 collective-permute-start
  1.2 0.4 collective-permute-start.3
  1.8 2.1 %own_features.1 = (f32[1024,256]{1,0:T(8,128)S(1)}, f32[512,256]{1,0:T(8,128)S(1)}, bf16[256,256]{1,0:T(8,128)(2,1)S(1)}, bf16[256,256]{1,0:T(8,128)(2,1)S(1)}, bf16[64,128]{1,0:T(8,128)(2,1)S(1)}) custom-call(s32[1]{0:T(128)} %bitcast.feat, bf16[1024,256]{1,0:T(8,128)(2,1)} %grid.1, bf16[512,256]{1,0:T(8,128)(2,1)} %refs_2_.1, bf16[512,256]{1,0:T(8,128)(2,1)} %w_send.2, ...), custom_call_target="tpu_custom_call" | custom-call | tf_op jit(solution)/shard_map/own_features/pallas_call | solution.py:49
  3.9 0.5 other_grid_features.1
  4.4 0.2 other_mesh_features.1.mesh_proj
  4.7 1.5 %pack_own.1 = (bf16[512,256]{1,0:T(8,128)(2,1)S(1)}, bf16[512,256]{1,0:T(8,128)(2,1)S(1)}) custom-call(s32[1]{0:T(128)} %bitcast.1.me, s32[1,4096]{1,0:T(1,128)S(1)} %copy-done.6, bf16[1024,128]{1,0:T(8,128)(2,1)S(1)} %get-tuple-element.86.g0, bf16[1024,128]{1,0:T(8,128)(2,1)S(1)} %get-tuple-element.87.g1), custom_call_target="tpu_custom_call" | custom-call | tf_op jit(solution)/shard_map/pack_own/pallas_call | solution.py:49
  6.2 4.1 %collective-permute-start.4 = (bf16[1088,128]{1,0:T(8,128)(2,1)S(1)}, bf16[1088,128]{1,0:T(8,128)(2,1)S(1)}, u32[]{:S(2)}, u32[]{:S(2)}) collective-permute-start(bf16[1088,128]{1,0:T(8,128)(2,1)S(1)} %get-tuple-element.97), channel_id=1, source_target_pairs={{0,8},{2,10},{4,12},{6,14},{8,0},{10,2},{12,4},{14,6},{1,9},{3,11}... | collective-permute-start | bytes 835592 | tf_op jit(solution)/shard_map/ppermute | solution.py:45
  10.2 2.5 %collective-permute-start.5 = (bf16[512,256]{1,0:T(8,128)(2,1)S(1)}, bf16[512,256]{1,0:T(8,128)(2,1)S(1)}, u32[]{:S(2)}, u32[]{:S(2)}) collective-permute-start(bf16[512,256]{1,0:T(8,128)(2,1)S(1)} %get-tuple-element.102), channel_id=1, source_target_pairs={{0,6},{2,4},{4,2},{6,0},{8,14},{10,12},{12,10},{14,8},{1,7},{3,5},... | collective-permute-start | bytes 786440 | tf_op jit(solution)/shard_map/ppermute | solution.py:45
  12.8 0.4 collective-permute-start.6
  13.2 0.3 collective-permute-start.12
  13.6 5.4 %aside.1 = (bf16[512,256]{1,0:T(8,128)(2,1)S(1)}, f32[512,256]{1,0:T(8,128)S(1)}, bf16[512,2048]{1,0:T(8,128)(2,1)S(1)}, f32[2048,256]{1,0:T(8,128)S(1)}, bf16[1...) custom-call(s32[1]{0:T(128)} %bitcast.1.me, ...), custom_call_target="tpu_custom_call" | custom-call | tf_op jit(solution)/shard_map/aside/pallas_call | solution.py:49
  19.0 0.3 collective-permute-start.7
  19.3 4.4 %collective-permute-done.4.mirrored = bf16[1088,128]{1,0:T(8,128)(2,1)S(1)} collective-permute-done((bf16[1088,128]{1,0:T(8,128)(2,1)S(1)}, bf16[1088,128]{1,0:T(8,128)(2,1)S(1)}, u32[]{:S(2)}, u32[]{:S(2)}) %collective-permute-start.4) | collective-permute-done | bytes 278560 | tf_op jit(solution)/shard_map/ppermute | solution.py:45
  23.8 1.0 %pick.1 = bf16[2048,1024]{1,0:T(8,128)(2,1)S(1)} custom-call(s32[1]{0:T(128)} %bitcast.1.me, bf16[1088,128]{1,0:T(8,128)(2,1)S(1)} %collective-permute-done.4.mirrored), custom_call_target="tpu_custom_call" | custom-call | tf_op jit(solution)/shard_map/pick/pallas_call | solution.py:49
  24.8 1.0 %pack_mirror.2 = (bf16[512,128]{1,0:T(8,128)(2,1)S(1)}, bf16[512,128]{1,0:T(8,128)(2,1)S(1)}, bf16[512,128]{1,0:T(8,128)(2,1)S(1)}) custom-call(bf16[2048,1024]{1,0:T(8,128)(2,1)S(1)} %pick.1, bf16[1088,128]{1,0:T(8,128)(2,1)S(1)} %collective-permute-done.4.mirrored), custom_call_target="tpu_custom_call" | custom-call | tf_op jit(solution)/shard_map/pack_mirror/pallas_call | solution.py:49
  25.8 1.2 %collective-permute-start.8 = (bf16[512,128]{1,0:T(8,128)(2,1)S(1)}, bf16[512,128]{1,0:T(8,128)(2,1)S(1)}, u32[]{:S(2)}, u32[]{:S(2)}) collective-permute-start(bf16[512,128]{1,0:T(8,128)(2,1)S(1)} %get-tuple-element.105), channel_id=1, source_target_pairs={{0,6},{2,4},{4,2},{6,0},{8,14},{10,12},{12,10},{14,8},{1,7},{3,5},... | collective-permute-start | bytes 393224 | tf_op jit(solution)/shard_map/ppermute | solution.py:45
  27.0 7.3 %collective-permute-done.12.mirrored = bf16[1024,128]{1,0:T(8,128)(2,1)S(1)} collective-permute-done((bf16[1024,128]{1,0:T(8,128)(2,1)S(1)}, bf16[1024,128]{1,0:T(8,128)(2,1)S(1)}, u32[]{:S(2)}, u32[]{:S(2)}) %collective-permute-start.12) | collective-permute-done | bytes 262176 | tf_op jit(solution)/shard_map/ppermute | solution.py:45
  34.3 1.0 %pack_mirror.3 = (bf16[512,128]{1,0:T(8,128)(2,1)S(1)}, bf16[512,128]{1,0:T(8,128)(2,1)S(1)}, bf16[512,128]{1,0:T(8,128)(2,1)S(1)}) custom-call(bf16[2048,1024]{1,0:T(8,128)(2,1)S(1)} %pick.1, bf16[1024,128]{1,0:T(8,128)(2,1)S(1)} %collective-permute-done.12.mirrored), custom_call_target="tpu_custom_call" | custom-call | tf_op jit(solution)/shard_map/pack_mirror/pallas_call | solution.py:49
  35.2 3.3 %collective-permute-start.13 = (bf16[512,128]{1,0:T(8,128)(2,1)S(1)}, bf16[512,128]{1,0:T(8,128)(2,1)S(1)}, u32[]{:S(2)}, u32[]{:S(2)}) collective-permute-start(bf16[512,128]{1,0:T(8,128)(2,1)S(1)} %get-tuple-element.111), channel_id=1, source_target_pairs={{0,6},{2,4},{4,2},{6,0},{8,14},{10,12},{12,10},{14,8},{1,7},{3,5},... | collective-permute-start | bytes 393224 | tf_op jit(solution)/shard_map/ppermute | solution.py:45
  38.5 0.6 collective-permute-start.10
  39.2 1.9 %collective-permute-start.14 = (bf16[512,128]{1,0:T(8,128)(2,1)S(1)}, bf16[512,128]{1,0:T(8,128)(2,1)S(1)}, u32[]{:S(2)}, u32[]{:S(2)}) collective-permute-start(bf16[512,128]{1,0:T(8,128)(2,1)S(1)} %get-tuple-element.112), channel_id=1, source_target_pairs={{0,4},{2,6},{4,0},{6,2},{8,12},{10,14},{12,8},{14,10},{1,5},{3,7},... | collective-permute-start | bytes 393224 | tf_op jit(solution)/shard_map/ppermute | solution.py:45
  41.1 1.5 %collective-permute-start.15 = (bf16[512,128]{1,0:T(8,128)(2,1)S(1)}, bf16[512,128]{1,0:T(8,128)(2,1)S(1)}, u32[]{:S(2)}, u32[]{:S(2)}) collective-permute-start(bf16[512,128]{1,0:T(8,128)(2,1)S(1)} %get-tuple-element.113), channel_id=1, source_target_pairs={{0,2},{2,0},{4,6},{6,4},{8,10},{10,8},{12,14},{14,12},{1,3},{3,1},... | collective-permute-start | bytes 393224 | tf_op jit(solution)/shard_map/ppermute | solution.py:45
  42.6 2.1 %arrived_sums.1.total = f32[512,256]{1,0:T(8,128)S(1)} custom-call(s32[1]{0:T(128)} %bitcast.1.me, s32[1,4096]{1,0:T(1,128)S(1)} %copy-done.7, bf16[512,256]{1,0:T(8,128)(2,1)S(1)} %other_mesh_features.1.mesh_proj, f32[1,256]{1,0:T(1,128)S(1)} %bitcast.5, f32[512,256]{1,0:T(8,128)S(1)} %get-tuple-element.101.start, ...), custom_call_target="tpu_custom_call" | custom-call | tf_op jit(solution)/shard_map/arrived_sums/pallas_call | solution.py:49
  44.7 0.9 %own_mirror_sums.2.total = f32[512,128]{1,0:T(8,128)S(1)} custom-call(bf16[2048,1024]{1,0:T(8,128)(2,1)S(1)} %pick.1, bf16[1088,128]{1,0:T(8,128)(2,1)S(1)} %collective-permute-done.4.mirrored, bf16[512,2048]{1,0:T(8,128)(2,1)S(1)} %get-tuple-element.99.into, f32[2048,256]{1,0:T(8,128)S(1)} %get-tuple-element.100.term, f32[512,256]{1,0:T(8,128)S(1)} %arrived_sums.1.total), custom_call_target="tpu_custom_call" | custom-call | tf_op jit(solution)/shard_map/own_mirror_sums/pallas_call | solution.py:49
  45.6 0.9 %own_mirror_sums.3.total = f32[512,128]{1,0:T(8,128)S(1)} custom-call(bf16[2048,1024]{1,0:T(8,128)(2,1)S(1)} %pick.1, bf16[1024,128]{1,0:T(8,128)(2,1)S(1)} %collective-permute-done.12.mirrored, bf16[512,2048]{1,0:T(8,128)(2,1)S(1)} %get-tuple-element.99.into, f32[2048,256]{1,0:T(8,128)S(1)} %get-tuple-element.100.term, f32[512,256]{1,0:T(8,128)S(1)} %arrived_sums.1.total), custom_call_target="tpu_custom_call" | custom-call | tf_op jit(solution)/shard_map/own_mirror_sums/pallas_call | solution.py:49
  46.5 0.6 mirror_sums.2.refs_0_
  47.3 0.6 mirror_sums.3.mine
  48.0 0.5 collective-permute-start.16
  48.5 0.1 collective-permute-done.11.refs_1_
  48.6 0.4 encode_base.1
  49.0 0.5 collective-permute-done.16.other
  49.5 1.2 %encode.1 = (bf16[512,512]{1,0:T(8,128)(2,1)S(1)}, bf16[512,256]{1,0:T(8,128)(2,1)S(1)}, bf16[128,256]{1,0:T(8,128)(2,1)S(1)}, bf16[128,256]{1,0:T(8,128)(2,1)S(...) custom-call(f32[512,512]{1,0:T(8,128)S(1)} %get-tuple-element.110.ba, ...), custom_call_target="tpu_custom_call" | custom-call | tf_op jit(solution)/shard_map/encode/pallas_call | solution.py:49
  50.7 3.8 %collective-permute-start.17 = (bf16[128,256]{1,0:T(8,128)(2,1)S(1)}, bf16[128,256]{1,0:T(8,128)(2,1)S(1)}, u32[]{:S(2)}, u32[]{:S(2)}) collective-permute-start(bf16[128,256]{1,0:T(8,128)(2,1)S(1)} %get-tuple-element.123), channel_id=1, source_target_pairs={{0,14},{2,12},{4,10},{6,8},{8,6},{10,4},{12,2},{14,0},{1,15},{3,13... | collective-permute-start | bytes 196616 | tf_op jit(solution)/shard_map/ppermute | solution.py:45
  54.5 0.1 collective-permute-start.18
  54.6 0.9 %collective-permute-start.19 = (bf16[128,256]{1,0:T(8,128)(2,1)S(1)}, bf16[128,256]{1,0:T(8,128)(2,1)S(1)}, u32[]{:S(2)}, u32[]{:S(2)}) collective-permute-start(bf16[128,256]{1,0:T(8,128)(2,1)S(1)} %get-tuple-element.125), channel_id=1, source_target_pairs={{0,10},{2,8},{4,14},{6,12},{8,2},{10,0},{12,6},{14,4},{1,11},{3,9}... | collective-permute-start | bytes 196616 | tf_op jit(solution)/shard_map/ppermute | solution.py:45
  55.5 3.0 %collective-permute-start.20 = (bf16[128,256]{1,0:T(8,128)(2,1)S(1)}, bf16[128,256]{1,0:T(8,128)(2,1)S(1)}, u32[]{:S(2)}, u32[]{:S(2)}) collective-permute-start(bf16[128,256]{1,0:T(8,128)(2,1)S(1)} %get-tuple-element.126), channel_id=1, source_target_pairs={{0,8},{2,10},{4,12},{6,14},{8,0},{10,2},{12,4},{14,6},{1,9},{3,11}... | collective-permute-start | bytes 196616 | tf_op jit(solution)/shard_map/ppermute | solution.py:45
  58.5 1.4 %collective-permute-start.21 = (bf16[128,256]{1,0:T(8,128)(2,1)S(1)}, bf16[128,256]{1,0:T(8,128)(2,1)S(1)}, u32[]{:S(2)}, u32[]{:S(2)}) collective-permute-start(bf16[128,256]{1,0:T(8,128)(2,1)S(1)} %get-tuple-element.127), channel_id=1, source_target_pairs={{0,6},{2,4},{4,2},{6,0},{8,14},{10,12},{12,10},{14,8},{1,7},{3,5},... | collective-permute-start | bytes 196616 | tf_op jit(solution)/shard_map/ppermute | solution.py:45
  59.8 0.6 collective-permute-start.22
  60.4 0.6 collective-permute-done.18.refs_1_
  61.1 0.9 %collective-permute-start.23 = (bf16[128,256]{1,0:T(8,128)(2,1)S(1)}, bf16[128,256]{1,0:T(8,128)(2,1)S(1)}, u32[]{:S(2)}, u32[]{:S(2)}) collective-permute-start(bf16[128,256]{1,0:T(8,128)(2,1)S(1)} %get-tuple-element.129), channel_id=1, source_target_pairs={{0,2},{2,0},{4,6},{6,4},{8,10},{10,8},{12,14},{14,12},{1,3},{3,1},... | collective-permute-start | bytes 196616 | tf_op jit(solution)/shard_map/ppermute | solution.py:45
  62.0 2.1 %near_edges.1 = (f32[2048,256]{1,0:T(8,128)S(1)}, bf16[512,256]{1,0:T(8,128)(2,1)}) custom-call(s32[1]{0:T(128)} %bitcast.feat, bf16[512,512]{1,0:T(8,128)(2,1)S(1)} %get-tuple-element.115.full, bf16[512,256]{1,0:T(8,128)(2,1)S(1)} %get-tuple-element.116.send_proj, bf16[512,256]{1,0:T(8,128)(2,1)S(1)} %copy-done.3, f32[1,256]{1,0:T(1,128)S(1)} %bitcast.6, ...), custom_call_target="tpu_custom_call" | custom-call | tf_op jit(solution)/shard_map/near_edges/pallas_call | solution.py:49
  64.1 1.8 %collective-permute-done.20.refs_3_ = bf16[128,256]{1,0:T(8,128)(2,1)S(1)} collective-permute-done((bf16[128,256]{1,0:T(8,128)(2,1)S(1)}, bf16[128,256]{1,0:T(8,128)(2,1)S(1)}, u32[]{:S(2)}, u32[]{:S(2)}) %collective-permute-start.20) | collective-permute-done | bytes 65568 | tf_op jit(solution)/shard_map/ppermute | solution.py:45
  65.8 0.1 collective-permute-done.21.refs_4_
  66.0 0.4 collective-permute-done.22.refs_5_
  66.4 2.3 %edge_sums.1.mine = bf16[512,256]{1,0:T(8,128)(2,1)S(1)} custom-call(f32[2048,256]{1,0:T(8,128)S(1)} %get-tuple-element.120.near, bf16[2048,1024]{1,0:T(8,128)(2,1)S(1)} %get-tuple-element.121.far_pick, bf16[512,2048]{1,0:T(8,128)(2,1)S(1)} %get-tuple-element.122.into, bf16[128,256]{1,0:T(8,128)(2,1)S(1)} %collective-permute-done.17.refs_0_, ...), custom_call_target="tpu_custom_call" | custom-call | tf_op jit(solution)/shard_map/edge_sums/pallas_call | solution.py:49
  68.8 0.2 own_output.1.part
  69.0 1.3 %collective-permute-done.24.other = bf16[512,256]{1,0:T(8,128)(2,1)S(1)} collective-permute-done((bf16[512,256]{1,0:T(8,128)(2,1)S(1)}, bf16[512,256]{1,0:T(8,128)(2,1)S(1)}, u32[]{:S(2)}, u32[]{:S(2)}) %collective-permute-start.24) | collective-permute-done | bytes 262176 | tf_op jit(solution)/shard_map/ppermute | solution.py:41
  70.3 0.9 %output.1 = bf16[512,256]{1,0:T(8,128)(2,1)} custom-call(f32[512,256]{1,0:T(8,128)S(1)} %own_output.1.part, bf16[512,256]{1,0:T(8,128)(2,1)S(1)} %collective-permute-done.24.other, bf16[512,256]{1,0:T(8,128)(2,1)S(1)} %get-tuple-element.131.w_out), custom_call_target="tpu_custom_call" | custom-call | tf_op jit(solution)/shard_map/output/pallas_call | solution.py:49
  (47 shorter events, 0.4 us)
Async XLA Ops:
  0.6 3.2 %collective-permute-start = (bf16[1024,256]{1,0:T(8,128)(2,1)}, bf16[1024,256]{1,0:T(8,128)(2,1)S(1)}, u32[]{:S(2)}, u32[]{:S(2)}) collective-permute-start(bf16[1024,256]{1,0:T(8,128)(2,1)} %grid.1), channel_id=1, source_target_pairs={{0,1},{1,0},{2,3},{3,2},{4,5},{5,4},{6,7},{7,6},{8,9},{9,8},{10,11... | collective-permute-start | bytes 1572872 | tf_op jit(solution)/shard_map/ppermute | solution.py:41
  1.2 3.3 %collective-permute-start.1 = (bf16[512,256]{1,0:T(8,128)(2,1)}, bf16[512,256]{1,0:T(8,128)(2,1)S(1)}, u32[]{:S(2)}, u32[]{:S(2)}) collective-permute-start(bf16[512,256]{1,0:T(8,128)(2,1)} %refs_2_.1), channel_id=1, source_target_pairs={{0,1},{1,0},{2,3},{3,2},{4,5},{5,4},{6,7},{7,6},{8,9},{9,8},{10,11... | collective-permute-start | bytes 786440 | tf_op jit(solution)/shard_map/ppermute | solution.py:41
  1.2 3.4 %collective-permute-start.3 = (bf16[256,512]{1,0:T(8,128)(2,1)}, bf16[256,512]{1,0:T(8,128)(2,1)S(1)}, u32[]{:S(2)}, u32[]{:S(2)}) collective-permute-start(bf16[256,512]{1,0:T(8,128)(2,1)} %refs_6_.1), channel_id=1, source_target_pairs={{0,1},{1,0},{2,3},{3,2},{4,5},{5,4},{6,7},{7,6},{8,9},{9,8},{10,11... | collective-permute-start | bytes 786440 | tf_op jit(solution)/shard_map/ppermute | solution.py:41
  1.7 3.0 %collective-permute-start.2 = (bf16[256,512]{1,0:T(8,128)(2,1)}, bf16[256,512]{1,0:T(8,128)(2,1)S(1)}, u32[]{:S(2)}, u32[]{:S(2)}) collective-permute-start(bf16[256,512]{1,0:T(8,128)(2,1)} %w_own.1), channel_id=1, source_target_pairs={{0,1},{1,0},{2,3},{3,2},{4,5},{5,4},{6,7},{7,6},{8,9},{9,8},{10,11... | collective-permute-start | bytes 786440 | tf_op jit(solution)/shard_map/ppermute | solution.py:41
  1.7 2.9 %copy-start.6 = (s32[1,4096]{1,0:T(1,128)S(1)}, s32[1,4096]{1,0:T(1,128)}, u32[]{:S(2)}) copy-start(s32[1,4096]{1,0:T(1,128)} %send.3) | copy-start | bytes 49156
  1.7 11.8 %copy-start.7 = (s32[1,4096]{1,0:T(1,128)S(1)}, s32[1,4096]{1,0:T(1,128)}, u32[]{:S(2)}) copy-start(s32[1,4096]{1,0:T(1,128)} %recv.1) | copy-start | bytes 49156
  1.7 11.8 %copy-start.8 = (s32[16,128]{1,0:T(8,128)S(1)}, s32[16,128]{1,0:T(8,128)}, u32[]{:S(2)}) copy-start(s32[16,128]{1,0:T(8,128)} %src.1) | copy-start | bytes 24580
  1.7 11.8 %copy-start.9 = (s32[16,128]{1,0:T(8,128)S(1)}, s32[16,128]{1,0:T(8,128)}, u32[]{:S(2)}) copy-start(s32[16,128]{1,0:T(8,128)} %dst.1) | copy-start | bytes 24580
  1.8 11.8 %copy-start.10 = (s32[1,1024]{1,0:T(1,128)S(1)}, s32[1,1024]{1,0:T(1,128)}, u32[]{:S(2)}) copy-start(s32[1,1024]{1,0:T(1,128)} %halo_rows.1) | copy-start | bytes 12292
  1.8 11.8 %copy-start.11 = (f32[256]{0:T(256)S(1)}, f32[256]{0:T(256)}, u32[]{:S(2)}) copy-start(f32[256]{0:T(256)} %param.19) | copy-start | bytes 3076
  6.2 17.6 %collective-permute-start.4 = (bf16[1088,128]{1,0:T(8,128)(2,1)S(1)}, bf16[1088,128]{1,0:T(8,128)(2,1)S(1)}, u32[]{:S(2)}, u32[]{:S(2)}) collective-permute-start(bf16[1088,128]{1,0:T(8,128)(2,1)S(1)} %get-tuple-element.97), channel_id=1, source_target_pairs={{0,8},{2,10},{4,12},{6,14},{8,0},{10,2},{12,4},{14,6},{1,9},{3,11}... | collective-permute-start | bytes 835592 | tf_op jit(solution)/shard_map/ppermute | solution.py:45
  10.2 28.3 %collective-permute-start.5 = (bf16[512,256]{1,0:T(8,128)(2,1)S(1)}, bf16[512,256]{1,0:T(8,128)(2,1)S(1)}, u32[]{:S(2)}, u32[]{:S(2)}) collective-permute-start(bf16[512,256]{1,0:T(8,128)(2,1)S(1)} %get-tuple-element.102), channel_id=1, source_target_pairs={{0,6},{2,4},{4,2},{6,0},{8,14},{10,12},{12,10},{14,8},{1,7},{3,5},... | collective-permute-start | bytes 786440 | tf_op jit(solution)/shard_map/ppermute | solution.py:45
  12.8 25.8 %collective-permute-start.6 = (bf16[512,256]{1,0:T(8,128)(2,1)S(1)}, bf16[512,256]{1,0:T(8,128)(2,1)S(1)}, u32[]{:S(2)}, u32[]{:S(2)}) collective-permute-start(bf16[512,256]{1,0:T(8,128)(2,1)S(1)} %get-tuple-element.103), channel_id=1, source_target_pairs={{0,4},{2,6},{4,0},{6,2},{8,12},{10,14},{12,8},{14,10},{1,5},{3,7},... | collective-permute-start | bytes 786440 | tf_op jit(solution)/shard_map/ppermute | solution.py:45
  13.2 21.1 %collective-permute-start.12 = (bf16[1024,128]{1,0:T(8,128)(2,1)S(1)}, bf16[1024,128]{1,0:T(8,128)(2,1)S(1)}, u32[]{:S(2)}, u32[]{:S(2)}) collective-permute-start(bf16[1024,128]{1,0:T(8,128)(2,1)S(1)} %get-tuple-element.87.g1), channel_id=1, source_target_pairs={{0,8},{2,10},{4,12},{6,14},{8,0},{10,2},{12,4},{14,6},{1,9},{3,11}... | collective-permute-start | bytes 786440 | tf_op jit(solution)/shard_map/ppermute | solution.py:45
  19.0 20.2 %collective-permute-start.7 = (bf16[512,256]{1,0:T(8,128)(2,1)S(1)}, bf16[512,256]{1,0:T(8,128)(2,1)S(1)}, u32[]{:S(2)}, u32[]{:S(2)}) collective-permute-start(bf16[512,256]{1,0:T(8,128)(2,1)S(1)} %get-tuple-element.104), channel_id=1, source_target_pairs={{0,2},{2,0},{4,6},{6,4},{8,10},{10,8},{12,14},{14,12},{1,3},{3,1},... | collective-permute-start | bytes 786440 | tf_op jit(solution)/shard_map/ppermute | solution.py:45
  25.8 15.3 %collective-permute-start.8 = (bf16[512,128]{1,0:T(8,128)(2,1)S(1)}, bf16[512,128]{1,0:T(8,128)(2,1)S(1)}, u32[]{:S(2)}, u32[]{:S(2)}) collective-permute-start(bf16[512,128]{1,0:T(8,128)(2,1)S(1)} %get-tuple-element.105), channel_id=1, source_target_pairs={{0,6},{2,4},{4,2},{6,0},{8,14},{10,12},{12,10},{14,8},{1,7},{3,5},... | collective-permute-start | bytes 393224 | tf_op jit(solution)/shard_map/ppermute | solution.py:45
  35.2 12.0 %collective-permute-start.13 = (bf16[512,128]{1,0:T(8,128)(2,1)S(1)}, bf16[512,128]{1,0:T(8,128)(2,1)S(1)}, u32[]{:S(2)}, u32[]{:S(2)}) collective-permute-start(bf16[512,128]{1,0:T(8,128)(2,1)S(1)} %get-tuple-element.111), channel_id=1, source_target_pairs={{0,6},{2,4},{4,2},{6,0},{8,14},{10,12},{12,10},{14,8},{1,7},{3,5},... | collective-permute-start | bytes 393224 | tf_op jit(solution)/shard_map/ppermute | solution.py:45
  38.5 7.9 %collective-permute-start.9 = (bf16[512,128]{1,0:T(8,128)(2,1)S(1)}, bf16[512,128]{1,0:T(8,128)(2,1)S(1)}, u32[]{:S(2)}, u32[]{:S(2)}) collective-permute-start(bf16[512,128]{1,0:T(8,128)(2,1)S(1)} %get-tuple-element.106), channel_id=1, source_target_pairs={{0,4},{2,6},{4,0},{6,2},{8,12},{10,14},{12,8},{14,10},{1,5},{3,7},... | collective-permute-start | bytes 393224 | tf_op jit(solution)/shard_map/ppermute | solution.py:45
  38.5 7.9 %collective-permute-start.10 = (bf16[512,128]{1,0:T(8,128)(2,1)S(1)}, bf16[512,128]{1,0:T(8,128)(2,1)S(1)}, u32[]{:S(2)}, u32[]{:S(2)}) collective-permute-start(bf16[512,128]{1,0:T(8,128)(2,1)S(1)} %get-tuple-element.107), channel_id=1, source_target_pairs={{0,2},{2,0},{4,6},{6,4},{8,10},{10,8},{12,14},{14,12},{1,3},{3,1},... | collective-permute-start | bytes 393224 | tf_op jit(solution)/shard_map/ppermute | solution.py:45
  39.2 8.1 %collective-permute-start.14 = (bf16[512,128]{1,0:T(8,128)(2,1)S(1)}, bf16[512,128]{1,0:T(8,128)(2,1)S(1)}, u32[]{:S(2)}, u32[]{:S(2)}) collective-permute-start(bf16[512,128]{1,0:T(8,128)(2,1)S(1)} %get-tuple-element.112), channel_id=1, source_target_pairs={{0,4},{2,6},{4,0},{6,2},{8,12},{10,14},{12,8},{14,10},{1,5},{3,7},... | collective-permute-start | bytes 393224 | tf_op jit(solution)/shard_map/ppermute | solution.py:45
  41.1 6.2 %collective-permute-start.15 = (bf16[512,128]{1,0:T(8,128)(2,1)S(1)}, bf16[512,128]{1,0:T(8,128)(2,1)S(1)}, u32[]{:S(2)}, u32[]{:S(2)}) collective-permute-start(bf16[512,128]{1,0:T(8,128)(2,1)S(1)} %get-tuple-element.113), channel_id=1, source_target_pairs={{0,2},{2,0},{4,6},{6,4},{8,10},{10,8},{12,14},{14,12},{1,3},{3,1},... | collective-permute-start | bytes 393224 | tf_op jit(solution)/shard_map/ppermute | solution.py:45
  47.1 1.5 %copy-start = (bf16[512,256]{1,0:T(8,128)(2,1)S(1)}, bf16[512,256]{1,0:T(8,128)(2,1)}, u32[]{:S(2)}) copy-start(bf16[512,256]{1,0:T(8,128)(2,1)} %refs_2_.1) | copy-start | bytes 786436
  47.1 1.5 %copy-start.1 = (bf16[256,512]{1,0:T(8,128)(2,1)S(1)}, bf16[256,512]{1,0:T(8,128)(2,1)}, u32[]{:S(2)}) copy-start(bf16[256,512]{1,0:T(8,128)(2,1)} %w_own.1) | copy-start | bytes 786436
  47.2 1.4 %copy-start.5 = (bf16[256,512]{1,0:T(8,128)(2,1)S(1)}, bf16[256,512]{1,0:T(8,128)(2,1)}, u32[]{:S(2)}) copy-start(bf16[256,512]{1,0:T(8,128)(2,1)} %refs_6_.1) | copy-start | bytes 786436
  47.2 2.3 %copy-start.2 = (bf16[512,256]{1,0:T(8,128)(2,1)S(1)}, bf16[512,256]{1,0:T(8,128)(2,1)}, u32[]{:S(2)}) copy-start(bf16[512,256]{1,0:T(8,128)(2,1)} %w_send.3) | copy-start | bytes 786436
  47.2 1.4 %collective-permute-start.11 = (bf16[512,128]{1,0:T(8,128)(2,1)S(1)}, bf16[512,128]{1,0:T(8,128)(2,1)S(1)}, u32[]{:S(2)}, u32[]{:S(2)}) collective-permute-start(bf16[512,128]{1,0:T(8,128)(2,1)S(1)} %mirror_sums.2.refs_0_), channel_id=1, source_target_pairs={{0,1},{1,0},{2,3},{3,2},{4,5},{5,4},{6,7},{7,6},{8,9},{9,8},{10,11... | collective-permute-start | bytes 393224 | tf_op jit(solution)/shard_map/ppermute | solution.py:41
  47.9 14.0 %copy-start.3 = (bf16[512,256]{1,0:T(8,128)(2,1)S(1)}, bf16[512,256]{1,0:T(8,128)(2,1)}, u32[]{:S(2)}) copy-start(bf16[512,256]{1,0:T(8,128)(2,1)} %w_recv.3) | copy-start | bytes 786436
  48.0 14.0 %copy-start.12 = (f32[256]{0:T(256)S(1)}, f32[256]{0:T(256)}, u32[]{:S(2)}) copy-start(f32[256]{0:T(256)} %param.23) | copy-start | bytes 3076
  48.0 1.5 %collective-permute-start.16 = (bf16[512,128]{1,0:T(8,128)(2,1)S(1)}, bf16[512,128]{1,0:T(8,128)(2,1)S(1)}, u32[]{:S(2)}, u32[]{:S(2)}) collective-permute-start(bf16[512,128]{1,0:T(8,128)(2,1)S(1)} %mirror_sums.3.mine), channel_id=1, source_target_pairs={{0,1},{1,0},{2,3},{3,2},{4,5},{5,4},{6,7},{7,6},{8,9},{9,8},{10,11... | collective-permute-start | bytes 393224 | tf_op jit(solution)/shard_map/ppermute | solution.py:41
  50.7 9.1 %collective-permute-start.17 = (bf16[128,256]{1,0:T(8,128)(2,1)S(1)}, bf16[128,256]{1,0:T(8,128)(2,1)S(1)}, u32[]{:S(2)}, u32[]{:S(2)}) collective-permute-start(bf16[128,256]{1,0:T(8,128)(2,1)S(1)} %get-tuple-element.123), channel_id=1, source_target_pairs={{0,14},{2,12},{4,10},{6,8},{8,6},{10,4},{12,2},{14,0},{1,15},{3,13... | collective-permute-start | bytes 196616 | tf_op jit(solution)/shard_map/ppermute | solution.py:45
  54.5 6.6 %collective-permute-start.18 = (bf16[128,256]{1,0:T(8,128)(2,1)S(1)}, bf16[128,256]{1,0:T(8,128)(2,1)S(1)}, u32[]{:S(2)}, u32[]{:S(2)}) collective-permute-start(bf16[128,256]{1,0:T(8,128)(2,1)S(1)} %get-tuple-element.124), channel_id=1, source_target_pairs={{0,12},{2,14},{4,8},{6,10},{8,4},{10,6},{12,0},{14,2},{1,13},{3,15... | collective-permute-start | bytes 196616 | tf_op jit(solution)/shard_map/ppermute | solution.py:45
  54.6 9.5 %collective-permute-start.19 = (bf16[128,256]{1,0:T(8,128)(2,1)S(1)}, bf16[128,256]{1,0:T(8,128)(2,1)S(1)}, u32[]{:S(2)}, u32[]{:S(2)}) collective-permute-start(bf16[128,256]{1,0:T(8,128)(2,1)S(1)} %get-tuple-element.125), channel_id=1, source_target_pairs={{0,10},{2,8},{4,14},{6,12},{8,2},{10,0},{12,6},{14,4},{1,11},{3,9}... | collective-permute-start | bytes 196616 | tf_op jit(solution)/shard_map/ppermute | solution.py:45
  55.5 10.4 %collective-permute-start.20 = (bf16[128,256]{1,0:T(8,128)(2,1)S(1)}, bf16[128,256]{1,0:T(8,128)(2,1)S(1)}, u32[]{:S(2)}, u32[]{:S(2)}) collective-permute-start(bf16[128,256]{1,0:T(8,128)(2,1)S(1)} %get-tuple-element.126), channel_id=1, source_target_pairs={{0,8},{2,10},{4,12},{6,14},{8,0},{10,2},{12,4},{14,6},{1,9},{3,11}... | collective-permute-start | bytes 196616 | tf_op jit(solution)/shard_map/ppermute | solution.py:45
  58.5 7.5 %collective-permute-start.21 = (bf16[128,256]{1,0:T(8,128)(2,1)S(1)}, bf16[128,256]{1,0:T(8,128)(2,1)S(1)}, u32[]{:S(2)}, u32[]{:S(2)}) collective-permute-start(bf16[128,256]{1,0:T(8,128)(2,1)S(1)} %get-tuple-element.127), channel_id=1, source_target_pairs={{0,6},{2,4},{4,2},{6,0},{8,14},{10,12},{12,10},{14,8},{1,7},{3,5},... | collective-permute-start | bytes 196616 | tf_op jit(solution)/shard_map/ppermute | solution.py:45
  59.8 6.6 %collective-permute-start.22 = (bf16[128,256]{1,0:T(8,128)(2,1)S(1)}, bf16[128,256]{1,0:T(8,128)(2,1)S(1)}, u32[]{:S(2)}, u32[]{:S(2)}) collective-permute-start(bf16[128,256]{1,0:T(8,128)(2,1)S(1)} %get-tuple-element.128), channel_id=1, source_target_pairs={{0,4},{2,6},{4,0},{6,2},{8,12},{10,14},{12,8},{14,10},{1,5},{3,7},... | collective-permute-start | bytes 196616 | tf_op jit(solution)/shard_map/ppermute | solution.py:45
  61.1 5.3 %collective-permute-start.23 = (bf16[128,256]{1,0:T(8,128)(2,1)S(1)}, bf16[128,256]{1,0:T(8,128)(2,1)S(1)}, u32[]{:S(2)}, u32[]{:S(2)}) collective-permute-start(bf16[128,256]{1,0:T(8,128)(2,1)S(1)} %get-tuple-element.129), channel_id=1, source_target_pairs={{0,2},{2,0},{4,6},{6,4},{8,10},{10,8},{12,14},{14,12},{1,3},{3,1},... | collective-permute-start | bytes 196616 | tf_op jit(solution)/shard_map/ppermute | solution.py:45
  66.4 2.4 %copy-start.4 = (bf16[512,256]{1,0:T(8,128)(2,1)S(1)}, bf16[512,256]{1,0:T(8,128)(2,1)}, u32[]{:S(2)}) copy-start(bf16[512,256]{1,0:T(8,128)(2,1)} %get-tuple-element.65.encoded) | copy-start | bytes 786436
  68.7 1.6 %collective-permute-start.24 = (bf16[512,256]{1,0:T(8,128)(2,1)S(1)}, bf16[512,256]{1,0:T(8,128)(2,1)S(1)}, u32[]{:S(2)}, u32[]{:S(2)}) collective-permute-start(bf16[512,256]{1,0:T(8,128)(2,1)S(1)} %edge_sums.1.mine), channel_id=1, source_target_pairs={{0,1},{1,0},{2,3},{3,2},{4,5},{5,4},{6,7},{7,6},{8,9},{9,8},{10,11... | collective-permute-start | bytes 786440 | tf_op jit(solution)/shard_map/ppermute | solution.py:41

commit v5 on v4

--- a/solution.py
+++ b/solution.py
@@ -78,20 +78,18 @@
         copy.wait()
 
 
-def own_features_kernel(feat, grid, mesh, w_send, w_recv, send, grid_part, mesh_part, send_rest, recv_rest, list_out, *scratch):
-    ws, g, wr, m, ids, sems = scratch
-    first = start_copies(w_send, ws, sems, 0, 4) + start_copies(grid, g, sems, 4, 4)
-    second = start_copies(w_recv, wr, sems, 8, 4) + start_copies(mesh, m, sems, 12, 4)
-    second += start_copies(send, ids, sems, 16, 1)
+def own_features_kernel(feat, grid, w_send, send, grid_part, send_rest, list_rows, digits, *scratch):
+    ws, g, ids, sems = scratch
+    copies = start_copies(send, ids, sems, 0, 1) + start_copies(w_send, ws, sems, 1, 4)
+    copies += start_copies(grid, g, sems, 5, 8)
     own, other = halves_of(feat[0], g.shape[1])
-    wait_copies(first)
+    wait_copies(copies[:1])
+    rows = jnp.concatenate([ids[:, a : a + LANES] for a in range(0, ids.shape[1], LANES)], axis=0)
+    list_rows[...] = rows
+    digits[...] = jnp.concatenate([rows // DIGIT, rows % DIGIT], axis=0).astype(F32).astype(BF16)
+    wait_copies(copies[1:])
     grid_part[...] = dot(g[...], ws[own, :])
     send_rest[...] = ws[other, :]
-    wait_copies(second)
-    mesh_part[...] = dot(m[...], wr[own, :])
-    recv_rest[...] = wr[other, :]
-    rows = jnp.concatenate([ids[:, a : a + LANES] for a in range(0, ids.shape[1], LANES)], axis=0)
-    list_out[...] = jnp.concatenate([rows // DIGIT, rows % DIGIT], axis=0).astype(F32).astype(BF16)
 
 
 def other_features_kernel(part, rest, other, *outs):
@@ -108,51 +106,58 @@
     first[part.shape[0] :, :] = digits[...]
 
 
-def project(grid, mesh, w_send, w_recv, send, n_chunks):
-    grid_other, mesh_other = swap(grid), swap(mesh)
+def project(grid, w_send, send, n_chunks):
+    grid_other = swap(grid)
     hidden, feats = w_send.shape[1], grid.shape[1]
-    parts = call(
+    lines = send.shape[1] // LANES
+    grid_part, send_rest, list_rows, digits = call(
         own_features_kernel,
         [
             shape_of((grid.shape[0], hidden), F32),
-            shape_of((mesh.shape[0], hidden), F32),
             shape_of((feats, hidden), BF16),
-            shape_of((feats, hidden), BF16),
-            shape_of((2 * send.shape[1] // LANES, LANES), BF16),
+            shape_of((lines, LANES), I32),
+            shape_of((2 * lines, LANES), BF16),
         ],
         position("feat"),
-        *[pltpu.with_memory_space_constraint(x, pltpu.HBM) for x in (grid, mesh, w_send, w_recv, send)],
-        specs=[SMEM] + [HBM] * 5,
-        scratch=[pltpu.VMEM(x.shape, x.dtype) for x in (w_send, grid, w_recv, mesh, send)]
-        + [pltpu.SemaphoreType.DMA((17,))],
+        *[pltpu.with_memory_space_constraint(x, pltpu.HBM) for x in (grid, w_send, send)],
+        specs=[SMEM] + [HBM] * 3,
+        scratch=[pltpu.VMEM(x.shape, x.dtype) for x in (w_send, grid, send)] + [pltpu.SemaphoreType.DMA((13,))],
         name="own_features",
-        mib=16,
-    )
-    grid_part, mesh_part, send_rest, recv_rest, digits = parts
+    )
     chunk = shape_of((grid.shape[0], hidden // n_chunks), BF16)
-    if n_chunks > 1:
-        first = shape_of((grid.shape[0] + digits.shape[0], chunk.shape[1]), BF16)
-        chunks = call(
-            with_list_kernel,
-            [chunk] * n_chunks + [first],
-            grid_part,
-            send_rest,
-            grid_other,
-            digits,
-            name="other_grid_features",
-        )
-    else:
-        chunks = call(other_features_kernel, [chunk], grid_part, send_rest, grid_other, name="other_grid_features")
-    chunks, mesh_part = lax.optimization_barrier((chunks, mesh_part))
-    (mesh_proj,) = call(
-        other_features_kernel,
-        [shape_of((mesh.shape[0], hidden), BF16)],
-        mesh_part,
-        recv_rest,
+    if n_chunks == 1:
+        return call(
+            other_features_kernel, [chunk], grid_part, send_rest, grid_other, name="other_grid_features"
+        ), list_rows
+    first = shape_of((grid.shape[0] + digits.shape[0], chunk.shape[1]), BF16)
+    chunks = call(
+        with_list_kernel,
+        [chunk] * n_chunks + [first],
+        grid_part,
+        send_rest,
+        grid_other,
+        digits,
+        name="other_grid_features",
+    )
+    return chunks, list_rows
+
+
+def mesh_features_kernel(feat, mesh, other_mesh, w_recv, out):
+    own, other = halves_of(feat[0], mesh.shape[1])
+    out[...] = (dot(mesh[...], w_recv[own, :]) + dot(other_mesh[...], w_recv[other, :])).astype(BF16)
+
+
+def project_mesh(mesh, mesh_other, w_recv):
+    return call(
+        mesh_features_kernel,
+        shape_of((mesh.shape[0], w_recv.shape[1]), BF16),
+        position("feat"),
+        mesh,
         mesh_other,
-        name="other_mesh_features",
-    )
-    return chunks, mesh_proj, mesh_other
+        w_recv,
+        specs=[SMEM] + [VMEM] * 3,
+        name="mesh_features",
+    )
 
 
 def across(row):
@@ -167,12 +172,12 @@
     return (across(row[:, at : at + LANES])[:, :1] == iota((LANES, width), 1)).astype(BF16)
 
 
-def pack_own_kernel(bits, me, send, g0, g1, *outs):
+def pack_own_kernel(bits, me, list_rows, g0, g1, *outs):
     width, cap = g0.shape[1], outs[0].shape[0]
     for k, out in zip(bits, outs):
-        ids = slots_of(send, me[0] ^ k, cap)
         for at in range(0, cap, LANES):
-            hot = one_hot_rows(ids, g0.shape[0], at)
+            ids = list_rows[pl.ds((me[0] ^ k) * (cap // LANES) + at // LANES, 1), :]
+            hot = one_hot_rows(ids, g0.shape[0], 0)
             out[at : at + LANES, :width] = dot(hot, g0[...]).astype(BF16)
             out[at : at + LANES, width:] = dot(hot, g1[...]).astype(BF16)
 
@@ -188,9 +193,9 @@
             term[here, :] = dot(one_hot_rows(rows, mesh_proj.shape[0], at), mesh_proj[...]) + bias[...]
 
 
-def aside_kernel(half, cap, blocks, me, send, recv, g0, g1, mesh_proj, bias, halo_rows, src, dst, *outs):
+def aside_kernel(half, cap, blocks, me, list_rows, send, recv, g0, g1, mesh_proj, bias, halo_rows, src, dst, *outs):
     packed, sums, into, term, *selections = outs
-    pack_own_kernel((1,), me, send, g0, g1, packed)
+    pack_own_kernel((1,), me, list_rows, g0, g1, packed)
     local_sums_kernel(cap, me, send, recv, g0, g1, mesh_proj, bias, sums)
     prepare_kernel(half, me, recv, mesh_proj, bias, into, term)
     select_kernel(blocks, me, halo_rows, src, dst, *selections)
@@ -255,9 +260,9 @@
     out[...] = sums.astype(out.dtype)
 
 
-def sums_by_halves(grid_chunks, mesh_rproj, bias, send_grid, recv_row, n_dom, select, lists):
+def sums_by_halves(grid_chunks, list_rows, mesh, bias, send_grid, recv_row, n_dom, select, lists):
     half = n_dom // 2
-    mesh_rows, hidden = mesh_rproj.shape
+    mesh_rows, hidden = mesh[0].shape[0], mesh[2].shape[1]
     *grid_chunks, with_list = grid_chunks
     grid_rows, width = grid_chunks[0].shape
     cap = send_grid.shape[1] // n_dom
@@ -268,7 +273,7 @@
             functools.partial(pack_own_kernel, bits),
             [shape_of((cap, hidden), BF16)] * len(bits),
             me,
-            send_grid,
+            list_rows,
             *grid_chunks,
             specs=[SMEM] + [VMEM] * 3,
             name="pack_own",
@@ -276,7 +281,8 @@
         return blocks
 
     packed = pack_own(3, 2)
-    packed, with_list, grid_chunks = lax.optimization_barrier((packed, with_list, grid_chunks))
+    packed, with_list, grid_chunks, mesh = lax.optimization_barrier((packed, with_list, grid_chunks, mesh))
+    mesh_rproj = project_mesh(*mesh)
     arrived = {k: from_xor(block, k, n_dom) for k, block in zip((3, 2), packed)}
     mirrored = [from_xor(with_list, half, n_dom)]
     selection_shapes, blocks = select
@@ -290,13 +296,14 @@
             *selection_shapes,
         ],
         me,
+        list_rows,
         send_grid,
         recv_row,
         *grid_chunks,
         mesh_rproj,
         bias,
         *lists,
-        specs=[SMEM] + [VMEM] * (6 + len(lists)),
+        specs=[SMEM] + [VMEM] * (7 + len(lists)),
         name="aside",
     )
     arrived[1] = from_xor(packed, 1, n_dom)
@@ -356,7 +363,9 @@
     return chunks, selections
 
 
-def sums_by_all_to_all(grid_chunks, mesh_rproj, bias, send_grid, recv_row, n_dom, select, lists):
+def sums_by_all_to_all(grid_chunks, list_rows, mesh, bias, send_grid, recv_row, n_dom, select, lists):
+    mesh_rproj = project_mesh(*mesh)
+
     def rows_of(table, index):
         hot = index[0][:, None] == iota((index.shape[1], table.shape[0]), 1)
         return dot(hot.astype(BF16), table)
@@ -478,12 +487,11 @@
     mesh_rows, feats = mesh_lat.shape
     hidden = w_grid_send.shape[1]
     halves = n_dom == 8
-    grid_chunks, mesh_rproj, mesh_other = project(
-        grid_lat, mesh_lat, w_grid_send, w_grid_recv, send_grid, 2 if halves else 1
-    )
-    grid_chunks, mesh_rproj, send_grid, recv_row, w_other, w2_other = lax.optimization_barrier(
-        (grid_chunks, mesh_rproj, send_grid, recv_row, swap(w_grid_out), swap(w_edge_out))
-    )
+    grid_chunks, list_rows = project(grid_lat, w_grid_send, send_grid, 2 if halves else 1)
+    grid_chunks, list_rows, send_grid, recv_row, mesh_lat, mesh_other, w_other, w2_other = lax.optimization_barrier(
+        (grid_chunks, list_rows, send_grid, recv_row, mesh_lat, swap(mesh_lat), swap(w_grid_out), swap(w_edge_out))
+    )
+    mesh = (mesh_lat, mesh_other, w_grid_recv)
     me, feat = position("dom"), position("feat")
     blocks = n_dom if halves else 1
     n_halo, edges = halo_rows.shape[1], edge_src.shape[0] * edge_src.shape[1]
@@ -499,7 +507,7 @@
     )
     sums = sums_by_halves if halves else sums_by_all_to_all
     lists = (halo_rows, edge_src, edge_dst)
-    chunks, selections = sums(grid_chunks, mesh_rproj, g2m_bias, send_grid, recv_row, n_dom, select, lists)
+    chunks, selections = sums(grid_chunks, list_rows, mesh, g2m_bias, send_grid, recv_row, n_dom, select, lists)
     pick, near_src, near_dst, far_src, into = selections
     *early, last = chunks
     base, w_out = call(

time: 71.4 us -> 70.8 us (level)
  transfers between devices with their start and end apart: 25 -> 25, of which waited for: 9 -> 11; matrix products, arithmetic and copies ran while one was open for 0% -> 0% of each run, Pallas kernels for 27% -> 27%
where the time goes in v5:
time: 70.8 us; the launch traced here: 70.6 us
  starting transfers between devices  28.5 us (40%)
  Pallas kernels  24.6 us (35%)
  waiting for transfers between devices  16.3 us (23%)
  between operations  1.01 us (1%)
    ppermute x18, starting transfers between devices, from_xor(): return lax.ppermute(x, 'dom', [(i, i ^ bits) for i in range(n_dom)])  26.7 us
    pallas_call x19, Pallas kernels, call(): pl.pallas_call(kernel, out_shape=out_shape, in_specs=[VMEM] * len(args) i...  24.6 us
    ppermute x18, waiting for transfers between devices, from_xor(): return lax.ppermute(x, 'dom', [(i, i ^ bits) for i in range(n_dom)])  14.4 us
    ppermute x7, waiting for transfers between devices, swap(): return lax.ppermute(x, 'feat', [(0, 1), (1, 0)])  1.92 us
    ppermute x7, starting transfers between devices, swap(): return lax.ppermute(x, 'feat', [(0, 1), (1, 0)])  1.79 us
  transfers between devices with their start and end apart: 25, of which 11 were waited for; matrix products, arithmetic and copies ran while one was open for 0% of the time, Pallas kernels for 27%

profile of v5, /device:TPU:0, one launch (start us, length us, event | category | flops | bytes accessed | tf_op | source)
XLA Modules:
  0.0 70.6 jit_solution(3218747328916337024)
XLA Ops:
  0.7 0.5 collective-permute-start
  1.2 0.1 collective-permute-start.1
  1.3 0.4 collective-permute-start.3
  1.8 1.6 %own_features.1 = (f32[1024,256]{1,0:T(8,128)S(1)}, bf16[256,256]{1,0:T(8,128)(2,1)S(1)}, s32[32,128]{1,0:T(8,128)S(1)}, bf16[64,128]{1,0:T(8,128)(2,1)S(1)}) custom-call(s32[1]{0:T(128)} %bitcast.feat, bf16[1024,256]{1,0:T(8,128)(2,1)} %grid.1, bf16[512,256]{1,0:T(8,128)(2,1)} %w_send.2, s32[1,4096]{1,0:T(1,128)} %send.2), custom_call_target="tpu_custom_call" | custom-call | tf_op jit(solution)/shard_map/own_features/pallas_call | solution.py:49
  3.4 0.6 other_grid_features.1
  4.0 0.1 collective-permute-done.2.refs_5_.w_other
  4.1 1.5 %pack_own.1 = (bf16[512,256]{1,0:T(8,128)(2,1)S(1)}, bf16[512,256]{1,0:T(8,128)(2,1)S(1)}) custom-call(s32[1]{0:T(128)} %bitcast.1.me, s32[32,128]{1,0:T(8,128)S(1)} %get-tuple-element.74.list_rows, bf16[1024,128]{1,0:T(8,128)(2,1)S(1)} %get-tuple-element.84.g0, bf16[1024,128]{1,0:T(8,128)(2,1)S(1)} %get-tuple-element.85.g1), custom_call_target="tpu_custom_call" | custom-call | tf_op jit(solution)/shard_map/pack_own/pallas_call | solution.py:49
  5.6 4.0 %collective-permute-start.4 = (bf16[1088,128]{1,0:T(8,128)(2,1)S(1)}, bf16[1088,128]{1,0:T(8,128)(2,1)S(1)}, u32[]{:S(2)}, u32[]{:S(2)}) collective-permute-start(bf16[1088,128]{1,0:T(8,128)(2,1)S(1)} %get-tuple-element.97), channel_id=1, source_target_pairs={{0,8},{2,10},{4,12},{6,14},{8,0},{10,2},{12,4},{14,6},{1,9},{3,11}... | collective-permute-start | bytes 835592 | tf_op jit(solution)/shard_map/ppermute | solution.py:45
  9.6 2.5 %collective-permute-start.5 = (bf16[512,256]{1,0:T(8,128)(2,1)S(1)}, bf16[512,256]{1,0:T(8,128)(2,1)S(1)}, u32[]{:S(2)}, u32[]{:S(2)}) collective-permute-start(bf16[512,256]{1,0:T(8,128)(2,1)S(1)} %get-tuple-element.102), channel_id=1, source_target_pairs={{0,6},{2,4},{4,2},{6,0},{8,14},{10,12},{12,10},{14,8},{1,7},{3,5},... | collective-permute-start | bytes 786440 | tf_op jit(solution)/shard_map/ppermute | solution.py:45
  12.1 0.4 collective-permute-start.6
  12.6 0.3 collective-permute-start.12
  12.9 0.3 mesh_features.1.mesh_proj
  13.3 5.4 %aside.1 = (bf16[512,256]{1,0:T(8,128)(2,1)S(1)}, f32[512,256]{1,0:T(8,128)S(1)}, bf16[512,2048]{1,0:T(8,128)(2,1)S(1)}, f32[2048,256]{1,0:T(8,128)S(1)}, bf16[1...) custom-call(s32[1]{0:T(128)} %bitcast.1.me, ...), custom_call_target="tpu_custom_call" | custom-call | tf_op jit(solution)/shard_map/aside/pallas_call | solution.py:49
  18.7 0.3 collective-permute-start.7
  19.0 4.1 %collective-permute-done.4.mirrored = bf16[1088,128]{1,0:T(8,128)(2,1)S(1)} collective-permute-done((bf16[1088,128]{1,0:T(8,128)(2,1)S(1)}, bf16[1088,128]{1,0:T(8,128)(2,1)S(1)}, u32[]{:S(2)}, u32[]{:S(2)}) %collective-permute-start.4) | collective-permute-done | bytes 278560 | tf_op jit(solution)/shard_map/ppermute | solution.py:45
  23.1 1.0 %pick.1 = bf16[2048,1024]{1,0:T(8,128)(2,1)S(1)} custom-call(s32[1]{0:T(128)} %bitcast.1.me, bf16[1088,128]{1,0:T(8,128)(2,1)S(1)} %collective-permute-done.4.mirrored), custom_call_target="tpu_custom_call" | custom-call | tf_op jit(solution)/shard_map/pick/pallas_call | solution.py:49
  24.1 1.0 %pack_mirror.2 = (bf16[512,128]{1,0:T(8,128)(2,1)S(1)}, bf16[512,128]{1,0:T(8,128)(2,1)S(1)}, bf16[512,128]{1,0:T(8,128)(2,1)S(1)}) custom-call(bf16[2048,1024]{1,0:T(8,128)(2,1)S(1)} %pick.1, bf16[1088,128]{1,0:T(8,128)(2,1)S(1)} %collective-permute-done.4.mirrored), custom_call_target="tpu_custom_call" | custom-call | tf_op jit(solution)/shard_map/pack_mirror/pallas_call | solution.py:49
  25.1 1.2 %collective-permute-start.8 = (bf16[512,128]{1,0:T(8,128)(2,1)S(1)}, bf16[512,128]{1,0:T(8,128)(2,1)S(1)}, u32[]{:S(2)}, u32[]{:S(2)}) collective-permute-start(bf16[512,128]{1,0:T(8,128)(2,1)S(1)} %get-tuple-element.105), channel_id=1, source_target_pairs={{0,6},{2,4},{4,2},{6,0},{8,14},{10,12},{12,10},{14,8},{1,7},{3,5},... | collective-permute-start | bytes 393224 | tf_op jit(solution)/shard_map/ppermute | solution.py:45
  26.4 7.2 %collective-permute-done.12.mirrored = bf16[1024,128]{1,0:T(8,128)(2,1)S(1)} collective-permute-done((bf16[1024,128]{1,0:T(8,128)(2,1)S(1)}, bf16[1024,128]{1,0:T(8,128)(2,1)S(1)}, u32[]{:S(2)}, u32[]{:S(2)}) %collective-permute-start.12) | collective-permute-done | bytes 262176 | tf_op jit(solution)/shard_map/ppermute | solution.py:45
  33.6 1.0 %pack_mirror.3 = (bf16[512,128]{1,0:T(8,128)(2,1)S(1)}, bf16[512,128]{1,0:T(8,128)(2,1)S(1)}, bf16[512,128]{1,0:T(8,128)(2,1)S(1)}) custom-call(bf16[2048,1024]{1,0:T(8,128)(2,1)S(1)} %pick.1, bf16[1024,128]{1,0:T(8,128)(2,1)S(1)} %collective-permute-done.12.mirrored), custom_call_target="tpu_custom_call" | custom-call | tf_op jit(solution)/shard_map/pack_mirror/pallas_call | solution.py:49
  34.6 3.3 %collective-permute-start.13 = (bf16[512,128]{1,0:T(8,128)(2,1)S(1)}, bf16[512,128]{1,0:T(8,128)(2,1)S(1)}, u32[]{:S(2)}, u32[]{:S(2)}) collective-permute-start(bf16[512,128]{1,0:T(8,128)(2,1)S(1)} %get-tuple-element.111), channel_id=1, source_target_pairs={{0,6},{2,4},{4,2},{6,0},{8,14},{10,12},{12,10},{14,8},{1,7},{3,5},... | collective-permute-start | bytes 393224 | tf_op jit(solution)/shard_map/ppermute | solution.py:45
  37.9 0.6 collective-permute-start.10
  38.5 1.9 %collective-permute-start.14 = (bf16[512,128]{1,0:T(8,128)(2,1)S(1)}, bf16[512,128]{1,0:T(8,128)(2,1)S(1)}, u32[]{:S(2)}, u32[]{:S(2)}) collective-permute-start(bf16[512,128]{1,0:T(8,128)(2,1)S(1)} %get-tuple-element.112), channel_id=1, source_target_pairs={{0,4},{2,6},{4,0},{6,2},{8,12},{10,14},{12,8},{14,10},{1,5},{3,7},... | collective-permute-start | bytes 393224 | tf_op jit(solution)/shard_map/ppermute | solution.py:45
  40.4 1.5 %collective-permute-start.15 = (bf16[512,128]{1,0:T(8,128)(2,1)S(1)}, bf16[512,128]{1,0:T(8,128)(2,1)S(1)}, u32[]{:S(2)}, u32[]{:S(2)}) collective-permute-start(bf16[512,128]{1,0:T(8,128)(2,1)S(1)} %get-tuple-element.113), channel_id=1, source_target_pairs={{0,2},{2,0},{4,6},{6,4},{8,10},{10,8},{12,14},{14,12},{1,3},{3,1},... | collective-permute-start | bytes 393224 | tf_op jit(solution)/shard_map/ppermute | solution.py:45
  41.9 2.0 %arrived_sums.1.total = f32[512,256]{1,0:T(8,128)S(1)} custom-call(s32[1]{0:T(128)} %bitcast.1.me, s32[1,4096]{1,0:T(1,128)S(1)} %copy-done.7, bf16[512,256]{1,0:T(8,128)(2,1)S(1)} %mesh_features.1.mesh_proj, f32[1,256]{1,0:T(1,128)S(1)} %bitcast.5, f32[512,256]{1,0:T(8,128)S(1)} %get-tuple-element.101.start, ...), custom_call_target="tpu_custom_call" | custom-call | tf_op jit(solution)/shard_map/arrived_sums/pallas_call | solution.py:49
  44.0 0.9 %own_mirror_sums.2.total = f32[512,128]{1,0:T(8,128)S(1)} custom-call(bf16[2048,1024]{1,0:T(8,128)(2,1)S(1)} %pick.1, bf16[1088,128]{1,0:T(8,128)(2,1)S(1)} %collective-permute-done.4.mirrored, bf16[512,2048]{1,0:T(8,128)(2,1)S(1)} %get-tuple-element.99.into, f32[2048,256]{1,0:T(8,128)S(1)} %get-tuple-element.100.term, f32[512,256]{1,0:T(8,128)S(1)} %arrived_sums.1.total), custom_call_target="tpu_custom_call" | custom-call | tf_op jit(solution)/shard_map/own_mirror_sums/pallas_call | solution.py:49
  44.9 0.9 %own_mirror_sums.3.total = f32[512,128]{1,0:T(8,128)S(1)} custom-call(bf16[2048,1024]{1,0:T(8,128)(2,1)S(1)} %pick.1, bf16[1024,128]{1,0:T(8,128)(2,1)S(1)} %collective-permute-done.12.mirrored, bf16[512,2048]{1,0:T(8,128)(2,1)S(1)} %get-tuple-element.99.into, f32[2048,256]{1,0:T(8,128)S(1)} %get-tuple-element.100.term, f32[512,256]{1,0:T(8,128)S(1)} %arrived_sums.1.total), custom_call_target="tpu_custom_call" | custom-call | tf_op jit(solution)/shard_map/own_mirror_sums/pallas_call | solution.py:49
  45.8 0.6 mirror_sums.2.refs_0_
  46.6 0.6 mirror_sums.3.mine
  47.3 0.5 collective-permute-start.16
  47.8 0.1 collective-permute-done.11.refs_1_
  47.9 0.4 encode_base.1
  48.3 0.5 collective-permute-done.16.other
  48.8 1.2 %encode.1 = (bf16[512,512]{1,0:T(8,128)(2,1)S(1)}, bf16[512,256]{1,0:T(8,128)(2,1)S(1)}, bf16[128,256]{1,0:T(8,128)(2,1)S(1)}, bf16[128,256]{1,0:T(8,128)(2,1)S(...) custom-call(f32[512,512]{1,0:T(8,128)S(1)} %get-tuple-element.110.ba, ...), custom_call_target="tpu_custom_call" | custom-call | tf_op jit(solution)/shard_map/encode/pallas_call | solution.py:49
  50.0 4.0 %collective-permute-start.17 = (bf16[128,256]{1,0:T(8,128)(2,1)S(1)}, bf16[128,256]{1,0:T(8,128)(2,1)S(1)}, u32[]{:S(2)}, u32[]{:S(2)}) collective-permute-start(bf16[128,256]{1,0:T(8,128)(2,1)S(1)} %get-tuple-element.123), channel_id=1, source_target_pairs={{0,14},{2,12},{4,10},{6,8},{8,6},{10,4},{12,2},{14,0},{1,15},{3,13... | collective-permute-start | bytes 196616 | tf_op jit(solution)/shard_map/ppermute | solution.py:45
  54.0 1.0 %collective-permute-start.19 = (bf16[128,256]{1,0:T(8,128)(2,1)S(1)}, bf16[128,256]{1,0:T(8,128)(2,1)S(1)}, u32[]{:S(2)}, u32[]{:S(2)}) collective-permute-start(bf16[128,256]{1,0:T(8,128)(2,1)S(1)} %get-tuple-element.125), channel_id=1, source_target_pairs={{0,10},{2,8},{4,14},{6,12},{8,2},{10,0},{12,6},{14,4},{1,11},{3,9}... | collective-permute-start | bytes 196616 | tf_op jit(solution)/shard_map/ppermute | solution.py:45
  55.0 2.7 %collective-permute-start.20 = (bf16[128,256]{1,0:T(8,128)(2,1)S(1)}, bf16[128,256]{1,0:T(8,128)(2,1)S(1)}, u32[]{:S(2)}, u32[]{:S(2)}) collective-permute-start(bf16[128,256]{1,0:T(8,128)(2,1)S(1)} %get-tuple-element.126), channel_id=1, source_target_pairs={{0,8},{2,10},{4,12},{6,14},{8,0},{10,2},{12,4},{14,6},{1,9},{3,11}... | collective-permute-start | bytes 196616 | tf_op jit(solution)/shard_map/ppermute | solution.py:45
  57.7 1.6 %collective-permute-start.21 = (bf16[128,256]{1,0:T(8,128)(2,1)S(1)}, bf16[128,256]{1,0:T(8,128)(2,1)S(1)}, u32[]{:S(2)}, u32[]{:S(2)}) collective-permute-start(bf16[128,256]{1,0:T(8,128)(2,1)S(1)} %get-tuple-element.127), channel_id=1, source_target_pairs={{0,6},{2,4},{4,2},{6,0},{8,14},{10,12},{12,10},{14,8},{1,7},{3,5},... | collective-permute-start | bytes 196616 | tf_op jit(solution)/shard_map/ppermute | solution.py:45
  59.3 0.6 collective-permute-start.22
  59.9 0.7 %collective-permute-done.18.refs_1_ = bf16[128,256]{1,0:T(8,128)(2,1)S(1)} collective-permute-done((bf16[128,256]{1,0:T(8,128)(2,1)S(1)}, bf16[128,256]{1,0:T(8,128)(2,1)S(1)}, u32[]{:S(2)}, u32[]{:S(2)}) %collective-permute-start.18) | collective-permute-done | bytes 65568 | tf_op jit(solution)/shard_map/ppermute | solution.py:45
  60.6 0.6 collective-permute-start.23
  61.2 2.1 %near_edges.1 = (f32[2048,256]{1,0:T(8,128)S(1)}, bf16[512,256]{1,0:T(8,128)(2,1)}) custom-call(s32[1]{0:T(128)} %bitcast.feat, bf16[512,512]{1,0:T(8,128)(2,1)S(1)} %get-tuple-element.115.full, bf16[512,256]{1,0:T(8,128)(2,1)S(1)} %get-tuple-element.116.send_proj, bf16[512,256]{1,0:T(8,128)(2,1)S(1)} %copy-done.3, f32[1,256]{1,0:T(1,128)S(1)} %bitcast.6, ...), custom_call_target="tpu_custom_call" | custom-call | tf_op jit(solution)/shard_map/near_edges/pallas_call | solution.py:49
  63.4 1.9 %collective-permute-done.20.refs_3_ = bf16[128,256]{1,0:T(8,128)(2,1)S(1)} collective-permute-done((bf16[128,256]{1,0:T(8,128)(2,1)S(1)}, bf16[128,256]{1,0:T(8,128)(2,1)S(1)}, u32[]{:S(2)}, u32[]{:S(2)}) %collective-permute-start.20) | collective-permute-done | bytes 65568 | tf_op jit(solution)/shard_map/ppermute | solution.py:45
  65.3 0.4 collective-permute-done.22.refs_5_
  65.7 2.3 %edge_sums.1.mine = bf16[512,256]{1,0:T(8,128)(2,1)S(1)} custom-call(f32[2048,256]{1,0:T(8,128)S(1)} %get-tuple-element.120.near, bf16[2048,1024]{1,0:T(8,128)(2,1)S(1)} %get-tuple-element.121.far_pick, bf16[512,2048]{1,0:T(8,128)(2,1)S(1)} %get-tuple-element.122.into, bf16[128,256]{1,0:T(8,128)(2,1)S(1)} %collective-permute-done.17.refs_0_, ...), custom_call_target="tpu_custom_call" | custom-call | tf_op jit(solution)/shard_map/edge_sums/pallas_call | solution.py:49
  68.1 0.2 own_output.1.part
  68.4 1.3 %collective-permute-done.24.other = bf16[512,256]{1,0:T(8,128)(2,1)S(1)} collective-permute-done((bf16[512,256]{1,0:T(8,128)(2,1)S(1)}, bf16[512,256]{1,0:T(8,128)(2,1)S(1)}, u32[]{:S(2)}, u32[]{:S(2)}) %collective-permute-start.24) | collective-permute-done | bytes 262176 | tf_op jit(solution)/shard_map/ppermute | solution.py:41
  69.7 0.9 %output.1 = bf16[512,256]{1,0:T(8,128)(2,1)} custom-call(f32[512,256]{1,0:T(8,128)S(1)} %own_output.1.part, bf16[512,256]{1,0:T(8,128)(2,1)S(1)} %collective-permute-done.24.other, bf16[512,256]{1,0:T(8,128)(2,1)S(1)} %get-tuple-element.131.w_out), custom_call_target="tpu_custom_call" | custom-call | tf_op jit(solution)/shard_map/output/pallas_call | solution.py:49
  (49 shorter events, 0.5 us)
Async XLA Ops:
  0.6 12.3 %copy-start.1 = (bf16[512,256]{1,0:T(8,128)(2,1)S(1)}, bf16[512,256]{1,0:T(8,128)(2,1)}, u32[]{:S(2)}) copy-start(bf16[512,256]{1,0:T(8,128)(2,1)} %refs_2_) | copy-start | bytes 786436
  0.6 12.6 %copy-start.8 = (s32[1,4096]{1,0:T(1,128)S(1)}, s32[1,4096]{1,0:T(1,128)}, u32[]{:S(2)}) copy-start(s32[1,4096]{1,0:T(1,128)} %send.2) | copy-start | bytes 49156
  0.7 12.6 %copy-start.7 = (s32[1,4096]{1,0:T(1,128)S(1)}, s32[1,4096]{1,0:T(1,128)}, u32[]{:S(2)}) copy-start(s32[1,4096]{1,0:T(1,128)} %recv.1) | copy-start | bytes 49156
  0.7 12.2 %copy-start.5 = (bf16[512,256]{1,0:T(8,128)(2,1)S(1)}, bf16[512,256]{1,0:T(8,128)(2,1)}, u32[]{:S(2)}) copy-start(bf16[512,256]{1,0:T(8,128)(2,1)} %w_recv.1) | copy-start | bytes 786436
  0.7 12.5 %copy-start.10 = (s32[16,128]{1,0:T(8,128)S(1)}, s32[16,128]{1,0:T(8,128)}, u32[]{:S(2)}) copy-start(s32[16,128]{1,0:T(8,128)} %dst.1) | copy-start | bytes 24580
  0.7 12.5 %copy-start.9 = (s32[16,128]{1,0:T(8,128)S(1)}, s32[16,128]{1,0:T(8,128)}, u32[]{:S(2)}) copy-start(s32[16,128]{1,0:T(8,128)} %src.1) | copy-start | bytes 24580
  0.7 12.5 %copy-start.11 = (s32[1,1024]{1,0:T(1,128)S(1)}, s32[1,1024]{1,0:T(1,128)}, u32[]{:S(2)}) copy-start(s32[1,1024]{1,0:T(1,128)} %halo_rows.1) | copy-start | bytes 12292
  0.7 12.5 %copy-start.12 = (f32[256]{0:T(256)S(1)}, f32[256]{0:T(256)}, u32[]{:S(2)}) copy-start(f32[256]{0:T(256)} %param.19) | copy-start | bytes 3076
  0.7 2.7 %collective-permute-start = (bf16[1024,256]{1,0:T(8,128)(2,1)}, bf16[1024,256]{1,0:T(8,128)(2,1)S(1)}, u32[]{:S(2)}, u32[]{:S(2)}) collective-permute-start(bf16[1024,256]{1,0:T(8,128)(2,1)} %grid.1), channel_id=1, source_target_pairs={{0,1},{1,0},{2,3},{3,2},{4,5},{5,4},{6,7},{7,6},{8,9},{9,8},{10,11... | collective-permute-start | bytes 1572872 | tf_op jit(solution)/shard_map/ppermute | solution.py:41
  1.2 2.8 %collective-permute-start.1 = (bf16[512,256]{1,0:T(8,128)(2,1)}, bf16[512,256]{1,0:T(8,128)(2,1)S(1)}, u32[]{:S(2)}, u32[]{:S(2)}) collective-permute-start(bf16[512,256]{1,0:T(8,128)(2,1)} %refs_2_), channel_id=1, source_target_pairs={{0,1},{1,0},{2,3},{3,2},{4,5},{5,4},{6,7},{7,6},{8,9},{9,8},{10,11... | collective-permute-start | bytes 786440 | tf_op jit(solution)/shard_map/ppermute | solution.py:41
  1.3 2.7 %collective-permute-start.3 = (bf16[256,512]{1,0:T(8,128)(2,1)}, bf16[256,512]{1,0:T(8,128)(2,1)S(1)}, u32[]{:S(2)}, u32[]{:S(2)}) collective-permute-start(bf16[256,512]{1,0:T(8,128)(2,1)} %refs_6_.1), channel_id=1, source_target_pairs={{0,1},{1,0},{2,3},{3,2},{4,5},{5,4},{6,7},{7,6},{8,9},{9,8},{10,11... | collective-permute-start | bytes 786440 | tf_op jit(solution)/shard_map/ppermute | solution.py:41
  1.7 2.4 %collective-permute-start.2 = (bf16[256,512]{1,0:T(8,128)(2,1)}, bf16[256,512]{1,0:T(8,128)(2,1)S(1)}, u32[]{:S(2)}, u32[]{:S(2)}) collective-permute-start(bf16[256,512]{1,0:T(8,128)(2,1)} %w_own.1), channel_id=1, source_target_pairs={{0,1},{1,0},{2,3},{3,2},{4,5},{5,4},{6,7},{7,6},{8,9},{9,8},{10,11... | collective-permute-start | bytes 786440 | tf_op jit(solution)/shard_map/ppermute | solution.py:41
  5.6 17.5 %collective-permute-start.4 = (bf16[1088,128]{1,0:T(8,128)(2,1)S(1)}, bf16[1088,128]{1,0:T(8,128)(2,1)S(1)}, u32[]{:S(2)}, u32[]{:S(2)}) collective-permute-start(bf16[1088,128]{1,0:T(8,128)(2,1)S(1)} %get-tuple-element.97), channel_id=1, source_target_pairs={{0,8},{2,10},{4,12},{6,14},{8,0},{10,2},{12,4},{14,6},{1,9},{3,11}... | collective-permute-start | bytes 835592 | tf_op jit(solution)/shard_map/ppermute | solution.py:45
  9.6 28.3 %collective-permute-start.5 = (bf16[512,256]{1,0:T(8,128)(2,1)S(1)}, bf16[512,256]{1,0:T(8,128)(2,1)S(1)}, u32[]{:S(2)}, u32[]{:S(2)}) collective-permute-start(bf16[512,256]{1,0:T(8,128)(2,1)S(1)} %get-tuple-element.102), channel_id=1, source_target_pairs={{0,6},{2,4},{4,2},{6,0},{8,14},{10,12},{12,10},{14,8},{1,7},{3,5},... | collective-permute-start | bytes 786440 | tf_op jit(solution)/shard_map/ppermute | solution.py:45
  12.1 25.8 %collective-permute-start.6 = (bf16[512,256]{1,0:T(8,128)(2,1)S(1)}, bf16[512,256]{1,0:T(8,128)(2,1)S(1)}, u32[]{:S(2)}, u32[]{:S(2)}) collective-permute-start(bf16[512,256]{1,0:T(8,128)(2,1)S(1)} %get-tuple-element.103), channel_id=1, source_target_pairs={{0,4},{2,6},{4,0},{6,2},{8,12},{10,14},{12,8},{14,10},{1,5},{3,7},... | collective-permute-start | bytes 786440 | tf_op jit(solution)/shard_map/ppermute | solution.py:45
  12.6 21.1 %collective-permute-start.12 = (bf16[1024,128]{1,0:T(8,128)(2,1)S(1)}, bf16[1024,128]{1,0:T(8,128)(2,1)S(1)}, u32[]{:S(2)}, u32[]{:S(2)}) collective-permute-start(bf16[1024,128]{1,0:T(8,128)(2,1)S(1)} %get-tuple-element.85.g1), channel_id=1, source_target_pairs={{0,8},{2,10},{4,12},{6,14},{8,0},{10,2},{12,4},{14,6},{1,9},{3,11}... | collective-permute-start | bytes 786440 | tf_op jit(solution)/shard_map/ppermute | solution.py:45
  18.7 19.8 %collective-permute-start.7 = (bf16[512,256]{1,0:T(8,128)(2,1)S(1)}, bf16[512,256]{1,0:T(8,128)(2,1)S(1)}, u32[]{:S(2)}, u32[]{:S(2)}) collective-permute-start(bf16[512,256]{1,0:T(8,128)(2,1)S(1)} %get-tuple-element.104), channel_id=1, source_target_pairs={{0,2},{2,0},{4,6},{6,4},{8,10},{10,8},{12,14},{14,12},{1,3},{3,1},... | collective-permute-start | bytes 786440 | tf_op jit(solution)/shard_map/ppermute | solution.py:45
  25.1 15.3 %collective-permute-start.8 = (bf16[512,128]{1,0:T(8,128)(2,1)S(1)}, bf16[512,128]{1,0:T(8,128)(2,1)S(1)}, u32[]{:S(2)}, u32[]{:S(2)}) collective-permute-start(bf16[512,128]{1,0:T(8,128)(2,1)S(1)} %get-tuple-element.105), channel_id=1, source_target_pairs={{0,6},{2,4},{4,2},{6,0},{8,14},{10,12},{12,10},{14,8},{1,7},{3,5},... | collective-permute-start | bytes 393224 | tf_op jit(solution)/shard_map/ppermute | solution.py:45
  34.6 12.0 %collective-permute-start.13 = (bf16[512,128]{1,0:T(8,128)(2,1)S(1)}, bf16[512,128]{1,0:T(8,128)(2,1)S(1)}, u32[]{:S(2)}, u32[]{:S(2)}) collective-permute-start(bf16[512,128]{1,0:T(8,128)(2,1)S(1)} %get-tuple-element.111), channel_id=1, source_target_pairs={{0,6},{2,4},{4,2},{6,0},{8,14},{10,12},{12,10},{14,8},{1,7},{3,5},... | collective-permute-start | bytes 393224 | tf_op jit(solution)/shard_map/ppermute | solution.py:45
  37.9 7.9 %collective-permute-start.9 = (bf16[512,128]{1,0:T(8,128)(2,1)S(1)}, bf16[512,128]{1,0:T(8,128)(2,1)S(1)}, u32[]{:S(2)}, u32[]{:S(2)}) collective-permute-start(bf16[512,128]{1,0:T(8,128)(2,1)S(1)} %get-tuple-element.106), channel_id=1, source_target_pairs={{0,4},{2,6},{4,0},{6,2},{8,12},{10,14},{12,8},{14,10},{1,5},{3,7},... | collective-permute-start | bytes 393224 | tf_op jit(solution)/shard_map/ppermute | solution.py:45
  37.9 7.9 %collective-permute-start.10 = (bf16[512,128]{1,0:T(8,128)(2,1)S(1)}, bf16[512,128]{1,0:T(8,128)(2,1)S(1)}, u32[]{:S(2)}, u32[]{:S(2)}) collective-permute-start(bf16[512,128]{1,0:T(8,128)(2,1)S(1)} %get-tuple-element.107), channel_id=1, source_target_pairs={{0,2},{2,0},{4,6},{6,4},{8,10},{10,8},{12,14},{14,12},{1,3},{3,1},... | collective-permute-start | bytes 393224 | tf_op jit(solution)/shard_map/ppermute | solution.py:45
  38.5 8.0 %collective-permute-start.14 = (bf16[512,128]{1,0:T(8,128)(2,1)S(1)}, bf16[512,128]{1,0:T(8,128)(2,1)S(1)}, u32[]{:S(2)}, u32[]{:S(2)}) collective-permute-start(bf16[512,128]{1,0:T(8,128)(2,1)S(1)} %get-tuple-element.112), channel_id=1, source_target_pairs={{0,4},{2,6},{4,0},{6,2},{8,12},{10,14},{12,8},{14,10},{1,5},{3,7},... | collective-permute-start | bytes 393224 | tf_op jit(solution)/shard_map/ppermute | solution.py:45
  40.4 6.1 %collective-permute-start.15 = (bf16[512,128]{1,0:T(8,128)(2,1)S(1)}, bf16[512,128]{1,0:T(8,128)(2,1)S(1)}, u32[]{:S(2)}, u32[]{:S(2)}) collective-permute-start(bf16[512,128]{1,0:T(8,128)(2,1)S(1)} %get-tuple-element.113), channel_id=1, source_target_pairs={{0,2},{2,0},{4,6},{6,4},{8,10},{10,8},{12,14},{14,12},{1,3},{3,1},... | collective-permute-start | bytes 393224 | tf_op jit(solution)/shard_map/ppermute | solution.py:45
  46.4 1.5 %copy-start = (bf16[256,512]{1,0:T(8,128)(2,1)S(1)}, bf16[256,512]{1,0:T(8,128)(2,1)}, u32[]{:S(2)}) copy-start(bf16[256,512]{1,0:T(8,128)(2,1)} %w_own.1) | copy-start | bytes 786436
  46.5 1.4 %copy-start.6 = (bf16[256,512]{1,0:T(8,128)(2,1)S(1)}, bf16[256,512]{1,0:T(8,128)(2,1)}, u32[]{:S(2)}) copy-start(bf16[256,512]{1,0:T(8,128)(2,1)} %refs_6_.1) | copy-start | bytes 786436
  46.5 2.3 %copy-start.2 = (bf16[512,256]{1,0:T(8,128)(2,1)S(1)}, bf16[512,256]{1,0:T(8,128)(2,1)}, u32[]{:S(2)}) copy-start(bf16[512,256]{1,0:T(8,128)(2,1)} %w_send.3) | copy-start | bytes 786436
  46.5 1.4 %collective-permute-start.11 = (bf16[512,128]{1,0:T(8,128)(2,1)S(1)}, bf16[512,128]{1,0:T(8,128)(2,1)S(1)}, u32[]{:S(2)}, u32[]{:S(2)}) collective-permute-start(bf16[512,128]{1,0:T(8,128)(2,1)S(1)} %mirror_sums.2.refs_0_), channel_id=1, source_target_pairs={{0,1},{1,0},{2,3},{3,2},{4,5},{5,4},{6,7},{7,6},{8,9},{9,8},{10,11... | collective-permute-start | bytes 393224 | tf_op jit(solution)/shard_map/ppermute | solution.py:41
  47.2 14.0 %copy-start.3 = (bf16[512,256]{1,0:T(8,128)(2,1)S(1)}, bf16[512,256]{1,0:T(8,128)(2,1)}, u32[]{:S(2)}) copy-start(bf16[512,256]{1,0:T(8,128)(2,1)} %w_recv.2) | copy-start | bytes 786436
  47.2 14.0 %copy-start.13 = (f32[256]{0:T(256)S(1)}, f32[256]{0:T(256)}, u32[]{:S(2)}) copy-start(f32[256]{0:T(256)} %param.23) | copy-start | bytes 3076
  47.3 1.5 %collective-permute-start.16 = (bf16[512,128]{1,0:T(8,128)(2,1)S(1)}, bf16[512,128]{1,0:T(8,128)(2,1)S(1)}, u32[]{:S(2)}, u32[]{:S(2)}) collective-permute-start(bf16[512,128]{1,0:T(8,128)(2,1)S(1)} %mirror_sums.3.mine), channel_id=1, source_target_pairs={{0,1},{1,0},{2,3},{3,2},{4,5},{5,4},{6,7},{7,6},{8,9},{9,8},{10,11... | collective-permute-start | bytes 393224 | tf_op jit(solution)/shard_map/ppermute | solution.py:41
  50.0 9.3 %collective-permute-start.17 = (bf16[128,256]{1,0:T(8,128)(2,1)S(1)}, bf16[128,256]{1,0:T(8,128)(2,1)S(1)}, u32[]{:S(2)}, u32[]{:S(2)}) collective-permute-start(bf16[128,256]{1,0:T(8,128)(2,1)S(1)} %get-tuple-element.123), channel_id=1, source_target_pairs={{0,14},{2,12},{4,10},{6,8},{8,6},{10,4},{12,2},{14,0},{1,15},{3,13... | collective-permute-start | bytes 196616 | tf_op jit(solution)/shard_map/ppermute | solution.py:45
  54.0 6.6 %collective-permute-start.18 = (bf16[128,256]{1,0:T(8,128)(2,1)S(1)}, bf16[128,256]{1,0:T(8,128)(2,1)S(1)}, u32[]{:S(2)}, u32[]{:S(2)}) collective-permute-start(bf16[128,256]{1,0:T(8,128)(2,1)S(1)} %get-tuple-element.124), channel_id=1, source_target_pairs={{0,12},{2,14},{4,8},{6,10},{8,4},{10,6},{12,0},{14,2},{1,13},{3,15... | collective-permute-start | bytes 196616 | tf_op jit(solution)/shard_map/ppermute | solution.py:45
  54.0 9.4 %collective-permute-start.19 = (bf16[128,256]{1,0:T(8,128)(2,1)S(1)}, bf16[128,256]{1,0:T(8,128)(2,1)S(1)}, u32[]{:S(2)}, u32[]{:S(2)}) collective-permute-start(bf16[128,256]{1,0:T(8,128)(2,1)S(1)} %get-tuple-element.125), channel_id=1, source_target_pairs={{0,10},{2,8},{4,14},{6,12},{8,2},{10,0},{12,6},{14,4},{1,11},{3,9}... | collective-permute-start | bytes 196616 | tf_op jit(solution)/shard_map/ppermute | solution.py:45
  55.0 10.3 %collective-permute-start.20 = (bf16[128,256]{1,0:T(8,128)(2,1)S(1)}, bf16[128,256]{1,0:T(8,128)(2,1)S(1)}, u32[]{:S(2)}, u32[]{:S(2)}) collective-permute-start(bf16[128,256]{1,0:T(8,128)(2,1)S(1)} %get-tuple-element.126), channel_id=1, source_target_pairs={{0,8},{2,10},{4,12},{6,14},{8,0},{10,2},{12,4},{14,6},{1,9},{3,11}... | collective-permute-start | bytes 196616 | tf_op jit(solution)/shard_map/ppermute | solution.py:45
  57.7 7.6 %collective-permute-start.21 = (bf16[128,256]{1,0:T(8,128)(2,1)S(1)}, bf16[128,256]{1,0:T(8,128)(2,1)S(1)}, u32[]{:S(2)}, u32[]{:S(2)}) collective-permute-start(bf16[128,256]{1,0:T(8,128)(2,1)S(1)} %get-tuple-element.127), channel_id=1, source_target_pairs={{0,6},{2,4},{4,2},{6,0},{8,14},{10,12},{12,10},{14,8},{1,7},{3,5},... | collective-permute-start | bytes 196616 | tf_op jit(solution)/shard_map/ppermute | solution.py:45
  59.3 6.4 %collective-permute-start.22 = (bf16[128,256]{1,0:T(8,128)(2,1)S(1)}, bf16[128,256]{1,0:T(8,128)(2,1)S(1)}, u32[]{:S(2)}, u32[]{:S(2)}) collective-permute-start(bf16[128,256]{1,0:T(8,128)(2,1)S(1)} %get-tuple-element.128), channel_id=1, source_target_pairs={{0,4},{2,6},{4,0},{6,2},{8,12},{10,14},{12,8},{14,10},{1,5},{3,7},... | collective-permute-start | bytes 196616 | tf_op jit(solution)/shard_map/ppermute | solution.py:45
  60.6 5.1 %collective-permute-start.23 = (bf16[128,256]{1,0:T(8,128)(2,1)S(1)}, bf16[128,256]{1,0:T(8,128)(2,1)S(1)}, u32[]{:S(2)}, u32[]{:S(2)}) collective-permute-start(bf16[128,256]{1,0:T(8,128)(2,1)S(1)} %get-tuple-element.129), channel_id=1, source_target_pairs={{0,2},{2,0},{4,6},{6,4},{8,10},{10,8},{12,14},{14,12},{1,3},{3,1},... | collective-permute-start | bytes 196616 | tf_op jit(solution)/shard_map/ppermute | solution.py:45
  65.7 2.4 %copy-start.4 = (bf16[512,256]{1,0:T(8,128)(2,1)S(1)}, bf16[512,256]{1,0:T(8,128)(2,1)}, u32[]{:S(2)}) copy-start(bf16[512,256]{1,0:T(8,128)(2,1)} %get-tuple-element.65.encoded) | copy-start | bytes 786436
  68.1 1.6 %collective-permute-start.24 = (bf16[512,256]{1,0:T(8,128)(2,1)S(1)}, bf16[512,256]{1,0:T(8,128)(2,1)S(1)}, u32[]{:S(2)}, u32[]{:S(2)}) collective-permute-start(bf16[512,256]{1,0:T(8,128)(2,1)S(1)} %edge_sums.1.mine), channel_id=1, source_target_pairs={{0,1},{1,0},{2,3},{3,2},{4,5},{5,4},{6,7},{7,6},{8,9},{9,8},{10,11... | collective-permute-start | bytes 786440 | tf_op jit(solution)/shard_map/ppermute | solution.py:41

commit v6 on v5

--- a/solution.py
+++ b/solution.py
@@ -182,11 +182,11 @@
             out[at : at + LANES, width:] = dot(hot, g1[...]).astype(BF16)
 
 
-def prepare_kernel(half, me, recv, mesh_proj, bias, into, term):
-    cap = term.shape[0] // half
-    for k in range(half):
-        rows = slots_of(recv, me[0] ^ k ^ half, cap)
-        first = k * cap
+def prepare_kernel(half, bits, me, recv, mesh_proj, bias, into, term):
+    cap = term.shape[0] // len(bits)
+    for n, k in enumerate(bits):
+        rows = slots_of(recv, me[0] ^ k, cap)
+        first = n * cap
         into[:, first : first + cap] = (iota((into.shape[0], cap), 0) == rows).astype(BF16)
         for at in range(0, cap, LANES):
             here = slice(first + at, first + at + LANES)
@@ -197,8 +197,12 @@
     packed, sums, into, term, *selections = outs
     pack_own_kernel((1,), me, list_rows, g0, g1, packed)
     local_sums_kernel(cap, me, send, recv, g0, g1, mesh_proj, bias, sums)
-    prepare_kernel(half, me, recv, mesh_proj, bias, into, term)
+    prepare_kernel(half, slot_order(half), me, recv, mesh_proj, bias, into, term)
     select_kernel(blocks, me, halo_rows, src, dst, *selections)
+
+
+def slot_order(half):
+    return [k ^ half for k in range(half)] + list(range(1, half))
 
 
 def pick_kernel(half, me, mirrored, pick, ids):
@@ -227,12 +231,14 @@
     out[...] = add_slots(0.0, grid, rows, mesh_proj, bias)
 
 
-def arrived_sums_kernel(cap, me, recv, mesh_proj, bias, start, *refs):
+def arrived_sums_kernel(first, into, term, *refs):
     *blocks, out = refs
     blocks.reverse()
-    total = start[...]
-    for k, block in enumerate(blocks, 1):
-        total = add_slots(total, block[...].astype(F32), slots_of(recv, me[0] ^ k, cap), mesh_proj, bias)
+    cap = blocks[0].shape[0]
+    total = 0.0
+    for k, block in enumerate(blocks):
+        rows = slice(first + k * cap, first + (k + 1) * cap)
+        total += dot(into[:, rows], silu_bf16(block[...].astype(F32) + term[rows, :]))
     out[...] = total
 
 
@@ -242,21 +248,22 @@
         out[...] = dot(pick[k * cap : (k + 1) * cap, :], mirrored[: pick.shape[1], :]).astype(BF16)
 
 
-def mirror_sums_kernel(chunk, first, pick, mirrored, into, term, total, *refs):
+def own_mirror_sums_kernel(chunk, pick, mirrored, into, term, own, out):
+    width, cap = out.shape[1], pick.shape[0] // 4
+    lanes = slice(chunk * width, (chunk + 1) * width)
+    grid = dot(pick[:cap, :], mirrored[: pick.shape[1], :])
+    out[...] = own[:, lanes] + dot(into[:, :cap], silu_bf16(grid + term[:cap, lanes]))
+
+
+def mirror_sums_kernel(chunk, into, term, total, arrived, *refs):
     *blocks, out = refs
-    width = out.shape[1]
+    blocks.reverse()
+    width, cap = out.shape[1], blocks[0].shape[0]
     lanes = slice(chunk * width, (chunk + 1) * width)
-    cap = into.shape[1] // 4
-    if first:
-        blocks = [dot(pick[:cap, :], mirrored[: pick.shape[1], :])]
-        sums = total[:, lanes]
-    else:
-        blocks.reverse()
-        sums = total[...]
-    for k, block in enumerate(blocks, 0 if first else 1):
+    sums = total[...] + arrived[:, lanes]
+    for k, block in enumerate(blocks, 1):
         rows = slice(k * cap, (k + 1) * cap)
-        hidden = silu_bf16(block[...].astype(F32) + term[rows, lanes])
-        sums += dot(into[:, rows], hidden)
+        sums += dot(into[:, rows], silu_bf16(block[...].astype(F32) + term[rows, lanes]))
     out[...] = sums.astype(out.dtype)
 
 
@@ -291,8 +298,8 @@
         [
             shape_of((cap, hidden), BF16),
             shape_of((mesh_rows, hidden), F32),
-            shape_of((mesh_rows, half * cap), BF16),
-            shape_of((half * cap, hidden), F32),
+            shape_of((mesh_rows, len(slot_order(half)) * cap), BF16),
+            shape_of((len(slot_order(half)) * cap, hidden), F32),
             *selection_shapes,
         ],
         me,
@@ -319,16 +326,12 @@
         scratch=[pltpu.VMEM((send_grid.shape[1] // LANES, LANES), I32)],
         name="pick",
     )
-    own = call(
-        functools.partial(arrived_sums_kernel, cap),
+    from_half = call(
+        functools.partial(arrived_sums_kernel, half * cap),
         shape_of((mesh_rows, hidden), F32),
-        me,
-        recv_row,
-        mesh_rproj,
-        bias,
-        own,
+        into,
+        term,
         *arrived[::-1],
-        specs=[SMEM] + [VMEM] * (4 + len(arrived)),
         name="arrived_sums",
     )
     chunks = []
@@ -338,7 +341,7 @@
         )
         blocks = [from_xor(block, k, n_dom) for k, block in enumerate(blocks, 1)]
         total = call(
-            functools.partial(mirror_sums_kernel, c, True),
+            functools.partial(own_mirror_sums_kernel, c),
             shape_of((mesh_rows, width), F32),
             pick,
             mirrored[c],
@@ -349,13 +352,12 @@
         )
         chunks.append(
             call(
-                functools.partial(mirror_sums_kernel, c, False),
+                functools.partial(mirror_sums_kernel, c),
                 shape_of((mesh_rows, width), BF16),
-                pick,
-                mirrored[c],
                 into,
                 term,
                 total,
+                from_half,
                 *blocks[::-1],
                 name="mirror_sums",
             )
@@ -488,8 +490,8 @@
     hidden = w_grid_send.shape[1]
     halves = n_dom == 8
     grid_chunks, list_rows = project(grid_lat, w_grid_send, send_grid, 2 if halves else 1)
-    grid_chunks, list_rows, send_grid, recv_row, mesh_lat, mesh_other, w_other, w2_other = lax.optimization_barrier(
-        (grid_chunks, list_rows, send_grid, recv_row, mesh_lat, swap(mesh_lat), swap(w_grid_out), swap(w_edge_out))
+    grid_chunks, list_rows, send_grid, recv_row, mesh_lat, mesh_other = lax.optimization_barrier(
+        (grid_chunks, list_rows, send_grid, recv_row, mesh_lat, swap(mesh_lat))
     )
     mesh = (mesh_lat, mesh_other, w_grid_recv)
     me, feat = position("dom"), position("feat")
@@ -508,6 +510,8 @@
     sums = sums_by_halves if halves else sums_by_all_to_all
     lists = (halo_rows, edge_src, edge_dst)
     chunks, selections = sums(grid_chunks, list_rows, mesh, g2m_bias, send_grid, recv_row, n_dom, select, lists)
+    selections, w_grid_out, w_edge_out = lax.optimization_barrier((selections, w_grid_out, w_edge_out))
+    w_other, w2_other = swap(w_grid_out), swap(w_edge_out)
     pick, near_src, near_dst, far_src, into = selections
     *early, last = chunks
     base, w_out = call(

time: 70.8 us -> 70.6 us (level)
  waiting for transfers between devices: 16.3 us -> 10.2 us
  starting transfers between devices: 28.5 us -> 32.9 us
  local copies, waits for them, and re-layouts: 0.07 us -> 1.97 us
    ppermute x18, waiting for transfers between devices: 14.4 us -> 7.92 us  [from_xor(): return lax.ppermute(x, 'dom', [(i, i ^ bits) for i in range(n_dom)])]
    ppermute x18, starting transfers between devices: 26.7 us -> 31.5 us  [from_xor(): return lax.ppermute(x, 'dom', [(i, i ^ bits) for i in range(n_dom)])]
    unnamed x28 -> x30, local copies, waits for them, and re-layouts: 0.07 us -> 1.97 us
  transfers between devices with their start and end apart: 25 -> 25, of which waited for: 11 -> 12; matrix products, arithmetic and copies ran while one was open for 0% -> 0% of each run, Pallas kernels for 27% -> 26%
where the time goes in v6:
time: 70.6 us; the launch traced here: 70.3 us
  starting transfers between devices  32.9 us (47%)
  Pallas kernels  24.3 us (34%)
  waiting for transfers between devices  10.2 us (14%)
  local copies, waits for them, and re-layouts  1.97 us (3%)
  between operations  1.03 us (1%)
    ppermute x18, starting transfers between devices, from_xor(): return lax.ppermute(x, 'dom', [(i, i ^ bits) for i in range(n_dom)])  31.5 us
    pallas_call x19, Pallas kernels, call(): pl.pallas_call(kernel, out_shape=out_shape, in_specs=[VMEM] * len(args) i...  24.3 us
    ppermute x18, waiting for transfers between devices, from_xor(): return lax.ppermute(x, 'dom', [(i, i ^ bits) for i in range(n_dom)])  7.92 us
    ppermute x7, waiting for transfers between devices, swap(): return lax.ppermute(x, 'feat', [(0, 1), (1, 0)])  2.24 us
    unnamed x30, local copies, waits for them, and re-layouts  1.97 us
  transfers between devices with their start and end apart: 25, of which 12 were waited for; matrix products, arithmetic and copies ran while one was open for 0% of the time, Pallas kernels for 26%

profile of v6, /device:TPU:0, one launch (start us, length us, event | category | flops | bytes accessed | tf_op | source)
XLA Modules:
  0.0 70.3 jit_solution(9803082150733519357)
XLA Ops:
  0.7 0.5 collective-permute-start
  1.3 1.6 %own_features.1 = (f32[1024,256]{1,0:T(8,128)S(1)}, bf16[256,256]{1,0:T(8,128)(2,1)S(1)}, s32[32,128]{1,0:T(8,128)S(1)}, bf16[64,128]{1,0:T(8,128)(2,1)S(1)}) custom-call(s32[1]{0:T(128)} %bitcast.feat, bf16[1024,256]{1,0:T(8,128)(2,1)} %grid.1, bf16[512,256]{1,0:T(8,128)(2,1)} %w_send.2, s32[1,4096]{1,0:T(1,128)} %send.2), custom_call_target="tpu_custom_call" | custom-call | tf_op jit(solution)/shard_map/own_features/pallas_call | solution.py:49
  3.0 0.5 other_grid_features.1
  3.5 1.5 %pack_own.1 = (bf16[512,256]{1,0:T(8,128)(2,1)S(1)}, bf16[512,256]{1,0:T(8,128)(2,1)S(1)}) custom-call(s32[1]{0:T(128)} %bitcast.1.me, s32[32,128]{1,0:T(8,128)S(1)} %get-tuple-element.79.list_rows, bf16[1024,128]{1,0:T(8,128)(2,1)S(1)} %get-tuple-element.89.g0, bf16[1024,128]{1,0:T(8,128)(2,1)S(1)} %get-tuple-element.90.g1), custom_call_target="tpu_custom_call" | custom-call | tf_op jit(solution)/shard_map/pack_own/pallas_call | solution.py:49
  5.0 4.0 %collective-permute-start.2 = (bf16[1088,128]{1,0:T(8,128)(2,1)S(1)}, bf16[1088,128]{1,0:T(8,128)(2,1)S(1)}, u32[]{:S(2)}, u32[]{:S(2)}) collective-permute-start(bf16[1088,128]{1,0:T(8,128)(2,1)S(1)} %get-tuple-element.102), channel_id=1, source_target_pairs={{0,8},{2,10},{4,12},{6,14},{8,0},{10,2},{12,4},{14,6},{1,9},{3,11}... | collective-permute-start | bytes 835592 | tf_op jit(solution)/shard_map/ppermute | solution.py:45
  9.0 2.5 %collective-permute-start.3 = (bf16[512,256]{1,0:T(8,128)(2,1)S(1)}, bf16[512,256]{1,0:T(8,128)(2,1)S(1)}, u32[]{:S(2)}, u32[]{:S(2)}) collective-permute-start(bf16[512,256]{1,0:T(8,128)(2,1)S(1)} %get-tuple-element.107), channel_id=1, source_target_pairs={{0,6},{2,4},{4,2},{6,0},{8,14},{10,12},{12,10},{14,8},{1,7},{3,5},... | collective-permute-start | bytes 786440 | tf_op jit(solution)/shard_map/ppermute | solution.py:45
  11.5 0.3 collective-permute-start.12
  11.8 0.5 collective-permute-start.4
  12.3 0.9 %copy-done.1 = bf16[512,256]{1,0:T(8,128)(2,1)S(1)} copy-done((bf16[512,256]{1,0:T(8,128)(2,1)S(1)}, bf16[512,256]{1,0:T(8,128)(2,1)}, u32[]{:S(2)}) %copy-start.1) | copy-done | bytes 262168
  13.2 0.9 %copy-done.6 = bf16[512,256]{1,0:T(8,128)(2,1)S(1)} copy-done((bf16[512,256]{1,0:T(8,128)(2,1)S(1)}, bf16[512,256]{1,0:T(8,128)(2,1)}, u32[]{:S(2)}) %copy-start.6) | copy-done | bytes 262168
  14.6 6.4 %aside.1 = (bf16[512,256]{1,0:T(8,128)(2,1)S(1)}, f32[512,256]{1,0:T(8,128)S(1)}, bf16[512,3584]{1,0:T(8,128)(2,1)S(1)}, f32[3584,256]{1,0:T(8,128)S(1)}, bf16[1...) custom-call(s32[1]{0:T(128)} %bitcast.1.me, ...), custom_call_target="tpu_custom_call" | custom-call | tf_op jit(solution)/shard_map/aside/pallas_call | solution.py:49
  21.0 0.3 collective-permute-start.5
  21.3 1.7 %collective-permute-done.2.mirrored = bf16[1088,128]{1,0:T(8,128)(2,1)S(1)} collective-permute-done((bf16[1088,128]{1,0:T(8,128)(2,1)S(1)}, bf16[1088,128]{1,0:T(8,128)(2,1)S(1)}, u32[]{:S(2)}, u32[]{:S(2)}) %collective-permute-start.2) | collective-permute-done | bytes 278560 | tf_op jit(solution)/shard_map/ppermute | solution.py:45
  23.0 1.0 %pick.1 = bf16[2048,1024]{1,0:T(8,128)(2,1)S(1)} custom-call(s32[1]{0:T(128)} %bitcast.1.me, bf16[1088,128]{1,0:T(8,128)(2,1)S(1)} %collective-permute-done.2.mirrored), custom_call_target="tpu_custom_call" | custom-call | tf_op jit(solution)/shard_map/pick/pallas_call | solution.py:49
  24.1 1.0 %pack_mirror.2 = (bf16[512,128]{1,0:T(8,128)(2,1)S(1)}, bf16[512,128]{1,0:T(8,128)(2,1)S(1)}, bf16[512,128]{1,0:T(8,128)(2,1)S(1)}) custom-call(bf16[2048,1024]{1,0:T(8,128)(2,1)S(1)} %pick.1, bf16[1088,128]{1,0:T(8,128)(2,1)S(1)} %collective-permute-done.2.mirrored), custom_call_target="tpu_custom_call" | custom-call | tf_op jit(solution)/shard_map/pack_mirror/pallas_call | solution.py:49
  25.1 5.6 %collective-permute-start.6 = (bf16[512,128]{1,0:T(8,128)(2,1)S(1)}, bf16[512,128]{1,0:T(8,128)(2,1)S(1)}, u32[]{:S(2)}, u32[]{:S(2)}) collective-permute-start(bf16[512,128]{1,0:T(8,128)(2,1)S(1)} %get-tuple-element.110), channel_id=1, source_target_pairs={{0,6},{2,4},{4,2},{6,0},{8,14},{10,12},{12,10},{14,8},{1,7},{3,5},... | collective-permute-start | bytes 393224 | tf_op jit(solution)/shard_map/ppermute | solution.py:45
  30.7 2.1 %collective-permute-start.7 = (bf16[512,128]{1,0:T(8,128)(2,1)S(1)}, bf16[512,128]{1,0:T(8,128)(2,1)S(1)}, u32[]{:S(2)}, u32[]{:S(2)}) collective-permute-start(bf16[512,128]{1,0:T(8,128)(2,1)S(1)} %get-tuple-element.111), channel_id=1, source_target_pairs={{0,4},{2,6},{4,0},{6,2},{8,12},{10,14},{12,8},{14,10},{1,5},{3,7},... | collective-permute-start | bytes 393224 | tf_op jit(solution)/shard_map/ppermute | solution.py:45
  32.8 0.5 collective-permute-done.12.mirrored
  33.3 1.5 %collective-permute-start.8 = (bf16[512,128]{1,0:T(8,128)(2,1)S(1)}, bf16[512,128]{1,0:T(8,128)(2,1)S(1)}, u32[]{:S(2)}, u32[]{:S(2)}) collective-permute-start(bf16[512,128]{1,0:T(8,128)(2,1)S(1)} %get-tuple-element.112), channel_id=1, source_target_pairs={{0,2},{2,0},{4,6},{6,4},{8,10},{10,8},{12,14},{14,12},{1,3},{3,1},... | collective-permute-start | bytes 393224 | tf_op jit(solution)/shard_map/ppermute | solution.py:45
  34.8 1.0 %pack_mirror.3 = (bf16[512,128]{1,0:T(8,128)(2,1)S(1)}, bf16[512,128]{1,0:T(8,128)(2,1)S(1)}, bf16[512,128]{1,0:T(8,128)(2,1)S(1)}) custom-call(bf16[2048,1024]{1,0:T(8,128)(2,1)S(1)} %pick.1, bf16[1024,128]{1,0:T(8,128)(2,1)S(1)} %collective-permute-done.12.mirrored), custom_call_target="tpu_custom_call" | custom-call | tf_op jit(solution)/shard_map/pack_mirror/pallas_call | solution.py:49
  35.9 0.5 collective-permute-start.10
  36.4 1.5 %collective-permute-done.6.refs_0_ = bf16[512,128]{1,0:T(8,128)(2,1)S(1)} collective-permute-done((bf16[512,128]{1,0:T(8,128)(2,1)S(1)}, bf16[512,128]{1,0:T(8,128)(2,1)S(1)}, u32[]{:S(2)}, u32[]{:S(2)}) %collective-permute-start.6) | collective-permute-done | bytes 131104 | tf_op jit(solution)/shard_map/ppermute | solution.py:45
  38.0 1.2 %collective-permute-start.13 = (bf16[512,128]{1,0:T(8,128)(2,1)S(1)}, bf16[512,128]{1,0:T(8,128)(2,1)S(1)}, u32[]{:S(2)}, u32[]{:S(2)}) collective-permute-start(bf16[512,128]{1,0:T(8,128)(2,1)S(1)} %get-tuple-element.121), channel_id=1, source_target_pairs={{0,6},{2,4},{4,2},{6,0},{8,14},{10,12},{12,10},{14,8},{1,7},{3,5},... | collective-permute-start | bytes 393224 | tf_op jit(solution)/shard_map/ppermute | solution.py:45
  39.1 0.8 %collective-permute-done.7.refs_1_ = bf16[512,128]{1,0:T(8,128)(2,1)S(1)} collective-permute-done((bf16[512,128]{1,0:T(8,128)(2,1)S(1)}, bf16[512,128]{1,0:T(8,128)(2,1)S(1)}, u32[]{:S(2)}, u32[]{:S(2)}) %collective-permute-start.7) | collective-permute-done | bytes 131104 | tf_op jit(solution)/shard_map/ppermute | solution.py:45
  39.9 1.0 %collective-permute-start.14 = (bf16[512,128]{1,0:T(8,128)(2,1)S(1)}, bf16[512,128]{1,0:T(8,128)(2,1)S(1)}, u32[]{:S(2)}, u32[]{:S(2)}) collective-permute-start(bf16[512,128]{1,0:T(8,128)(2,1)S(1)} %get-tuple-element.122), channel_id=1, source_target_pairs={{0,4},{2,6},{4,0},{6,2},{8,12},{10,14},{12,8},{14,10},{1,5},{3,7},... | collective-permute-start | bytes 393224 | tf_op jit(solution)/shard_map/ppermute | solution.py:45
  40.9 0.8 %collective-permute-start.15 = (bf16[512,128]{1,0:T(8,128)(2,1)S(1)}, bf16[512,128]{1,0:T(8,128)(2,1)S(1)}, u32[]{:S(2)}, u32[]{:S(2)}) collective-permute-start(bf16[512,128]{1,0:T(8,128)(2,1)S(1)} %get-tuple-element.123), channel_id=1, source_target_pairs={{0,2},{2,0},{4,6},{6,4},{8,10},{10,8},{12,14},{14,12},{1,3},{3,1},... | collective-permute-start | bytes 393224 | tf_op jit(solution)/shard_map/ppermute | solution.py:45
  41.8 0.9 %own_mirror_sums.2.total = f32[512,128]{1,0:T(8,128)S(1)} custom-call(bf16[2048,1024]{1,0:T(8,128)(2,1)S(1)} %pick.1, bf16[1088,128]{1,0:T(8,128)(2,1)S(1)} %collective-permute-done.2.mirrored, bf16[512,3584]{1,0:T(8,128)(2,1)S(1)} %get-tuple-element.103.into, f32[3584,256]{1,0:T(8,128)S(1)} %get-tuple-element.104.term, f32[512,256]{1,0:T(8,128)S(1)} %get-tuple-element.106.own), custom_call_target="tpu_custom_call" | custom-call | tf_op jit(solution)/shard_map/own_mirror_sums/pallas_call | solution.py:49
  42.6 0.9 %own_mirror_sums.3.total = f32[512,128]{1,0:T(8,128)S(1)} custom-call(bf16[2048,1024]{1,0:T(8,128)(2,1)S(1)} %pick.1, bf16[1024,128]{1,0:T(8,128)(2,1)S(1)} %collective-permute-done.12.mirrored, bf16[512,3584]{1,0:T(8,128)(2,1)S(1)} %get-tuple-element.103.into, f32[3584,256]{1,0:T(8,128)S(1)} %get-tuple-element.104.term, f32[512,256]{1,0:T(8,128)S(1)} %get-tuple-element.106.own), custom_call_target="tpu_custom_call" | custom-call | tf_op jit(solution)/shard_map/own_mirror_sums/pallas_call | solution.py:49
  43.5 0.7 %arrived_sums.1.arrived = f32[512,256]{1,0:T(8,128)S(1)} custom-call(bf16[512,3584]{1,0:T(8,128)(2,1)S(1)} %get-tuple-element.103.into, f32[3584,256]{1,0:T(8,128)S(1)} %get-tuple-element.104.term, bf16[512,256]{1,0:T(8,128)(2,1)S(1)} %collective-permute-done.3.refs_0_, bf16[512,256]{1,0:T(8,128)(2,1)S(1)} %collective-permute-done.4.refs_1_, ...), custom_call_target="tpu_custom_call" | custom-call | tf_op jit(solution)/shard_map/arrived_sums/pallas_call | solution.py:49
  44.3 0.6 mirror_sums.2.refs_0_
  45.0 0.5 collective-permute-done.14.refs_1_
  45.5 0.6 collective-permute-done.15.refs_2_
  46.1 0.6 mirror_sums.3.mine
  46.9 0.4 encode_base.1
  47.3 0.9 %collective-permute-done.16.other = bf16[512,128]{1,0:T(8,128)(2,1)S(1)} collective-permute-done((bf16[512,128]{1,0:T(8,128)(2,1)S(1)}, bf16[512,128]{1,0:T(8,128)(2,1)S(1)}, u32[]{:S(2)}, u32[]{:S(2)}) %collective-permute-start.16) | collective-permute-done | bytes 131104 | tf_op jit(solution)/shard_map/ppermute | solution.py:41
  48.2 1.2 %encode.1 = (bf16[512,512]{1,0:T(8,128)(2,1)S(1)}, bf16[512,256]{1,0:T(8,128)(2,1)S(1)}, bf16[128,256]{1,0:T(8,128)(2,1)S(1)}, bf16[128,256]{1,0:T(8,128)(2,1)S(...) custom-call(f32[512,512]{1,0:T(8,128)S(1)} %get-tuple-element.120.ba, ...), custom_call_target="tpu_custom_call" | custom-call | tf_op jit(solution)/shard_map/encode/pallas_call | solution.py:49
  49.4 3.9 %collective-permute-start.17 = (bf16[128,256]{1,0:T(8,128)(2,1)S(1)}, bf16[128,256]{1,0:T(8,128)(2,1)S(1)}, u32[]{:S(2)}, u32[]{:S(2)}) collective-permute-start(bf16[128,256]{1,0:T(8,128)(2,1)S(1)} %get-tuple-element.133), channel_id=1, source_target_pairs={{0,14},{2,12},{4,10},{6,8},{8,6},{10,4},{12,2},{14,0},{1,15},{3,13... | collective-permute-start | bytes 196616 | tf_op jit(solution)/shard_map/ppermute | solution.py:45
  53.3 0.9 %collective-permute-start.18 = (bf16[128,256]{1,0:T(8,128)(2,1)S(1)}, bf16[128,256]{1,0:T(8,128)(2,1)S(1)}, u32[]{:S(2)}, u32[]{:S(2)}) collective-permute-start(bf16[128,256]{1,0:T(8,128)(2,1)S(1)} %get-tuple-element.134), channel_id=1, source_target_pairs={{0,12},{2,14},{4,8},{6,10},{8,4},{10,6},{12,0},{14,2},{1,13},{3,15... | collective-permute-start | bytes 196616 | tf_op jit(solution)/shard_map/ppermute | solution.py:45
  54.2 2.9 %collective-permute-start.20 = (bf16[128,256]{1,0:T(8,128)(2,1)S(1)}, bf16[128,256]{1,0:T(8,128)(2,1)S(1)}, u32[]{:S(2)}, u32[]{:S(2)}) collective-permute-start(bf16[128,256]{1,0:T(8,128)(2,1)S(1)} %get-tuple-element.136), channel_id=1, source_target_pairs={{0,8},{2,10},{4,12},{6,14},{8,0},{10,2},{12,4},{14,6},{1,9},{3,11}... | collective-permute-start | bytes 196616 | tf_op jit(solution)/shard_map/ppermute | solution.py:45
  57.1 1.5 %collective-permute-start.21 = (bf16[128,256]{1,0:T(8,128)(2,1)S(1)}, bf16[128,256]{1,0:T(8,128)(2,1)S(1)}, u32[]{:S(2)}, u32[]{:S(2)}) collective-permute-start(bf16[128,256]{1,0:T(8,128)(2,1)S(1)} %get-tuple-element.137), channel_id=1, source_target_pairs={{0,6},{2,4},{4,2},{6,0},{8,14},{10,12},{12,10},{14,8},{1,7},{3,5},... | collective-permute-start | bytes 196616 | tf_op jit(solution)/shard_map/ppermute | solution.py:45
  58.6 1.8 %collective-permute-start.22 = (bf16[128,256]{1,0:T(8,128)(2,1)S(1)}, bf16[128,256]{1,0:T(8,128)(2,1)S(1)}, u32[]{:S(2)}, u32[]{:S(2)}) collective-permute-start(bf16[128,256]{1,0:T(8,128)(2,1)S(1)} %get-tuple-element.138), channel_id=1, source_target_pairs={{0,4},{2,6},{4,0},{6,2},{8,12},{10,14},{12,8},{14,10},{1,5},{3,7},... | collective-permute-start | bytes 196616 | tf_op jit(solution)/shard_map/ppermute | solution.py:45
  60.4 0.6 collective-permute-start.23
  61.0 2.1 %near_edges.1 = (f32[2048,256]{1,0:T(8,128)S(1)}, bf16[512,256]{1,0:T(8,128)(2,1)}) custom-call(s32[1]{0:T(128)} %bitcast.feat, bf16[512,512]{1,0:T(8,128)(2,1)S(1)} %get-tuple-element.125.full, bf16[512,256]{1,0:T(8,128)(2,1)S(1)} %get-tuple-element.126.send_proj, bf16[512,256]{1,0:T(8,128)(2,1)S(1)} %copy-done.4, f32[1,256]{1,0:T(1,128)S(1)} %bitcast.5, ...), custom_call_target="tpu_custom_call" | custom-call | tf_op jit(solution)/shard_map/near_edges/pallas_call | solution.py:49
  63.1 1.4 %collective-permute-done.19.refs_2_ = bf16[128,256]{1,0:T(8,128)(2,1)S(1)} collective-permute-done((bf16[128,256]{1,0:T(8,128)(2,1)S(1)}, bf16[128,256]{1,0:T(8,128)(2,1)S(1)}, u32[]{:S(2)}, u32[]{:S(2)}) %collective-permute-start.19) | collective-permute-done | bytes 65568 | tf_op jit(solution)/shard_map/ppermute | solution.py:45
  64.8 0.6 collective-permute-done.22.refs_5_
  65.5 2.3 %edge_sums.1.mine = bf16[512,256]{1,0:T(8,128)(2,1)S(1)} custom-call(f32[2048,256]{1,0:T(8,128)S(1)} %get-tuple-element.130.near, bf16[2048,1024]{1,0:T(8,128)(2,1)S(1)} %get-tuple-element.131.far_pick, bf16[512,2048]{1,0:T(8,128)(2,1)S(1)} %get-tuple-element.132.into, bf16[128,256]{1,0:T(8,128)(2,1)S(1)} %collective-permute-done.17.refs_0_, ...), custom_call_target="tpu_custom_call" | custom-call | tf_op jit(solution)/shard_map/edge_sums/pallas_call | solution.py:49
  68.1 1.3 %collective-permute-done.24.other = bf16[512,256]{1,0:T(8,128)(2,1)S(1)} collective-permute-done((bf16[512,256]{1,0:T(8,128)(2,1)S(1)}, bf16[512,256]{1,0:T(8,128)(2,1)S(1)}, u32[]{:S(2)}, u32[]{:S(2)}) %collective-permute-start.24) | collective-permute-done | bytes 262176 | tf_op jit(solution)/shard_map/ppermute | solution.py:41
  69.4 0.9 %output.1 = bf16[512,256]{1,0:T(8,128)(2,1)} custom-call(f32[512,256]{1,0:T(8,128)S(1)} %own_output.1.part, bf16[512,256]{1,0:T(8,128)(2,1)S(1)} %collective-permute-done.24.other, bf16[512,256]{1,0:T(8,128)(2,1)S(1)} %get-tuple-element.141.w_out), custom_call_target="tpu_custom_call" | custom-call | tf_op jit(solution)/shard_map/output/pallas_call | solution.py:49
  (51 shorter events, 1.3 us)
Async XLA Ops:
  0.6 13.9 %copy-start.8 = (s32[1,4096]{1,0:T(1,128)S(1)}, s32[1,4096]{1,0:T(1,128)}, u32[]{:S(2)}) copy-start(s32[1,4096]{1,0:T(1,128)} %send.2) | copy-start | bytes 49156
  0.6 13.9 %copy-start.9 = (s32[1,4096]{1,0:T(1,128)S(1)}, s32[1,4096]{1,0:T(1,128)}, u32[]{:S(2)}) copy-start(s32[1,4096]{1,0:T(1,128)} %recv) | copy-start | bytes 49156
  0.7 13.9 %copy-start.11 = (s32[16,128]{1,0:T(8,128)S(1)}, s32[16,128]{1,0:T(8,128)}, u32[]{:S(2)}) copy-start(s32[16,128]{1,0:T(8,128)} %dst.1) | copy-start | bytes 24580
  0.7 13.9 %copy-start.10 = (s32[16,128]{1,0:T(8,128)S(1)}, s32[16,128]{1,0:T(8,128)}, u32[]{:S(2)}) copy-start(s32[16,128]{1,0:T(8,128)} %src.1) | copy-start | bytes 24580
  0.7 13.9 %copy-start.12 = (s32[1,1024]{1,0:T(1,128)S(1)}, s32[1,1024]{1,0:T(1,128)}, u32[]{:S(2)}) copy-start(s32[1,1024]{1,0:T(1,128)} %halo_rows.1) | copy-start | bytes 12292
  0.7 13.9 %copy-start.13 = (f32[256]{0:T(256)S(1)}, f32[256]{0:T(256)}, u32[]{:S(2)}) copy-start(f32[256]{0:T(256)} %param.19) | copy-start | bytes 3076
  0.7 2.3 %collective-permute-start = (bf16[1024,256]{1,0:T(8,128)(2,1)}, bf16[1024,256]{1,0:T(8,128)(2,1)S(1)}, u32[]{:S(2)}, u32[]{:S(2)}) collective-permute-start(bf16[1024,256]{1,0:T(8,128)(2,1)} %grid.1), channel_id=1, source_target_pairs={{0,1},{1,0},{2,3},{3,2},{4,5},{5,4},{6,7},{7,6},{8,9},{9,8},{10,11... | collective-permute-start | bytes 1572872 | tf_op jit(solution)/shard_map/ppermute | solution.py:41
  1.2 2.3 %collective-permute-start.1 = (bf16[512,256]{1,0:T(8,128)(2,1)}, bf16[512,256]{1,0:T(8,128)(2,1)S(1)}, u32[]{:S(2)}, u32[]{:S(2)}) collective-permute-start(bf16[512,256]{1,0:T(8,128)(2,1)} %refs_2_), channel_id=1, source_target_pairs={{0,1},{1,0},{2,3},{3,2},{4,5},{5,4},{6,7},{7,6},{8,9},{9,8},{10,11... | collective-permute-start | bytes 786440 | tf_op jit(solution)/shard_map/ppermute | solution.py:41
  5.0 18.0 %collective-permute-start.2 = (bf16[1088,128]{1,0:T(8,128)(2,1)S(1)}, bf16[1088,128]{1,0:T(8,128)(2,1)S(1)}, u32[]{:S(2)}, u32[]{:S(2)}) collective-permute-start(bf16[1088,128]{1,0:T(8,128)(2,1)S(1)} %get-tuple-element.102), channel_id=1, source_target_pairs={{0,8},{2,10},{4,12},{6,14},{8,0},{10,2},{12,4},{14,6},{1,9},{3,11}... | collective-permute-start | bytes 835592 | tf_op jit(solution)/shard_map/ppermute | solution.py:45
  9.0 21.7 %collective-permute-start.3 = (bf16[512,256]{1,0:T(8,128)(2,1)S(1)}, bf16[512,256]{1,0:T(8,128)(2,1)S(1)}, u32[]{:S(2)}, u32[]{:S(2)}) collective-permute-start(bf16[512,256]{1,0:T(8,128)(2,1)S(1)} %get-tuple-element.107), channel_id=1, source_target_pairs={{0,6},{2,4},{4,2},{6,0},{8,14},{10,12},{12,10},{14,8},{1,7},{3,5},... | collective-permute-start | bytes 786440 | tf_op jit(solution)/shard_map/ppermute | solution.py:45
  11.5 21.8 %collective-permute-start.12 = (bf16[1024,128]{1,0:T(8,128)(2,1)S(1)}, bf16[1024,128]{1,0:T(8,128)(2,1)S(1)}, u32[]{:S(2)}, u32[]{:S(2)}) collective-permute-start(bf16[1024,128]{1,0:T(8,128)(2,1)S(1)} %get-tuple-element.90.g1), channel_id=1, source_target_pairs={{0,8},{2,10},{4,12},{6,14},{8,0},{10,2},{12,4},{14,6},{1,9},{3,11}... | collective-permute-start | bytes 786440 | tf_op jit(solution)/shard_map/ppermute | solution.py:45
  11.8 24.0 %collective-permute-start.4 = (bf16[512,256]{1,0:T(8,128)(2,1)S(1)}, bf16[512,256]{1,0:T(8,128)(2,1)S(1)}, u32[]{:S(2)}, u32[]{:S(2)}) collective-permute-start(bf16[512,256]{1,0:T(8,128)(2,1)S(1)} %get-tuple-element.108), channel_id=1, source_target_pairs={{0,4},{2,6},{4,0},{6,2},{8,12},{10,14},{12,8},{14,10},{1,5},{3,7},... | collective-permute-start | bytes 786440 | tf_op jit(solution)/shard_map/ppermute | solution.py:45
  12.3 0.9 %copy-start.1 = (bf16[512,256]{1,0:T(8,128)(2,1)S(1)}, bf16[512,256]{1,0:T(8,128)(2,1)}, u32[]{:S(2)}) copy-start(bf16[512,256]{1,0:T(8,128)(2,1)} %refs_2_) | copy-start | bytes 786436
  13.2 0.9 %copy-start.6 = (bf16[512,256]{1,0:T(8,128)(2,1)S(1)}, bf16[512,256]{1,0:T(8,128)(2,1)}, u32[]{:S(2)}) copy-start(bf16[512,256]{1,0:T(8,128)(2,1)} %w_recv.1) | copy-start | bytes 786436
  21.0 14.9 %collective-permute-start.5 = (bf16[512,256]{1,0:T(8,128)(2,1)S(1)}, bf16[512,256]{1,0:T(8,128)(2,1)S(1)}, u32[]{:S(2)}, u32[]{:S(2)}) collective-permute-start(bf16[512,256]{1,0:T(8,128)(2,1)S(1)} %get-tuple-element.109), channel_id=1, source_target_pairs={{0,2},{2,0},{4,6},{6,4},{8,10},{10,8},{12,14},{14,12},{1,3},{3,1},... | collective-permute-start | bytes 786440 | tf_op jit(solution)/shard_map/ppermute | solution.py:45
  24.0 11.8 %copy-start.7 = (bf16[256,512]{1,0:T(8,128)(2,1)S(1)}, bf16[256,512]{1,0:T(8,128)(2,1)}, u32[]{:S(2)}) copy-start(bf16[256,512]{1,0:T(8,128)(2,1)} %refs_6_) | copy-start | bytes 786436
  24.1 11.9 %copy-start = (bf16[256,512]{1,0:T(8,128)(2,1)S(1)}, bf16[256,512]{1,0:T(8,128)(2,1)}, u32[]{:S(2)}) copy-start(bf16[256,512]{1,0:T(8,128)(2,1)} %w_own) | copy-start | bytes 786436
  25.1 12.9 %collective-permute-start.6 = (bf16[512,128]{1,0:T(8,128)(2,1)S(1)}, bf16[512,128]{1,0:T(8,128)(2,1)S(1)}, u32[]{:S(2)}, u32[]{:S(2)}) collective-permute-start(bf16[512,128]{1,0:T(8,128)(2,1)S(1)} %get-tuple-element.110), channel_id=1, source_target_pairs={{0,6},{2,4},{4,2},{6,0},{8,14},{10,12},{12,10},{14,8},{1,7},{3,5},... | collective-permute-start | bytes 393224 | tf_op jit(solution)/shard_map/ppermute | solution.py:45
  30.7 9.2 %collective-permute-start.7 = (bf16[512,128]{1,0:T(8,128)(2,1)S(1)}, bf16[512,128]{1,0:T(8,128)(2,1)S(1)}, u32[]{:S(2)}, u32[]{:S(2)}) collective-permute-start(bf16[512,128]{1,0:T(8,128)(2,1)S(1)} %get-tuple-element.111), channel_id=1, source_target_pairs={{0,4},{2,6},{4,0},{6,2},{8,12},{10,14},{12,8},{14,10},{1,5},{3,7},... | collective-permute-start | bytes 393224 | tf_op jit(solution)/shard_map/ppermute | solution.py:45
  33.3 7.6 %collective-permute-start.8 = (bf16[512,128]{1,0:T(8,128)(2,1)S(1)}, bf16[512,128]{1,0:T(8,128)(2,1)S(1)}, u32[]{:S(2)}, u32[]{:S(2)}) collective-permute-start(bf16[512,128]{1,0:T(8,128)(2,1)S(1)} %get-tuple-element.112), channel_id=1, source_target_pairs={{0,2},{2,0},{4,6},{6,4},{8,10},{10,8},{12,14},{14,12},{1,3},{3,1},... | collective-permute-start | bytes 393224 | tf_op jit(solution)/shard_map/ppermute | solution.py:45
  35.8 11.0 %collective-permute-start.11 = (bf16[256,512]{1,0:T(8,128)(2,1)S(1)}, bf16[256,512]{1,0:T(8,128)(2,1)S(1)}, u32[]{:S(2)}, u32[]{:S(2)}) collective-permute-start(bf16[256,512]{1,0:T(8,128)(2,1)S(1)} %copy-done.7), channel_id=1, source_target_pairs={{0,1},{1,0},{2,3},{3,2},{4,5},{5,4},{6,7},{7,6},{8,9},{9,8},{10,11... | collective-permute-start | bytes 786440 | tf_op jit(solution)/shard_map/ppermute | solution.py:41
  35.9 10.9 %collective-permute-start.10 = (bf16[256,512]{1,0:T(8,128)(2,1)S(1)}, bf16[256,512]{1,0:T(8,128)(2,1)S(1)}, u32[]{:S(2)}, u32[]{:S(2)}) collective-permute-start(bf16[256,512]{1,0:T(8,128)(2,1)S(1)} %copy-done), channel_id=1, source_target_pairs={{0,1},{1,0},{2,3},{3,2},{4,5},{5,4},{6,7},{7,6},{8,9},{9,8},{10,11... | collective-permute-start | bytes 786440 | tf_op jit(solution)/shard_map/ppermute | solution.py:41
  38.0 7.0 %collective-permute-start.13 = (bf16[512,128]{1,0:T(8,128)(2,1)S(1)}, bf16[512,128]{1,0:T(8,128)(2,1)S(1)}, u32[]{:S(2)}, u32[]{:S(2)}) collective-permute-start(bf16[512,128]{1,0:T(8,128)(2,1)S(1)} %get-tuple-element.121), channel_id=1, source_target_pairs={{0,6},{2,4},{4,2},{6,0},{8,14},{10,12},{12,10},{14,8},{1,7},{3,5},... | collective-permute-start | bytes 393224 | tf_op jit(solution)/shard_map/ppermute | solution.py:45
  39.9 5.6 %collective-permute-start.14 = (bf16[512,128]{1,0:T(8,128)(2,1)S(1)}, bf16[512,128]{1,0:T(8,128)(2,1)S(1)}, u32[]{:S(2)}, u32[]{:S(2)}) collective-permute-start(bf16[512,128]{1,0:T(8,128)(2,1)S(1)} %get-tuple-element.122), channel_id=1, source_target_pairs={{0,4},{2,6},{4,0},{6,2},{8,12},{10,14},{12,8},{14,10},{1,5},{3,7},... | collective-permute-start | bytes 393224 | tf_op jit(solution)/shard_map/ppermute | solution.py:45
  40.9 5.2 %collective-permute-start.15 = (bf16[512,128]{1,0:T(8,128)(2,1)S(1)}, bf16[512,128]{1,0:T(8,128)(2,1)S(1)}, u32[]{:S(2)}, u32[]{:S(2)}) collective-permute-start(bf16[512,128]{1,0:T(8,128)(2,1)S(1)} %get-tuple-element.123), channel_id=1, source_target_pairs={{0,2},{2,0},{4,6},{6,4},{8,10},{10,8},{12,14},{14,12},{1,3},{3,1},... | collective-permute-start | bytes 393224 | tf_op jit(solution)/shard_map/ppermute | solution.py:45
  44.9 2.0 %copy-start.2 = (bf16[512,256]{1,0:T(8,128)(2,1)S(1)}, bf16[512,256]{1,0:T(8,128)(2,1)}, u32[]{:S(2)}) copy-start(bf16[512,256]{1,0:T(8,128)(2,1)} %refs_2_) | copy-start | bytes 786436
  44.9 3.3 %copy-start.3 = (bf16[512,256]{1,0:T(8,128)(2,1)S(1)}, bf16[512,256]{1,0:T(8,128)(2,1)}, u32[]{:S(2)}) copy-start(bf16[512,256]{1,0:T(8,128)(2,1)} %w_send.3) | copy-start | bytes 786436
  45.0 1.9 %collective-permute-start.9 = (bf16[512,128]{1,0:T(8,128)(2,1)S(1)}, bf16[512,128]{1,0:T(8,128)(2,1)S(1)}, u32[]{:S(2)}, u32[]{:S(2)}) collective-permute-start(bf16[512,128]{1,0:T(8,128)(2,1)S(1)} %mirror_sums.2.refs_0_), channel_id=1, source_target_pairs={{0,1},{1,0},{2,3},{3,2},{4,5},{5,4},{6,7},{7,6},{8,9},{9,8},{10,11... | collective-permute-start | bytes 393224 | tf_op jit(solution)/shard_map/ppermute | solution.py:41
  46.8 14.3 %copy-start.4 = (bf16[512,256]{1,0:T(8,128)(2,1)S(1)}, bf16[512,256]{1,0:T(8,128)(2,1)}, u32[]{:S(2)}) copy-start(bf16[512,256]{1,0:T(8,128)(2,1)} %w_recv.2) | copy-start | bytes 786436
  46.8 14.2 %copy-start.14 = (f32[256]{0:T(256)S(1)}, f32[256]{0:T(256)}, u32[]{:S(2)}) copy-start(f32[256]{0:T(256)} %param.23) | copy-start | bytes 3076
  46.8 1.4 %collective-permute-start.16 = (bf16[512,128]{1,0:T(8,128)(2,1)S(1)}, bf16[512,128]{1,0:T(8,128)(2,1)S(1)}, u32[]{:S(2)}, u32[]{:S(2)}) collective-permute-start(bf16[512,128]{1,0:T(8,128)(2,1)S(1)} %mirror_sums.3.mine), channel_id=1, source_target_pairs={{0,1},{1,0},{2,3},{3,2},{4,5},{5,4},{6,7},{7,6},{8,9},{9,8},{10,11... | collective-permute-start | bytes 393224 | tf_op jit(solution)/shard_map/ppermute | solution.py:41
  49.4 9.2 %collective-permute-start.17 = (bf16[128,256]{1,0:T(8,128)(2,1)S(1)}, bf16[128,256]{1,0:T(8,128)(2,1)S(1)}, u32[]{:S(2)}, u32[]{:S(2)}) collective-permute-start(bf16[128,256]{1,0:T(8,128)(2,1)S(1)} %get-tuple-element.133), channel_id=1, source_target_pairs={{0,14},{2,12},{4,10},{6,8},{8,6},{10,4},{12,2},{14,0},{1,15},{3,13... | collective-permute-start | bytes 196616 | tf_op jit(solution)/shard_map/ppermute | solution.py:45
  53.3 7.0 %collective-permute-start.18 = (bf16[128,256]{1,0:T(8,128)(2,1)S(1)}, bf16[128,256]{1,0:T(8,128)(2,1)S(1)}, u32[]{:S(2)}, u32[]{:S(2)}) collective-permute-start(bf16[128,256]{1,0:T(8,128)(2,1)S(1)} %get-tuple-element.134), channel_id=1, source_target_pairs={{0,12},{2,14},{4,8},{6,10},{8,4},{10,6},{12,0},{14,2},{1,13},{3,15... | collective-permute-start | bytes 196616 | tf_op jit(solution)/shard_map/ppermute | solution.py:45
  54.2 10.3 %collective-permute-start.19 = (bf16[128,256]{1,0:T(8,128)(2,1)S(1)}, bf16[128,256]{1,0:T(8,128)(2,1)S(1)}, u32[]{:S(2)}, u32[]{:S(2)}) collective-permute-start(bf16[128,256]{1,0:T(8,128)(2,1)S(1)} %get-tuple-element.135), channel_id=1, source_target_pairs={{0,10},{2,8},{4,14},{6,12},{8,2},{10,0},{12,6},{14,4},{1,11},{3,9}... | collective-permute-start | bytes 196616 | tf_op jit(solution)/shard_map/ppermute | solution.py:45
  54.2 10.6 %collective-permute-start.20 = (bf16[128,256]{1,0:T(8,128)(2,1)S(1)}, bf16[128,256]{1,0:T(8,128)(2,1)S(1)}, u32[]{:S(2)}, u32[]{:S(2)}) collective-permute-start(bf16[128,256]{1,0:T(8,128)(2,1)S(1)} %get-tuple-element.136), channel_id=1, source_target_pairs={{0,8},{2,10},{4,12},{6,14},{8,0},{10,2},{12,4},{14,6},{1,9},{3,11}... | collective-permute-start | bytes 196616 | tf_op jit(solution)/shard_map/ppermute | solution.py:45
  57.1 7.7 %collective-permute-start.21 = (bf16[128,256]{1,0:T(8,128)(2,1)S(1)}, bf16[128,256]{1,0:T(8,128)(2,1)S(1)}, u32[]{:S(2)}, u32[]{:S(2)}) collective-permute-start(bf16[128,256]{1,0:T(8,128)(2,1)S(1)} %get-tuple-element.137), channel_id=1, source_target_pairs={{0,6},{2,4},{4,2},{6,0},{8,14},{10,12},{12,10},{14,8},{1,7},{3,5},... | collective-permute-start | bytes 196616 | tf_op jit(solution)/shard_map/ppermute | solution.py:45
  58.6 6.8 %collective-permute-start.22 = (bf16[128,256]{1,0:T(8,128)(2,1)S(1)}, bf16[128,256]{1,0:T(8,128)(2,1)S(1)}, u32[]{:S(2)}, u32[]{:S(2)}) collective-permute-start(bf16[128,256]{1,0:T(8,128)(2,1)S(1)} %get-tuple-element.138), channel_id=1, source_target_pairs={{0,4},{2,6},{4,0},{6,2},{8,12},{10,14},{12,8},{14,10},{1,5},{3,7},... | collective-permute-start | bytes 196616 | tf_op jit(solution)/shard_map/ppermute | solution.py:45
  60.4 5.1 %collective-permute-start.23 = (bf16[128,256]{1,0:T(8,128)(2,1)S(1)}, bf16[128,256]{1,0:T(8,128)(2,1)S(1)}, u32[]{:S(2)}, u32[]{:S(2)}) collective-permute-start(bf16[128,256]{1,0:T(8,128)(2,1)S(1)} %get-tuple-element.139), channel_id=1, source_target_pairs={{0,2},{2,0},{4,6},{6,4},{8,10},{10,8},{12,14},{14,12},{1,3},{3,1},... | collective-permute-start | bytes 196616 | tf_op jit(solution)/shard_map/ppermute | solution.py:45
  65.4 2.4 %copy-start.5 = (bf16[512,256]{1,0:T(8,128)(2,1)S(1)}, bf16[512,256]{1,0:T(8,128)(2,1)}, u32[]{:S(2)}) copy-start(bf16[512,256]{1,0:T(8,128)(2,1)} %get-tuple-element.70.encoded) | copy-start | bytes 786436
  67.8 1.6 %collective-permute-start.24 = (bf16[512,256]{1,0:T(8,128)(2,1)S(1)}, bf16[512,256]{1,0:T(8,128)(2,1)S(1)}, u32[]{:S(2)}, u32[]{:S(2)}) collective-permute-start(bf16[512,256]{1,0:T(8,128)(2,1)S(1)} %edge_sums.1.mine), channel_id=1, source_target_pairs={{0,1},{1,0},{2,3},{3,2},{4,5},{5,4},{6,7},{7,6},{8,9},{9,8},{10,11... | collective-permute-start | bytes 786440 | tf_op jit(solution)/shard_map/ppermute | solution.py:41
